TPU v7x, 512 devices: a whole 4x8x8 slice. The times are simulated.
512 devices in a mesh: wide: 32 (over z, y_hi), narrow: 16 (over y_lo, x, core).
Axes of the slice: x: 4, y: 8 (y_hi: 4, y_lo: 2; y = y_hi * 2 + y_lo), z: 8, core: 2. Of those that a mesh axis runs over, the one named last changes fastest.
Arguments:
- images: bfloat16 [131072, 1152], P(('wide', 'narrow')), may hold values from -0.1875 to 0.1875
- texts: bfloat16 [131072, 1152], P(('wide', 'narrow')), may hold values from -0.1875 to 0.1875
- labels: int32 [131072], P(('wide', 'narrow')), may hold values from 0 to 131071, as said below
- log_scale: float32 [1], replicated, may hold values from 1 to 2.3
- bias: float32 [1], replicated, may hold values from -4 to -2
Outputs:
- grad_images: float32 [131072, 1152], P(('wide', 'narrow'))
- grad_texts: float32 [131072, 1152], P(('wide', 'narrow'))
Inputs may be any that keep to these rules, and one draw needn't show every extreme that they name: labels_i names a text row of the same block of 256 rows as row i, and the labels of each block are a permutation of that block's rows.
All inputs are finite; a program needn't handle non-finite values.
Results may differ from a plain program's by a relative error of at most 0.0042.
Values may be sent and summed in bfloat16 or wider, within the bound.
No kernel may reach another device: no remote copies, remote signals or barrier semaphores. Data moves between devices by JAX's collectives and lax.ppermute only.
A program may use at most 64 MiB of HBM per device.

v0:
```python
import jax
import jax.numpy as jnp
from jax import lax
from jax.sharding import PartitionSpec as P

WINDOW = 4


EPS = 1e-06


def shifted(value, axis, steps):
    count = lax.axis_size(axis)
    pairs = [(source, (source + steps) % count) for source in range(count)]
    return lax.ppermute(value, axis, pairs)


def normalize(vectors):
    floats = vectors.astype(jnp.float32)
    inverse = lax.rsqrt(jnp.sum(floats * floats, axis=-1, keepdims=True) + EPS)
    return (floats * inverse, inverse)


def unit_backward(unit_rows, inverse, upstream):
    return inverse * (upstream - unit_rows * jnp.sum(unit_rows * upstream, axis=-1, keepdims=True))


def shortest(distance, count):
    remain = distance % count
    return remain - count


def weigh_block(image_rows, text_rows, row_labels, target, temper, offset):
    scores = jnp.einsum("id,jd->ij", image_rows, text_rows, preferred_element_type=jnp.float32)
    logits = temper * scores + offset
    positive = (row_labels[:, None] == target[None, :]).astype(jnp.float32)
    residual = jax.nn.sigmoid(logits) - positive
    return (temper * residual).astype(jnp.bfloat16)


def image_side(image_grad, visitor, image_half, labels, temper, offset, anchor):
    block_rows = visitor.shape[0]
    target = anchor * block_rows + jnp.arange(block_rows, dtype=jnp.int32)
    weighted = weigh_block(image_half, visitor, labels, target, temper, offset)
    image_grad = image_grad + jnp.dot(weighted, visitor, preferred_element_type=jnp.float32)
    return (image_grad, weighted)


def visit(image_grad, visitor, carried, image_half, labels, temper, offset, anchor):
    image_grad, weighted = image_side(
        image_grad, visitor, image_half, labels, temper, offset, anchor
    )
    carried = carried + jnp.einsum(
        "ij,id->jd", weighted, image_half, preferred_element_type=jnp.float32
    )
    return (image_grad, carried)


def shards(images, texts, labels, log_scale, bias):
    image_unit, image_inverse = normalize(images)
    text_unit, text_inverse = normalize(texts)
    image_half = image_unit.astype(jnp.bfloat16)
    text_half = text_unit.astype(jnp.bfloat16)
    temper = jnp.exp(log_scale[0])
    offset = bias[0]
    wide_count = lax.axis_size("wide")
    narrow_count = lax.axis_size("narrow")
    wide_index = lax.axis_index("wide")
    narrow_index = lax.axis_index("narrow")

    def source(wide_back, narrow_back):
        return (wide_index - wide_back) % wide_count * narrow_count + (
            narrow_index - narrow_back
        ) % narrow_count

    image_grad = jnp.zeros(images.shape, jnp.float32)
    visitor = text_half
    carried = jnp.zeros(images.shape, jnp.float32)
    for number in range(2 * WINDOW):
        wide_back = number // WINDOW
        narrow_back = number - wide_back * WINDOW + wide_back * (WINDOW - 1)
        image_grad, carried = visit(
            image_grad,
            visitor,
            carried,
            image_half,
            labels,
            temper,
            offset,
            source(wide_back, narrow_back),
        )
        if number == WINDOW - 1:
            visitor = shifted(visitor, "wide", 1)
            carried = shifted(carried, "wide", 1)
        elif number < 2 * WINDOW - 1:
            visitor = shifted(visitor, "narrow", 1)
            carried = shifted(carried, "narrow", 1)
    carried = shifted(carried, "wide", -1)
    return_hop = shortest(-(2 * WINDOW - 2), narrow_count)
    carried = shifted(carried, "narrow", return_hop)
    grad_images = unit_backward(image_unit, image_inverse, image_grad)
    grad_texts = unit_backward(text_unit, text_inverse, carried)
    return (grad_images, grad_texts)


def solution(mesh):
    return jax.shard_map(
        shards,
        mesh=mesh,
        in_specs=(
            P(("wide", "narrow"), None),
            P(("wide", "narrow"), None),
            P(("wide", "narrow")),
            P(),
            P(),
        ),
        out_specs=(P(("wide", "narrow"), None), P(("wide", "narrow"), None)),
        check_vma=False,
    )
```

profile of v0, /device:TPU:7, one launch (start us, length us, event | category | flops | bytes accessed | tf_op | source)
XLA Modules:
  0.0 339.8 jit_solution(15755655692956344214)
XLA Ops:
  0.7 1.3 fusion.9
  2.0 1.3 fusion.13
  4.9 0.4 fusion.70
  5.3 0.4 fusion.91
  5.7 3.7 %collective-permute-start.7 = (f32[256,1152]{1,0:T(8,128)S(1)}, f32[256,1152]{1,0:T(8,128)}, u32[]{:S(2)}, u32[]{:S(2)}) collective-permute-start(f32[256,1152]{1,0:T(8,128)S(1)} %fusion.91), channel_id=1, source_target_pairs={{0,1},{1,2},{2,3},{3,4},{4,5},{5,6},{6,7},{7,8},{8,9},{9,10},{10,1... | collective-permute-start | bytes 3538952 | tf_op jit(solution)/shard_map/ppermute | solution.py:15
  9.4 1.9 collective-permute-start
  11.4 17.5 %collective-permute-done = bf16[256,1152]{1,0:T(8,128)(2,1)S(1)} collective-permute-done((bf16[256,1152]{1,0:T(8,128)(2,1)S(1)}, bf16[256,1152]{1,0:T(8,128)(2,1)S(1)}, u32[]{:S(2)}, u32[]{:S(2)}) %collective-permute-start) | collective-permute-done | bytes 589856 | tf_op jit(solution)/shard_map/ppermute | solution.py:15
  28.9 0.4 fusion.71
  29.3 1.7 convolution_add_fusion
  31.1 6.5 %collective-permute-start.8 = (f32[256,1152]{1,0:T(8,128)S(1)}, f32[256,1152]{1,0:T(8,128)}, u32[]{:S(2)}, u32[]{:S(2)}) collective-permute-start(f32[256,1152]{1,0:T(8,128)S(1)} %convolution_add_fusion), channel_id=1, source_target_pairs={{0,1},{1,2},{2,3},{3,4},{4,5},{5,6},{6,7},{7,8},{8,9},{9,10},{10,1... | collective-permute-start | bytes 3538952 | tf_op jit(solution)/shard_map/ppermute | solution.py:15
  37.6 1.9 collective-permute-start.1
  39.5 17.5 %collective-permute-done.1 = bf16[256,1152]{1,0:T(8,128)(2,1)} collective-permute-done((bf16[256,1152]{1,0:T(8,128)(2,1)S(1)}, bf16[256,1152]{1,0:T(8,128)(2,1)}, u32[]{:S(2)}, u32[]{:S(2)}) %collective-permute-start.1) | collective-permute-done | bytes 589856 | tf_op jit(solution)/shard_map/ppermute | solution.py:15
  57.0 1.5 fusion.72
  58.5 0.4 fusion.88
  58.9 0.2 copy-done.4
  59.2 1.4 add.322
  60.6 6.6 %collective-permute-start.9 = (f32[256,1152]{1,0:T(8,128)S(1)}, f32[256,1152]{1,0:T(8,128)}, u32[]{:S(2)}, u32[]{:S(2)}) collective-permute-start(f32[256,1152]{1,0:T(8,128)S(1)} %add.322), channel_id=1, source_target_pairs={{0,1},{1,2},{2,3},{3,4},{4,5},{5,6},{6,7},{7,8},{8,9},{9,10},{10,1... | collective-permute-start | bytes 3538952 | tf_op jit(solution)/shard_map/ppermute | solution.py:15
  67.2 1.9 collective-permute-start.2
  69.2 17.6 %collective-permute-done.2 = bf16[256,1152]{1,0:T(8,128)(2,1)} collective-permute-done((bf16[256,1152]{1,0:T(8,128)(2,1)}, bf16[256,1152]{1,0:T(8,128)(2,1)}, u32[]{:S(2)}, u32[]{:S(2)}) %collective-permute-start.2) | collective-permute-done | bytes 589856 | tf_op jit(solution)/shard_map/ppermute | solution.py:15
  86.7 1.5 fusion.73
  88.2 0.4 fusion.86
  88.7 0.2 copy-done.6
  88.9 1.4 add.323
  90.3 4.2 %collective-permute-start.10 = (f32[256,1152]{1,0:T(8,128)S(1)}, f32[256,1152]{1,0:T(8,128)}, u32[]{:S(2)}, u32[]{:S(2)}) collective-permute-start(f32[256,1152]{1,0:T(8,128)S(1)} %add.323), channel_id=1, source_target_pairs={{0,16},{16,32},{32,48},{48,64},{64,80},{80,96},{96,112},{112,128},... | collective-permute-start | bytes 3538952 | tf_op jit(solution)/shard_map/ppermute | solution.py:15
  94.5 4.5 %collective-permute-start.3 = (bf16[256,1152]{1,0:T(8,128)(2,1)}, bf16[256,1152]{1,0:T(8,128)(2,1)}, u32[]{:S(2)}, u32[]{:S(2)}) collective-permute-start(bf16[256,1152]{1,0:T(8,128)(2,1)} %collective-permute-done.2), channel_id=1, source_target_pairs={{0,16},{16,32},{32,48},{48,64},{64,80},{80,96},{96,112},{112,128},... | collective-permute-start | bytes 1769480 | tf_op jit(solution)/shard_map/ppermute | solution.py:15
  99.1 73.8 %collective-permute-done.3 = bf16[256,1152]{1,0:T(8,128)(2,1)} collective-permute-done((bf16[256,1152]{1,0:T(8,128)(2,1)}, bf16[256,1152]{1,0:T(8,128)(2,1)}, u32[]{:S(2)}, u32[]{:S(2)}) %collective-permute-start.3) | collective-permute-done | bytes 589856 | tf_op jit(solution)/shard_map/ppermute | solution.py:15
  172.9 1.5 fusion.74
  174.4 0.4 fusion.84
  174.8 0.2 copy-done.8
  175.1 1.4 add.324
  176.5 7.2 %collective-permute-start.11 = (f32[256,1152]{1,0:T(8,128)S(1)}, f32[256,1152]{1,0:T(8,128)}, u32[]{:S(2)}, u32[]{:S(2)}) collective-permute-start(f32[256,1152]{1,0:T(8,128)S(1)} %add.324), channel_id=1, source_target_pairs={{0,1},{1,2},{2,3},{3,4},{4,5},{5,6},{6,7},{7,8},{8,9},{9,10},{10,1... | collective-permute-start | bytes 3538952 | tf_op jit(solution)/shard_map/ppermute | solution.py:15
  183.7 1.9 collective-permute-start.4
  185.7 17.6 %collective-permute-done.4 = bf16[256,1152]{1,0:T(8,128)(2,1)} collective-permute-done((bf16[256,1152]{1,0:T(8,128)(2,1)}, bf16[256,1152]{1,0:T(8,128)(2,1)}, u32[]{:S(2)}, u32[]{:S(2)}) %collective-permute-start.4) | collective-permute-done | bytes 589856 | tf_op jit(solution)/shard_map/ppermute | solution.py:15
  203.2 1.5 fusion.75
  204.8 0.4 fusion.82
  205.2 0.2 copy-done.10
  205.4 1.4 add.325
  206.8 6.5 %collective-permute-start.12 = (f32[256,1152]{1,0:T(8,128)S(1)}, f32[256,1152]{1,0:T(8,128)}, u32[]{:S(2)}, u32[]{:S(2)}) collective-permute-start(f32[256,1152]{1,0:T(8,128)S(1)} %add.325), channel_id=1, source_target_pairs={{0,1},{1,2},{2,3},{3,4},{4,5},{5,6},{6,7},{7,8},{8,9},{9,10},{10,1... | collective-permute-start | bytes 3538952 | tf_op jit(solution)/shard_map/ppermute | solution.py:15
  213.3 1.9 collective-permute-start.5
  215.3 17.6 %collective-permute-done.5 = bf16[256,1152]{1,0:T(8,128)(2,1)} collective-permute-done((bf16[256,1152]{1,0:T(8,128)(2,1)}, bf16[256,1152]{1,0:T(8,128)(2,1)}, u32[]{:S(2)}, u32[]{:S(2)}) %collective-permute-start.5) | collective-permute-done | bytes 589856 | tf_op jit(solution)/shard_map/ppermute | solution.py:15
  232.9 6.5 %collective-permute-start.6 = (bf16[256,1152]{1,0:T(8,128)(2,1)}, bf16[256,1152]{1,0:T(8,128)(2,1)S(1)}, u32[]{:S(2)}, u32[]{:S(2)}) collective-permute-start(bf16[256,1152]{1,0:T(8,128)(2,1)} %collective-permute-done.5), channel_id=1, source_target_pairs={{0,1},{1,2},{2,3},{3,4},{4,5},{5,6},{6,7},{7,8},{8,9},{9,10},{10,1... | collective-permute-start | bytes 1769480 | tf_op jit(solution)/shard_map/ppermute | solution.py:15
  239.3 1.5 fusion.76
  240.9 0.4 fusion.80
  241.3 1.4 add.326
  242.7 2.1 collective-permute-start.13
  244.8 0.3 fusion.101
  245.2 0.4 convolution_add_fusion.7
  245.5 0.9 collective-permute-done.6
  246.5 0.4 fusion.77
  246.9 0.4 fusion.78
  247.3 11.7 %collective-permute-done.13 = f32[256,1152]{1,0:T(8,128)S(1)} collective-permute-done((f32[256,1152]{1,0:T(8,128)S(1)}, f32[256,1152]{1,0:T(8,128)S(1)}, u32[]{:S(2)}, u32[]{:S(2)}) %collective-permute-start.13) | collective-permute-done | bytes 1179680 | tf_op jit(solution)/shard_map/ppermute | solution.py:15
  259.1 5.2 %collective-permute-start.14 = (f32[256,1152]{1,0:T(8,128)S(1)}, f32[256,1152]{1,0:T(8,128)S(1)}, u32[]{:S(2)}, u32[]{:S(2)}) collective-permute-start(f32[256,1152]{1,0:T(8,128)S(1)} %add.327), channel_id=1, source_target_pairs={{0,496},{16,0},{32,16},{48,32},{64,48},{80,64},{96,80},{112,96},{1... | collective-permute-start | bytes 3538952 | tf_op jit(solution)/shard_map/ppermute | solution.py:15
  264.3 1.4 convolution_add_fusion.6
  265.7 1.4 convolution_add_fusion.5
  267.2 1.4 convolution_add_fusion.4
  268.7 1.4 convolution_add_fusion.3
  270.1 37.6 %collective-permute-done.14 = f32[256,1152]{1,0:T(8,128)S(1)} collective-permute-done((f32[256,1152]{1,0:T(8,128)S(1)}, f32[256,1152]{1,0:T(8,128)S(1)}, u32[]{:S(2)}, u32[]{:S(2)}) %collective-permute-start.14) | collective-permute-done | bytes 1179680 | tf_op jit(solution)/shard_map/ppermute | solution.py:15
  307.7 1.9 collective-permute-start.15
  309.6 1.4 convolution_add_fusion.2
  311.0 0.5 fusion.6
  311.5 1.3 fusion.8
  312.8 25.4 %collective-permute-done.15 = f32[256,1152]{1,0:T(8,128)S(1)} collective-permute-done((f32[256,1152]{1,0:T(8,128)S(1)}, f32[256,1152]{1,0:T(8,128)S(1)}, u32[]{:S(2)}, u32[]{:S(2)}) %collective-permute-start.15) | collective-permute-done | bytes 1179680 | tf_op jit(solution)/shard_map/ppermute | solution.py:15
  338.2 0.3 fusion.10
  338.5 1.3 fusion.12
  (44 shorter events, 0.4 us)
Async XLA Ops:
  0.6 2.7 copy-start.1
  0.7 4.2 %copy-start = (bf16[256,1152]{1,0:T(8,128)(2,1)S(1)}, bf16[256,1152]{1,0:T(8,128)(2,1)}, u32[]{:S(2)}) copy-start(bf16[256,1152]{1,0:T(8,128)(2,1)} %param.5) | copy-start | bytes 1769476
  0.7 4.2 %copy-start.14 = (s32[256]{0:T(256)S(1)}, s32[256]{0:T(256)}, u32[]{:S(2)}) copy-start(s32[256]{0:T(256)} %param.7) | copy-start | bytes 3076
  5.3 4.1 %copy-start.12 = (bf16[256,256]{1,0:T(8,128)(2,1)}, bf16[256,256]{1,0:T(8,128)(2,1)S(1)}, u32[]{:S(2)}) copy-start(bf16[256,256]{1,0:T(8,128)(2,1)S(1)} %fusion.70) | copy-start | bytes 393220
  5.7 23.6 %collective-permute-start.7 = (f32[256,1152]{1,0:T(8,128)S(1)}, f32[256,1152]{1,0:T(8,128)}, u32[]{:S(2)}, u32[]{:S(2)}) collective-permute-start(f32[256,1152]{1,0:T(8,128)S(1)} %fusion.91), channel_id=1, source_target_pairs={{0,1},{1,2},{2,3},{3,4},{4,5},{5,6},{6,7},{7,8},{8,9},{9,10},{10,1... | collective-permute-start | bytes 3538952 | tf_op jit(solution)/shard_map/ppermute | solution.py:15
  9.4 19.4 %collective-permute-start = (bf16[256,1152]{1,0:T(8,128)(2,1)S(1)}, bf16[256,1152]{1,0:T(8,128)(2,1)S(1)}, u32[]{:S(2)}, u32[]{:S(2)}) collective-permute-start(bf16[256,1152]{1,0:T(8,128)(2,1)S(1)} %fusion.2), channel_id=1, source_target_pairs={{0,1},{1,2},{2,3},{3,4},{4,5},{5,6},{6,7},{7,8},{8,9},{9,10},{10,1... | collective-permute-start | bytes 1769480 | tf_op jit(solution)/shard_map/ppermute | solution.py:15
  29.3 1.8 copy-start.2
  31.1 28.1 %collective-permute-start.8 = (f32[256,1152]{1,0:T(8,128)S(1)}, f32[256,1152]{1,0:T(8,128)}, u32[]{:S(2)}, u32[]{:S(2)}) collective-permute-start(f32[256,1152]{1,0:T(8,128)S(1)} %convolution_add_fusion), channel_id=1, source_target_pairs={{0,1},{1,2},{2,3},{3,4},{4,5},{5,6},{6,7},{7,8},{8,9},{9,10},{10,1... | collective-permute-start | bytes 3538952 | tf_op jit(solution)/shard_map/ppermute | solution.py:15
  37.6 19.4 %collective-permute-start.1 = (bf16[256,1152]{1,0:T(8,128)(2,1)S(1)}, bf16[256,1152]{1,0:T(8,128)(2,1)}, u32[]{:S(2)}, u32[]{:S(2)}) collective-permute-start(bf16[256,1152]{1,0:T(8,128)(2,1)S(1)} %collective-permute-done), channel_id=1, source_target_pairs={{0,1},{1,2},{2,3},{3,4},{4,5},{5,6},{6,7},{7,8},{8,9},{9,10},{10,1... | collective-permute-start | bytes 1769480 | tf_op jit(solution)/shard_map/ppermute | solution.py:15
  58.5 0.7 copy-start.4
  60.6 28.3 %collective-permute-start.9 = (f32[256,1152]{1,0:T(8,128)S(1)}, f32[256,1152]{1,0:T(8,128)}, u32[]{:S(2)}, u32[]{:S(2)}) collective-permute-start(f32[256,1152]{1,0:T(8,128)S(1)} %add.322), channel_id=1, source_target_pairs={{0,1},{1,2},{2,3},{3,4},{4,5},{5,6},{6,7},{7,8},{8,9},{9,10},{10,1... | collective-permute-start | bytes 3538952 | tf_op jit(solution)/shard_map/ppermute | solution.py:15
  67.2 19.6 %collective-permute-start.2 = (bf16[256,1152]{1,0:T(8,128)(2,1)}, bf16[256,1152]{1,0:T(8,128)(2,1)}, u32[]{:S(2)}, u32[]{:S(2)}) collective-permute-start(bf16[256,1152]{1,0:T(8,128)(2,1)} %collective-permute-done.1), channel_id=1, source_target_pairs={{0,1},{1,2},{2,3},{3,4},{4,5},{5,6},{6,7},{7,8},{8,9},{9,10},{10,1... | collective-permute-start | bytes 1769480 | tf_op jit(solution)/shard_map/ppermute | solution.py:15
  88.2 0.7 copy-start.6
  90.3 84.8 %collective-permute-start.10 = (f32[256,1152]{1,0:T(8,128)S(1)}, f32[256,1152]{1,0:T(8,128)}, u32[]{:S(2)}, u32[]{:S(2)}) collective-permute-start(f32[256,1152]{1,0:T(8,128)S(1)} %add.323), channel_id=1, source_target_pairs={{0,16},{16,32},{32,48},{48,64},{64,80},{80,96},{96,112},{112,128},... | collective-permute-start | bytes 3538952 | tf_op jit(solution)/shard_map/ppermute | solution.py:15
  94.5 78.4 %collective-permute-start.3 = (bf16[256,1152]{1,0:T(8,128)(2,1)}, bf16[256,1152]{1,0:T(8,128)(2,1)}, u32[]{:S(2)}, u32[]{:S(2)}) collective-permute-start(bf16[256,1152]{1,0:T(8,128)(2,1)} %collective-permute-done.2), channel_id=1, source_target_pairs={{0,16},{16,32},{32,48},{48,64},{64,80},{80,96},{96,112},{112,128},... | collective-permute-start | bytes 1769480 | tf_op jit(solution)/shard_map/ppermute | solution.py:15
  174.4 0.7 copy-start.8
  176.5 28.9 %collective-permute-start.11 = (f32[256,1152]{1,0:T(8,128)S(1)}, f32[256,1152]{1,0:T(8,128)}, u32[]{:S(2)}, u32[]{:S(2)}) collective-permute-start(f32[256,1152]{1,0:T(8,128)S(1)} %add.324), channel_id=1, source_target_pairs={{0,1},{1,2},{2,3},{3,4},{4,5},{5,6},{6,7},{7,8},{8,9},{9,10},{10,1... | collective-permute-start | bytes 3538952 | tf_op jit(solution)/shard_map/ppermute | solution.py:15
  183.7 19.6 %collective-permute-start.4 = (bf16[256,1152]{1,0:T(8,128)(2,1)}, bf16[256,1152]{1,0:T(8,128)(2,1)}, u32[]{:S(2)}, u32[]{:S(2)}) collective-permute-start(bf16[256,1152]{1,0:T(8,128)(2,1)} %collective-permute-done.3), channel_id=1, source_target_pairs={{0,1},{1,2},{2,3},{3,4},{4,5},{5,6},{6,7},{7,8},{8,9},{9,10},{10,1... | collective-permute-start | bytes 1769480 | tf_op jit(solution)/shard_map/ppermute | solution.py:15
  204.7 0.7 copy-start.10
  206.8 34.5 %collective-permute-start.12 = (f32[256,1152]{1,0:T(8,128)S(1)}, f32[256,1152]{1,0:T(8,128)}, u32[]{:S(2)}, u32[]{:S(2)}) collective-permute-start(f32[256,1152]{1,0:T(8,128)S(1)} %add.325), channel_id=1, source_target_pairs={{0,1},{1,2},{2,3},{3,4},{4,5},{5,6},{6,7},{7,8},{8,9},{9,10},{10,1... | collective-permute-start | bytes 3538952 | tf_op jit(solution)/shard_map/ppermute | solution.py:15
  213.3 19.6 %collective-permute-start.5 = (bf16[256,1152]{1,0:T(8,128)(2,1)}, bf16[256,1152]{1,0:T(8,128)(2,1)}, u32[]{:S(2)}, u32[]{:S(2)}) collective-permute-start(bf16[256,1152]{1,0:T(8,128)(2,1)} %collective-permute-done.4), channel_id=1, source_target_pairs={{0,1},{1,2},{2,3},{3,4},{4,5},{5,6},{6,7},{7,8},{8,9},{9,10},{10,1... | collective-permute-start | bytes 1769480 | tf_op jit(solution)/shard_map/ppermute | solution.py:15
  232.9 13.6 %collective-permute-start.6 = (bf16[256,1152]{1,0:T(8,128)(2,1)}, bf16[256,1152]{1,0:T(8,128)(2,1)S(1)}, u32[]{:S(2)}, u32[]{:S(2)}) collective-permute-start(bf16[256,1152]{1,0:T(8,128)(2,1)} %collective-permute-done.5), channel_id=1, source_target_pairs={{0,1},{1,2},{2,3},{3,4},{4,5},{5,6},{6,7},{7,8},{8,9},{9,10},{10,1... | collective-permute-start | bytes 1769480 | tf_op jit(solution)/shard_map/ppermute | solution.py:15
  241.3 3.5 %copy-start.13 = (bf16[256,256]{1,0:T(8,128)(2,1)S(1)}, bf16[256,256]{1,0:T(8,128)(2,1)}, u32[]{:S(2)}) copy-start(bf16[256,256]{1,0:T(8,128)(2,1)} %copy-done.12) | copy-start | bytes 393220
  242.7 2.4 copy-start.3
  242.7 16.3 %collective-permute-start.13 = (f32[256,1152]{1,0:T(8,128)S(1)}, f32[256,1152]{1,0:T(8,128)S(1)}, u32[]{:S(2)}, u32[]{:S(2)}) collective-permute-start(f32[256,1152]{1,0:T(8,128)S(1)} %add.326), channel_id=1, source_target_pairs={{0,1},{1,2},{2,3},{3,4},{4,5},{5,6},{6,7},{7,8},{8,9},{9,10},{10,1... | collective-permute-start | bytes 3538952 | tf_op jit(solution)/shard_map/ppermute | solution.py:15
  247.3 17.0 %copy-start.5 = (bf16[256,256]{1,0:T(8,128)(2,1)S(1)}, bf16[256,256]{1,0:T(8,128)(2,1)}, u32[]{:S(2)}) copy-start(bf16[256,256]{1,0:T(8,128)(2,1)} %copy-done.4) | copy-start | bytes 393220
  259.1 6.6 %copy-start.7 = (bf16[256,256]{1,0:T(8,128)(2,1)S(1)}, bf16[256,256]{1,0:T(8,128)(2,1)}, u32[]{:S(2)}) copy-start(bf16[256,256]{1,0:T(8,128)(2,1)} %copy-done.6) | copy-start | bytes 393220
  259.1 48.6 %collective-permute-start.14 = (f32[256,1152]{1,0:T(8,128)S(1)}, f32[256,1152]{1,0:T(8,128)S(1)}, u32[]{:S(2)}, u32[]{:S(2)}) collective-permute-start(f32[256,1152]{1,0:T(8,128)S(1)} %add.327), channel_id=1, source_target_pairs={{0,496},{16,0},{32,16},{48,32},{64,48},{80,64},{96,80},{112,96},{1... | collective-permute-start | bytes 3538952 | tf_op jit(solution)/shard_map/ppermute | solution.py:15
  265.7 1.5 copy-start.9
  267.2 1.5 copy-start.11
  307.7 30.5 %collective-permute-start.15 = (f32[256,1152]{1,0:T(8,128)S(1)}, f32[256,1152]{1,0:T(8,128)S(1)}, u32[]{:S(2)}, u32[]{:S(2)}) collective-permute-start(f32[256,1152]{1,0:T(8,128)S(1)} %collective-permute-done.14), channel_id=1, source_target_pairs={{0,10},{1,11},{2,12},{3,13},{4,14},{5,15},{6,0},{7,1},{8,2},{9,3},... | collective-permute-start | bytes 3538952 | tf_op jit(solution)/shard_map/ppermute | solution.py:15
where the time goes:
time: 346 us; the launch traced here: 340 us
  waiting for transfers between devices  237 us (68%)
  starting transfers between devices  64.5 us (19%)
  matrix products  21.6 us (6%)
  other arithmetic  12.8 us (4%)
    ppermute x16, waiting for transfers between devices, shifted(): return lax.ppermute(value, axis, pairs)  237 us
    ppermute x16, starting transfers between devices, shifted(): return lax.ppermute(value, axis, pairs)  64.5 us
    dot_general x8, matrix products, weigh_block(): jnp.einsum('id,jd->ij', image_rows, text_rows, preferred_element_type=jnp...  8.72 us
    dot_general x8, matrix products, image_side(): jnp.dot(weighted, visitor, preferred_element_type=jnp.float32)  8.28 us
    add x6, other arithmetic, visit(): carried + jnp.einsum('ij,id->jd', weighted, image_half, preferred_element...  7.12 us
  transfers between devices with their start and end apart: 16, of which 10 were waited for; matrix products, arithmetic and copies ran while one was open for 6% of the time, Pallas kernels for 0%

commit v1 on v0

v1 whole, which is shorter than its diff:
```python
import functools

import jax
import jax.numpy as jnp
from jax import lax
from jax.experimental import pallas as pl
from jax.experimental.pallas import tpu as pltpu
from jax.sharding import PartitionSpec as P

EPS = 1e-06
AXES = ("wide", "narrow")
NT = (((1,), (1,)), ((), ()))
NN = (((1,), (0,)), ((), ()))
TN = (((0,), (0,)), ((), ()))
VMEM_LIMIT = 48 * 1024 * 1024
F32 = jnp.float32
BF16 = jnp.bfloat16


def mm(a, b, dims):
    return lax.dot_general(a, b, dims, preferred_element_type=F32)


def whole(space=pltpu.VMEM):
    return pl.BlockSpec(memory_space=space)


def unit_of(rows):
    floats = rows.astype(F32)
    inverse = lax.rsqrt(jnp.sum(floats * floats, axis=-1, keepdims=True) + EPS)
    return floats * inverse, inverse


def weights(scores, temper, offset):
    return (temper * jax.nn.sigmoid(temper * scores + offset)).astype(BF16)


def call(kernel, outs, inputs, matmuls, aliases=None):
    specs = [whole(pltpu.SMEM if x.ndim == 1 else pltpu.VMEM) for x in inputs]
    moved = sum(x.size * x.dtype.itemsize for x in inputs)
    moved += sum(x.size * x.dtype.itemsize for x in outs)
    return pl.pallas_call(
        kernel,
        out_shape=outs,
        in_specs=specs,
        out_specs=[whole() for _ in outs],
        input_output_aliases=aliases or {},
        compiler_params=pltpu.CompilerParams(vmem_limit_bytes=VMEM_LIMIT),
        cost_estimate=pl.CostEstimate(
            flops=matmuls * 2 * 256 * 256 * 1152, bytes_accessed=moved, transcendentals=0
        ),
    )(*inputs)


def prepare_kernel(texts, images, text_half, image_half, both):
    rows = texts.shape[0]
    half = unit_of(texts[...])[0].astype(BF16)
    text_half[...] = half
    both[:rows] = half
    half = unit_of(images[...])[0].astype(BF16)
    image_half[...] = half
    both[rows:] = half


def own_kernel(
    temper, flags, labels, text_half, image_half, text_other, image_other,
    image_own, image_far, text_own, text_far,
):
    scale, offset = temper[0], temper[1]
    text, image = text_half[...], image_half[...]
    scores = mm(image, text, NT)
    target = lax.broadcasted_iota(jnp.int32, scores.shape, 1)
    positive = (labels[...] == target).astype(F32)
    residual = jax.nn.sigmoid(scale * scores + offset) - positive
    weighted = (scale * residual).astype(BF16)
    image_own[...] = mm(weighted, text, NN)
    text_own[...] = mm(weighted, image, TN)

    @pl.when(flags[0] == 0)
    def _():
        part = weights(mm(image_other[...], text, NT), scale, offset)
        image_far[...] = mm(part, text, NN)
        text_far[...] = jnp.zeros(text_far.shape, F32)

    @pl.when(flags[0] == 1)
    def _():
        part = weights(mm(text_other[...], image, NT), scale, offset)
        text_far[...] = mm(part, image, NN)
        image_far[...] = jnp.zeros(image_far.shape, F32)


def visit_kernel(
    always, temper, flags, visitor, own, other, own_in, far_in, own_out, far_out
):
    scale, offset = temper[0], temper[1]
    block = visitor[...]

    def far():
        part = weights(mm(other[...], block, NT), scale, offset)
        far_out[...] = far_in[...] + mm(part, block, NN)

    if always is None:
        far()
    else:
        pl.when(flags[0] == always)(far)

        @pl.when(flags[0] != always)
        def _():
            far_out[...] = far_in[...]

    part = weights(mm(own[...], block, NT), scale, offset)
    own_out[...] = own_in[...] + mm(part, block, NN)


def last_kernel(temper, visitor, own, rows, own_in, received, grad):
    scale, offset = temper[0], temper[1]
    block = visitor[...]
    part = weights(mm(own[...], block, NT), scale, offset)
    upstream = own_in[...] + received[...] + mm(part, block, NN)
    unit, inverse = unit_of(rows[...])
    along = jnp.sum(unit * upstream, axis=-1, keepdims=True)
    grad[...] = inverse * (upstream - unit * along)


def shards(images, texts, labels, log_scale, bias):
    n_wide, n_narrow = lax.axis_size("wide"), lax.axis_size("narrow")
    wide, narrow = lax.axis_index("wide"), lax.axis_index("narrow")
    rows, width = images.shape
    core = narrow % 2

    def moved(value, place):
        pairs = []
        for w in range(n_wide):
            for n in range(n_narrow):
                a, b = place(w, n)
                pairs.append((w * n_narrow + n, a % n_wide * n_narrow + b % n_narrow))
        return lax.ppermute(value, AXES, pairs)

    def hop(value, sign, w_step, chips):
        return moved(value, lambda w, n: (w + sign * w_step, n + 2 * sign * chips))

    def last_hop(value, sign):
        def place(w, n):
            even = n % 2 == (0 if sign > 0 else 1)
            m = n + 1 - 2 * (n % 2)
            return (w + sign, m) if even else (w, m + 2 * sign)

        return moved(value, place)

    def swapped(value):
        return moved(value, lambda w, n: (w, n + 1 - 2 * (n % 2)))

    temper = jnp.stack([jnp.exp(log_scale[0]), bias[0]])
    flags = core.reshape(1).astype(jnp.int32)
    local = (labels - (wide * n_narrow + narrow) * rows).reshape(rows, 1)
    half = jax.ShapeDtypeStruct((rows, width), BF16)
    full = jax.ShapeDtypeStruct((rows, width), F32)
    pair = jax.ShapeDtypeStruct((2 * rows, width), BF16)

    text_half, image_half, both = call(prepare_kernel, [half, half, pair], [texts, images], 0)
    both = swapped(both)
    a_text, a_image = hop(text_half, 1, 0, 1), hop(image_half, -1, 0, 1)
    d_text, d_image = hop(text_half, 1, 1, 3), hop(image_half, -1, 1, 3)
    text_other, image_other = both[:rows], both[rows:]
    image_own, image_far, text_own, text_far = call(
        own_kernel,
        [full] * 4,
        [temper, flags, local, text_half, image_half, text_other, image_other],
        5,
    )
    b_text, b_image = last_hop(a_text, 1), last_hop(a_image, -1)
    c_text, c_image = hop(d_text, 1, 0, -1), hop(d_image, -1, 0, -1)

    def visit(always, visitor, own, other, own_sum, far_sum):
        return call(
            functools.partial(visit_kernel, always),
            [full, full],
            [temper, flags, visitor, own, other, own_sum, far_sum],
            4,
            {5: 0, 6: 1},
        )

    for always_t, always_i, text, image in (
        (None, None, a_text, a_image),
        (1, 0, d_text, d_image),
        (None, None, c_text, c_image),
    ):
        image_own, image_far = visit(always_t, text, image_half, image_other, image_own, image_far)
        text_own, text_far = visit(always_i, image, text_half, text_other, text_own, text_far)
    image_back, text_back = swapped(image_far), swapped(text_far)
    (grad_images,) = call(
        last_kernel, [full], [temper, b_text, image_half, images, image_own, image_back], 2
    )
    (grad_texts,) = call(
        last_kernel, [full], [temper, b_image, text_half, texts, text_own, text_back], 2
    )
    return (grad_images, grad_texts)


def solution(mesh):
    return jax.shard_map(
        shards,
        mesh=mesh,
        in_specs=(P(AXES, None), P(AXES, None), P(AXES), P(), P()),
        out_specs=(P(AXES, None), P(AXES, None)),
        check_vma=False,
    )
```

time: 346 us -> 120 us (0.35); the launches traced: 340 us -> 119 us
  waiting for transfers between devices: 237 us -> 39.2 us
  Pallas kernels: 0 us -> 23.9 us
  matrix products: 21.6 us -> 0 us
  starting transfers between devices: 64.5 us -> 48.3 us
  other arithmetic: 12.8 us -> 0.08 us
  local copies, waits for them, and re-layouts: 1 us -> 5.55 us
    ppermute x16 -> x11, waiting for transfers between devices: 237 us -> 39.2 us  [moved(): return lax.ppermute(value, AXES, pairs)]
    pallas_call x0 -> x10, Pallas kernels: none -> 23.9 us  [call(): pl.pallas_call(kernel, out_shape=outs, in_specs=specs, out_specs=[whole()...]
    dot_general x24 -> x0, matrix products: 21.6 us -> none  [the longest x8 8.72 us: weigh_block(): jnp.einsum('id,jd->ij', image_rows, text_rows, preferred_element_type=jnp...]
    ppermute x16 -> x11, starting transfers between devices: 64.5 us -> 48.3 us  [moved(): return lax.ppermute(value, AXES, pairs)]
    add x14 -> x0, other arithmetic: 7.15 us -> none  [the longest x6 7.12 us: visit(): carried + jnp.einsum('ij,id->jd', weighted, image_half, preferred_element...]
  transfers between devices with their start and end apart: 16 -> 11, of which waited for: 10 -> 5; matrix products, arithmetic and copies ran while one was open for 6% -> 2% of each run, Pallas kernels for 0% -> 16%
where the time goes in v1:
time: 120 us; the launch traced here: 119 us
  starting transfers between devices  48.3 us (40%)
  waiting for transfers between devices  39.2 us (33%)
  Pallas kernels  23.9 us (20%)
  local copies, waits for them, and re-layouts  5.55 us (5%)
  between operations  2.19 us (2%)
    ppermute x11, starting transfers between devices, moved(): return lax.ppermute(value, AXES, pairs)  48.3 us
    ppermute x11, waiting for transfers between devices, moved(): return lax.ppermute(value, AXES, pairs)  39.2 us
    pallas_call x10, Pallas kernels, call(): pl.pallas_call(kernel, out_shape=outs, in_specs=specs, out_specs=[whole()...  23.9 us
    unnamed x14, local copies, waits for them, and re-layouts  3.41 us
  transfers between devices with their start and end apart: 11, of which 5 were waited for; matrix products, arithmetic and copies ran while one was open for 2% of the time, Pallas kernels for 16%

profile of v1, /device:TPU:7, one launch (start us, length us, event | category | flops | bytes accessed | tf_op | source)
XLA Modules:
  0.0 119.2 jit_solution(16813710880018005903)
XLA Ops:
  0.6 0.0 copy-start.1
  0.6 1.1 copy-done.1
  1.7 0.0 copy-start.3
  1.7 1.1 copy-done.3
  2.8 0.0 copy-start.6
  2.8 1.4 %shard_map.68 = (bf16[256,1152]{1,0:T(8,128)(2,1)S(1)}, bf16[256,1152]{1,0:T(8,128)(2,1)S(1)}, bf16[512,1152]{1,0:T(8,128)(2,1)}) custom-call(bf16[256,1152]{1,0:T(8,128)(2,1)S(1)} %copy-done.1, bf16[256,1152]{1,0:T(8,128)(2,1)S(1)} %copy-done.3), custom_call_target="tpu_custom_call" | custom-call | bytes 3538944 | tf_op jit(solution)/shard_map/pallas_call | solution.py:42
  4.2 2.6 %collective-permute-start.4 = (bf16[512,1152]{1,0:T(8,128)(2,1)}, bf16[512,1152]{1,0:T(8,128)(2,1)}, u32[]{:S(2)}, u32[]{:S(2)}) collective-permute-start(bf16[512,1152]{1,0:T(8,128)(2,1)} %get-tuple-element.23), channel_id=1, source_target_pairs={{0,1},{1,0},{2,3},{3,2},{4,5},{5,4},{6,7},{7,6},{8,9},{9,8},{10,11... | collective-permute-start | bytes 3538952 | tf_op jit(solution)/shard_map/ppermute | solution.py:137
  6.8 14.3 %collective-permute-start.8 = (bf16[256,1152]{1,0:T(8,128)(2,1)S(1)}, bf16[256,1152]{1,0:T(8,128)(2,1)S(1)}, u32[]{:S(2)}, u32[]{:S(2)}) collective-permute-start(bf16[256,1152]{1,0:T(8,128)(2,1)S(1)} %get-tuple-element.22.image_half.own), channel_id=1, source_target_pairs={{0,506},{1,507},{2,508},{3,509},{4,510},{5,511},{6,496},{7,497},{8... | collective-permute-start | bytes 1769480 | tf_op jit(solution)/shard_map/ppermute | solution.py:137
  21.0 1.9 %collective-permute-start.2 = (bf16[256,1152]{1,0:T(8,128)(2,1)S(1)}, bf16[256,1152]{1,0:T(8,128)(2,1)S(1)}, u32[]{:S(2)}, u32[]{:S(2)}) collective-permute-start(bf16[256,1152]{1,0:T(8,128)(2,1)S(1)} %get-tuple-element.21.text_half.own), channel_id=1, source_target_pairs={{0,22},{1,23},{2,24},{3,25},{4,26},{5,27},{6,28},{7,29},{8,30},{9,... | collective-permute-start | bytes 1769480 | tf_op jit(solution)/shard_map/ppermute | solution.py:137
  23.0 2.4 %collective-permute-start.6 = (bf16[256,1152]{1,0:T(8,128)(2,1)S(1)}, bf16[256,1152]{1,0:T(8,128)(2,1)S(1)}, u32[]{:S(2)}, u32[]{:S(2)}) collective-permute-start(bf16[256,1152]{1,0:T(8,128)(2,1)S(1)} %get-tuple-element.22.image_half.own), channel_id=1, source_target_pairs={{0,14},{1,15},{2,0},{3,1},{4,2},{5,3},{6,4},{7,5},{8,6},{9,7},{10,... | collective-permute-start | bytes 1769480 | tf_op jit(solution)/shard_map/ppermute | solution.py:137
  25.4 5.0 %collective-permute-start = (bf16[256,1152]{1,0:T(8,128)(2,1)S(1)}, bf16[256,1152]{1,0:T(8,128)(2,1)S(1)}, u32[]{:S(2)}, u32[]{:S(2)}) collective-permute-start(bf16[256,1152]{1,0:T(8,128)(2,1)S(1)} %get-tuple-element.21.text_half.own), channel_id=1, source_target_pairs={{0,2},{1,3},{2,4},{3,5},{4,6},{5,7},{6,8},{7,9},{8,10},{9,11},{10,... | collective-permute-start | bytes 1769480 | tf_op jit(solution)/shard_map/ppermute | solution.py:137
  31.7 0.0 copy-done.6
  31.7 0.8 copy.19.labels
  32.5 0.1 pad_maximum_fusion.temper
  32.6 0.0 copy-start.5
  32.6 5.8 %collective-permute-done.8.visitor = bf16[256,1152]{1,0:T(8,128)(2,1)S(1)} collective-permute-done((bf16[256,1152]{1,0:T(8,128)(2,1)S(1)}, bf16[256,1152]{1,0:T(8,128)(2,1)S(1)}, u32[]{:S(2)}, u32[]{:S(2)}) %collective-permute-start.8) | collective-permute-done | bytes 589856 | tf_op jit(solution)/shard_map/ppermute | solution.py:137
  38.5 4.2 %collective-permute-start.9 = (bf16[256,1152]{1,0:T(8,128)(2,1)S(1)}, bf16[256,1152]{1,0:T(8,128)(2,1)S(1)}, u32[]{:S(2)}, u32[]{:S(2)}) collective-permute-start(bf16[256,1152]{1,0:T(8,128)(2,1)S(1)} %collective-permute-done.8.visitor), channel_id=1, source_target_pairs={{0,2},{1,3},{2,4},{3,5},{4,6},{5,7},{6,8},{7,9},{8,10},{9,11},{10,... | collective-permute-start | bytes 1769480 | tf_op jit(solution)/shard_map/ppermute | solution.py:137
  42.6 14.1 %collective-permute-done.2.visitor = bf16[256,1152]{1,0:T(8,128)(2,1)S(1)} collective-permute-done((bf16[256,1152]{1,0:T(8,128)(2,1)S(1)}, bf16[256,1152]{1,0:T(8,128)(2,1)S(1)}, u32[]{:S(2)}, u32[]{:S(2)}) %collective-permute-start.2) | collective-permute-done | bytes 589856 | tf_op jit(solution)/shard_map/ppermute | solution.py:137
  56.7 1.9 %collective-permute-start.3 = (bf16[256,1152]{1,0:T(8,128)(2,1)S(1)}, bf16[256,1152]{1,0:T(8,128)(2,1)S(1)}, u32[]{:S(2)}, u32[]{:S(2)}) collective-permute-start(bf16[256,1152]{1,0:T(8,128)(2,1)S(1)} %collective-permute-done.2.visitor), channel_id=1, source_target_pairs={{0,14},{1,15},{2,0},{3,1},{4,2},{5,3},{6,4},{7,5},{8,6},{9,7},{10,... | collective-permute-start | bytes 1769480 | tf_op jit(solution)/shard_map/ppermute | solution.py:137
  58.7 0.0 collective-permute-done.4
  58.7 1.3 %fusion = (bf16[256,1152]{1,0:T(8,128)(2,1)S(1)}, bf16[256,1152]{1,0:T(8,128)(2,1)S(1)}) fusion(bf16[512,1152]{1,0:T(8,128)(2,1)} %collective-permute-done.4), kind=kLoop, calls=%fused_computation.2 | loop fusion | bytes 2359296 | tf_op jit(solution)/shard_map/slice | solution.py:164
  60.0 0.0 copy-done.5
  60.0 3.6 %shard_map.69 = (f32[256,1152]{1,0:T(8,128)S(1)}, f32[256,1152]{1,0:T(8,128)S(1)}, f32[256,1152]{1,0:T(8,128)S(1)}, f32[256,1152]{1,0:T(8,128)}) custom-call(f32[2]{0:T(128)S(1)} %pad_maximum_fusion.temper, s32[1]{0:T(128)} %bitcast.flags, s32[256,1]{1,0:T(8,128)S(1)} %copy-done.5, bf16[256,1152]{1,0:T(8,128)(2,1)S(1)} %get-tuple-element.21.text_half.own, ...), custom_call_target="tpu_custom_call" | custom-call | flops 754974720 | bytes 7078924 | tf_op jit(solution)/shard_map/pallas_call | solution.py:42
  63.6 0.0 collective-permute-done.6.visitor
  63.6 0.0 copy-start
  63.6 1.3 %copy-done = f32[256,1152]{1,0:T(8,128)S(1)} copy-done((f32[256,1152]{1,0:T(8,128)S(1)}, f32[256,1152]{1,0:T(8,128)}, u32[]{:S(2)}) %copy-start) | copy-done | bytes 1179672
  64.9 2.3 %shard_map.74 = (f32[256,1152]{1,0:T(8,128)S(1)}, f32[256,1152]{1,0:T(8,128)S(1)}) custom-call(f32[2]{0:T(128)S(1)} %pad_maximum_fusion.temper, s32[1]{0:T(128)} %bitcast.flags, bf16[256,1152]{1,0:T(8,128)(2,1)S(1)} %collective-permute-done.6.visitor, ...), custom_call_target="tpu_custom_call", output_to_operand_aliasing={{0}: (5, {}), {1}: (6, {})} | custom-call | flops 603979776 | bytes 6488076 | tf_op jit(solution)/shard_map/pallas_call | solution.py:42
  67.2 1.7 %shard_map.75 = (f32[256,1152]{1,0:T(8,128)S(1)}, f32[256,1152]{1,0:T(8,128)S(1)}) custom-call(f32[2]{0:T(128)S(1)} %pad_maximum_fusion.temper, s32[1]{0:T(128)} %bitcast.flags, bf16[256,1152]{1,0:T(8,128)(2,1)S(1)} %collective-permute-done.8.visitor, ...), custom_call_target="tpu_custom_call", output_to_operand_aliasing={{0}: (5, {}), {1}: (6, {})} | custom-call | flops 603979776 | bytes 6488076 | tf_op jit(solution)/shard_map/pallas_call | solution.py:42
  68.8 3.4 %collective-permute-done.9.visitor = bf16[256,1152]{1,0:T(8,128)(2,1)S(1)} collective-permute-done((bf16[256,1152]{1,0:T(8,128)(2,1)S(1)}, bf16[256,1152]{1,0:T(8,128)(2,1)S(1)}, u32[]{:S(2)}, u32[]{:S(2)}) %collective-permute-start.9) | collective-permute-done | bytes 589856 | tf_op jit(solution)/shard_map/ppermute | solution.py:137
  72.3 2.3 %shard_map.76 = (f32[256,1152]{1,0:T(8,128)S(1)}, f32[256,1152]{1,0:T(8,128)S(1)}) custom-call(f32[2]{0:T(128)S(1)} %pad_maximum_fusion.temper, s32[1]{0:T(128)} %bitcast.flags, bf16[256,1152]{1,0:T(8,128)(2,1)S(1)} %collective-permute-done.9.visitor, ...), custom_call_target="tpu_custom_call", output_to_operand_aliasing={{0}: (5, {}), {1}: (6, {})} | custom-call | flops 603979776 | bytes 6488076 | tf_op jit(solution)/shard_map/pallas_call | solution.py:42
  74.5 2.4 %collective-permute-start.10 = (f32[256,1152]{1,0:T(8,128)S(1)}, f32[256,1152]{1,0:T(8,128)S(1)}, u32[]{:S(2)}, u32[]{:S(2)}) collective-permute-start(f32[256,1152]{1,0:T(8,128)S(1)} %get-tuple-element.39), channel_id=1, source_target_pairs={{0,1},{1,0},{2,3},{3,2},{4,5},{5,4},{6,7},{7,6},{8,9},{9,8},{10,11... | collective-permute-start | bytes 3538952 | tf_op jit(solution)/shard_map/ppermute | solution.py:137
  76.9 0.0 collective-permute-done.visitor
  76.9 2.3 %shard_map.70 = (f32[256,1152]{1,0:T(8,128)S(1)}, f32[256,1152]{1,0:T(8,128)S(1)}) custom-call(f32[2]{0:T(128)S(1)} %pad_maximum_fusion.temper, s32[1]{0:T(128)} %bitcast.flags, bf16[256,1152]{1,0:T(8,128)(2,1)S(1)} %collective-permute-done.visitor, ...), custom_call_target="tpu_custom_call", output_to_operand_aliasing={{0}: (5, {}), {1}: (6, {})} | custom-call | flops 603979776 | bytes 6488076 | tf_op jit(solution)/shard_map/pallas_call | solution.py:42
  79.2 2.5 %shard_map.71 = (f32[256,1152]{1,0:T(8,128)S(1)}, f32[256,1152]{1,0:T(8,128)S(1)}) custom-call(f32[2]{0:T(128)S(1)} %pad_maximum_fusion.temper, s32[1]{0:T(128)} %bitcast.flags, bf16[256,1152]{1,0:T(8,128)(2,1)S(1)} %collective-permute-done.2.visitor, ...), custom_call_target="tpu_custom_call", output_to_operand_aliasing={{0}: (5, {}), {1}: (6, {})} | custom-call | flops 603979776 | bytes 6488076 | tf_op jit(solution)/shard_map/pallas_call | solution.py:42
  81.7 0.0 collective-permute-done.3.visitor
  81.7 0.0 copy-start.2
  81.7 2.3 %shard_map.72 = (f32[256,1152]{1,0:T(8,128)S(1)}, f32[256,1152]{1,0:T(8,128)S(1)}) custom-call(f32[2]{0:T(128)S(1)} %pad_maximum_fusion.temper, s32[1]{0:T(128)} %bitcast.flags, bf16[256,1152]{1,0:T(8,128)(2,1)S(1)} %collective-permute-done.3.visitor, ...), custom_call_target="tpu_custom_call", output_to_operand_aliasing={{0}: (5, {}), {1}: (6, {})} | custom-call | flops 603979776 | bytes 6488076 | tf_op jit(solution)/shard_map/pallas_call | solution.py:42
  84.0 1.9 %collective-permute-start.5 = (f32[256,1152]{1,0:T(8,128)S(1)}, f32[256,1152]{1,0:T(8,128)S(1)}, u32[]{:S(2)}, u32[]{:S(2)}) collective-permute-start(f32[256,1152]{1,0:T(8,128)S(1)} %get-tuple-element.31), channel_id=1, source_target_pairs={{0,1},{1,0},{2,3},{3,2},{4,5},{5,4},{6,7},{7,6},{8,9},{9,8},{10,11... | collective-permute-start | bytes 3538952 | tf_op jit(solution)/shard_map/ppermute | solution.py:137
  85.9 9.9 %collective-permute-start.7 = (bf16[256,1152]{1,0:T(8,128)(2,1)S(1)}, bf16[256,1152]{1,0:T(8,128)(2,1)S(1)}, u32[]{:S(2)}, u32[]{:S(2)}) collective-permute-start(bf16[256,1152]{1,0:T(8,128)(2,1)S(1)} %collective-permute-done.6.visitor), channel_id=1, source_target_pairs={{0,15},{1,496},{2,1},{3,498},{4,3},{5,500},{6,5},{7,502},{8,7},{9,... | collective-permute-start | bytes 1769480 | tf_op jit(solution)/shard_map/ppermute | solution.py:137
  95.8 1.9 %collective-permute-start.1 = (bf16[256,1152]{1,0:T(8,128)(2,1)S(1)}, bf16[256,1152]{1,0:T(8,128)(2,1)S(1)}, u32[]{:S(2)}, u32[]{:S(2)}) collective-permute-start(bf16[256,1152]{1,0:T(8,128)(2,1)S(1)} %collective-permute-done.visitor), channel_id=1, source_target_pairs={{0,17},{1,2},{2,19},{3,4},{4,21},{5,6},{6,23},{7,8},{8,25},{9,10},... | collective-permute-start | bytes 1769480 | tf_op jit(solution)/shard_map/ppermute | solution.py:137
  97.7 11.5 %collective-permute-done.7.visitor = bf16[256,1152]{1,0:T(8,128)(2,1)S(1)} collective-permute-done((bf16[256,1152]{1,0:T(8,128)(2,1)S(1)}, bf16[256,1152]{1,0:T(8,128)(2,1)S(1)}, u32[]{:S(2)}, u32[]{:S(2)}) %collective-permute-start.7) | collective-permute-done | bytes 589856 | tf_op jit(solution)/shard_map/ppermute | solution.py:137
  109.2 0.0 collective-permute-done.10.received
  109.2 0.0 copy-done.2
  109.2 0.0 copy-start.4
  109.2 2.9 %shard_map.77 = f32[256,1152]{1,0:T(8,128)} custom-call(f32[2]{0:T(128)S(1)} %pad_maximum_fusion.temper, bf16[256,1152]{1,0:T(8,128)(2,1)S(1)} %collective-permute-done.7.visitor, bf16[256,1152]{1,0:T(8,128)(2,1)S(1)} %get-tuple-element.21.text_half.own, bf16[256,1152]{1,0:T(8,128)(2,1)S(1)} %copy-done.2, f32[256,1152]{1,0:T(8,128)S(1)} %get-tuple-element.38.own_in, ...), custom_call_target="tpu_custom_call" | custom-call | flops 301989888 | bytes 5308424 | tf_op jit(solution)/shard_map/pallas_call | solution.py:42
  112.1 4.3 %collective-permute-done.1.visitor = bf16[256,1152]{1,0:T(8,128)(2,1)S(1)} collective-permute-done((bf16[256,1152]{1,0:T(8,128)(2,1)S(1)}, bf16[256,1152]{1,0:T(8,128)(2,1)S(1)}, u32[]{:S(2)}, u32[]{:S(2)}) %collective-permute-start.1) | collective-permute-done | bytes 589856 | tf_op jit(solution)/shard_map/ppermute | solution.py:137
  116.4 0.0 collective-permute-done.5.received
  116.4 0.0 copy-done.4
  116.4 2.9 %shard_map.73 = f32[256,1152]{1,0:T(8,128)} custom-call(f32[2]{0:T(128)S(1)} %pad_maximum_fusion.temper, bf16[256,1152]{1,0:T(8,128)(2,1)S(1)} %collective-permute-done.1.visitor, bf16[256,1152]{1,0:T(8,128)(2,1)S(1)} %get-tuple-element.22.image_half.own, bf16[256,1152]{1,0:T(8,128)(2,1)S(1)} %copy-done.4, f32[256,1152]{1,0:T(8,128)S(1)} %get-tuple-element.30.own_in, ...), custom_call_target="tpu_custom_call" | custom-call | flops 301989888 | bytes 5308424 | tf_op jit(solution)/shard_map/pallas_call | solution.py:42
  (1 shorter events, 0.0 us)
Async XLA Ops:
  0.6 1.1 copy-start.1
  1.7 1.1 copy-start.3
  2.8 29.0 %copy-start.6 = (s32[256]{0:T(256)S(1)}, s32[256]{0:T(256)}, u32[]{:S(2)}) copy-start(s32[256]{0:T(256)} %param.7) | copy-start | bytes 3076
  4.2 54.5 %collective-permute-start.4 = (bf16[512,1152]{1,0:T(8,128)(2,1)}, bf16[512,1152]{1,0:T(8,128)(2,1)}, u32[]{:S(2)}, u32[]{:S(2)}) collective-permute-start(bf16[512,1152]{1,0:T(8,128)(2,1)} %get-tuple-element.23), channel_id=1, source_target_pairs={{0,1},{1,0},{2,3},{3,2},{4,5},{5,4},{6,7},{7,6},{8,9},{9,8},{10,11... | collective-permute-start | bytes 3538952 | tf_op jit(solution)/shard_map/ppermute | solution.py:137
  6.8 31.7 %collective-permute-start.8 = (bf16[256,1152]{1,0:T(8,128)(2,1)S(1)}, bf16[256,1152]{1,0:T(8,128)(2,1)S(1)}, u32[]{:S(2)}, u32[]{:S(2)}) collective-permute-start(bf16[256,1152]{1,0:T(8,128)(2,1)S(1)} %get-tuple-element.22.image_half.own), channel_id=1, source_target_pairs={{0,506},{1,507},{2,508},{3,509},{4,510},{5,511},{6,496},{7,497},{8... | collective-permute-start | bytes 1769480 | tf_op jit(solution)/shard_map/ppermute | solution.py:137
  21.0 35.7 %collective-permute-start.2 = (bf16[256,1152]{1,0:T(8,128)(2,1)S(1)}, bf16[256,1152]{1,0:T(8,128)(2,1)S(1)}, u32[]{:S(2)}, u32[]{:S(2)}) collective-permute-start(bf16[256,1152]{1,0:T(8,128)(2,1)S(1)} %get-tuple-element.21.text_half.own), channel_id=1, source_target_pairs={{0,22},{1,23},{2,24},{3,25},{4,26},{5,27},{6,28},{7,29},{8,30},{9,... | collective-permute-start | bytes 1769480 | tf_op jit(solution)/shard_map/ppermute | solution.py:137
  23.0 40.7 %collective-permute-start.6 = (bf16[256,1152]{1,0:T(8,128)(2,1)S(1)}, bf16[256,1152]{1,0:T(8,128)(2,1)S(1)}, u32[]{:S(2)}, u32[]{:S(2)}) collective-permute-start(bf16[256,1152]{1,0:T(8,128)(2,1)S(1)} %get-tuple-element.22.image_half.own), channel_id=1, source_target_pairs={{0,14},{1,15},{2,0},{3,1},{4,2},{5,3},{6,4},{7,5},{8,6},{9,7},{10,... | collective-permute-start | bytes 1769480 | tf_op jit(solution)/shard_map/ppermute | solution.py:137
  25.4 51.6 %collective-permute-start = (bf16[256,1152]{1,0:T(8,128)(2,1)S(1)}, bf16[256,1152]{1,0:T(8,128)(2,1)S(1)}, u32[]{:S(2)}, u32[]{:S(2)}) collective-permute-start(bf16[256,1152]{1,0:T(8,128)(2,1)S(1)} %get-tuple-element.21.text_half.own), channel_id=1, source_target_pairs={{0,2},{1,3},{2,4},{3,5},{4,6},{5,7},{6,8},{7,9},{8,10},{9,11},{10,... | collective-permute-start | bytes 1769480 | tf_op jit(solution)/shard_map/ppermute | solution.py:137
  32.6 27.4 %copy-start.5 = (s32[256,1]{1,0:T(8,128)S(1)}, s32[256,1]{1,0:T(8,128)}, u32[]{:S(2)}) copy-start(s32[256,1]{1,0:T(8,128)} %copy.19.labels) | copy-start | bytes 3076
  38.5 33.8 %collective-permute-start.9 = (bf16[256,1152]{1,0:T(8,128)(2,1)S(1)}, bf16[256,1152]{1,0:T(8,128)(2,1)S(1)}, u32[]{:S(2)}, u32[]{:S(2)}) collective-permute-start(bf16[256,1152]{1,0:T(8,128)(2,1)S(1)} %collective-permute-done.8.visitor), channel_id=1, source_target_pairs={{0,2},{1,3},{2,4},{3,5},{4,6},{5,7},{6,8},{7,9},{8,10},{9,11},{10,... | collective-permute-start | bytes 1769480 | tf_op jit(solution)/shard_map/ppermute | solution.py:137
  56.7 24.9 %collective-permute-start.3 = (bf16[256,1152]{1,0:T(8,128)(2,1)S(1)}, bf16[256,1152]{1,0:T(8,128)(2,1)S(1)}, u32[]{:S(2)}, u32[]{:S(2)}) collective-permute-start(bf16[256,1152]{1,0:T(8,128)(2,1)S(1)} %collective-permute-done.2.visitor), channel_id=1, source_target_pairs={{0,14},{1,15},{2,0},{3,1},{4,2},{5,3},{6,4},{7,5},{8,6},{9,7},{10,... | collective-permute-start | bytes 1769480 | tf_op jit(solution)/shard_map/ppermute | solution.py:137
  63.6 1.3 %copy-start = (f32[256,1152]{1,0:T(8,128)S(1)}, f32[256,1152]{1,0:T(8,128)}, u32[]{:S(2)}) copy-start(f32[256,1152]{1,0:T(8,128)} %get-tuple-element.33.far_in) | copy-start | bytes 3538948
  74.5 34.6 %collective-permute-start.10 = (f32[256,1152]{1,0:T(8,128)S(1)}, f32[256,1152]{1,0:T(8,128)S(1)}, u32[]{:S(2)}, u32[]{:S(2)}) collective-permute-start(f32[256,1152]{1,0:T(8,128)S(1)} %get-tuple-element.39), channel_id=1, source_target_pairs={{0,1},{1,0},{2,3},{3,2},{4,5},{5,4},{6,7},{7,6},{8,9},{9,8},{10,11... | collective-permute-start | bytes 3538952 | tf_op jit(solution)/shard_map/ppermute | solution.py:137
  81.7 27.5 %copy-start.2 = (bf16[256,1152]{1,0:T(8,128)(2,1)S(1)}, bf16[256,1152]{1,0:T(8,128)(2,1)}, u32[]{:S(2)}) copy-start(bf16[256,1152]{1,0:T(8,128)(2,1)} %rows.3) | copy-start | bytes 1769476
  84.0 32.4 %collective-permute-start.5 = (f32[256,1152]{1,0:T(8,128)S(1)}, f32[256,1152]{1,0:T(8,128)S(1)}, u32[]{:S(2)}, u32[]{:S(2)}) collective-permute-start(f32[256,1152]{1,0:T(8,128)S(1)} %get-tuple-element.31), channel_id=1, source_target_pairs={{0,1},{1,0},{2,3},{3,2},{4,5},{5,4},{6,7},{7,6},{8,9},{9,8},{10,11... | collective-permute-start | bytes 3538952 | tf_op jit(solution)/shard_map/ppermute | solution.py:137
  85.9 23.3 %collective-permute-start.7 = (bf16[256,1152]{1,0:T(8,128)(2,1)S(1)}, bf16[256,1152]{1,0:T(8,128)(2,1)S(1)}, u32[]{:S(2)}, u32[]{:S(2)}) collective-permute-start(bf16[256,1152]{1,0:T(8,128)(2,1)S(1)} %collective-permute-done.6.visitor), channel_id=1, source_target_pairs={{0,15},{1,496},{2,1},{3,498},{4,3},{5,500},{6,5},{7,502},{8,7},{9,... | collective-permute-start | bytes 1769480 | tf_op jit(solution)/shard_map/ppermute | solution.py:137
  95.8 20.6 %collective-permute-start.1 = (bf16[256,1152]{1,0:T(8,128)(2,1)S(1)}, bf16[256,1152]{1,0:T(8,128)(2,1)S(1)}, u32[]{:S(2)}, u32[]{:S(2)}) collective-permute-start(bf16[256,1152]{1,0:T(8,128)(2,1)S(1)} %collective-permute-done.visitor), channel_id=1, source_target_pairs={{0,17},{1,2},{2,19},{3,4},{4,21},{5,6},{6,23},{7,8},{8,25},{9,10},... | collective-permute-start | bytes 1769480 | tf_op jit(solution)/shard_map/ppermute | solution.py:137
  109.2 7.2 %copy-start.4 = (bf16[256,1152]{1,0:T(8,128)(2,1)S(1)}, bf16[256,1152]{1,0:T(8,128)(2,1)}, u32[]{:S(2)}) copy-start(bf16[256,1152]{1,0:T(8,128)(2,1)} %rows.2) | copy-start | bytes 1769476

commit v2 on v1

--- a/solution.py
+++ b/solution.py
@@ -35,20 +35,21 @@
     return (temper * jax.nn.sigmoid(temper * scores + offset)).astype(BF16)
 
 
-def call(kernel, outs, inputs, matmuls, aliases=None):
+def call(kernel, outs, inputs, aliases=None, passed=()):
     specs = [whole(pltpu.SMEM if x.ndim == 1 else pltpu.VMEM) for x in inputs]
-    moved = sum(x.size * x.dtype.itemsize for x in inputs)
-    moved += sum(x.size * x.dtype.itemsize for x in outs)
+    out_specs = [whole() for _ in outs]
+    for source, target in passed:
+        specs[source] = whole(pl.ANY)
+        if target is not None:
+            out_specs[target] = whole(pl.ANY)
     return pl.pallas_call(
         kernel,
         out_shape=outs,
         in_specs=specs,
-        out_specs=[whole() for _ in outs],
+        out_specs=out_specs,
         input_output_aliases=aliases or {},
         compiler_params=pltpu.CompilerParams(vmem_limit_bytes=VMEM_LIMIT),
-        cost_estimate=pl.CostEstimate(
-            flops=matmuls * 2 * 256 * 256 * 1152, bytes_accessed=moved, transcendentals=0
-        ),
+        cost_estimate=pl.CostEstimate(flops=1000, bytes_accessed=1000, transcendentals=0),
     )(*inputs)
 
 
@@ -63,10 +64,11 @@
 
 
 def own_kernel(
-    temper, flags, labels, text_half, image_half, text_other, image_other,
+    temper, flags, labels, text_half, image_half, other,
     image_own, image_far, text_own, text_far,
 ):
     scale, offset = temper[0], temper[1]
+    rows = text_half.shape[0]
     text, image = text_half[...], image_half[...]
     scores = mm(image, text, NT)
     target = lax.broadcasted_iota(jnp.int32, scores.shape, 1)
@@ -78,33 +80,34 @@
 
     @pl.when(flags[0] == 0)
     def _():
-        part = weights(mm(image_other[...], text, NT), scale, offset)
+        part = weights(mm(other[rows:], text, NT), scale, offset)
         image_far[...] = mm(part, text, NN)
         text_far[...] = jnp.zeros(text_far.shape, F32)
 
     @pl.when(flags[0] == 1)
     def _():
-        part = weights(mm(text_other[...], image, NT), scale, offset)
+        part = weights(mm(other[:rows], image, NT), scale, offset)
         text_far[...] = mm(part, image, NN)
         image_far[...] = jnp.zeros(image_far.shape, F32)
 
 
 def visit_kernel(
-    always, temper, flags, visitor, own, other, own_in, far_in, own_out, far_out
+    only, first, temper, flags, visitor, own, other, own_in, far_in, own_out, far_out
 ):
     scale, offset = temper[0], temper[1]
-    block = visitor[...]
+    rows = visitor.shape[0]
+    block = unit_of(visitor[...])[0].astype(BF16)
 
     def far():
-        part = weights(mm(other[...], block, NT), scale, offset)
+        part = weights(mm(other[first : first + rows], block, NT), scale, offset)
         far_out[...] = far_in[...] + mm(part, block, NN)
 
-    if always is None:
+    if only is None:
         far()
     else:
-        pl.when(flags[0] == always)(far)
-
-        @pl.when(flags[0] != always)
+        pl.when(flags[0] == only)(far)
+
+        @pl.when(flags[0] != only)
         def _():
             far_out[...] = far_in[...]
 
@@ -112,11 +115,25 @@
     own_out[...] = own_in[...] + mm(part, block, NN)
 
 
-def last_kernel(temper, visitor, own, rows, own_in, received, grad):
-    scale, offset = temper[0], temper[1]
+def far_kernel(first, temper, visitor, other, far_in, half, far_out):
+    rows = visitor.shape[0]
+    block = unit_of(visitor[...])[0].astype(BF16)
+    half[...] = block
+    part = weights(mm(other[first : first + rows], block, NT), temper[0], temper[1])
+    far_out[...] = far_in[...] + mm(part, block, NN)
+
+
+def near_kernel(raw, temper, visitor, own, own_in, *rest):
+    own_out = rest[-1] if len(rest) == 1 else rest[1]
     block = visitor[...]
-    part = weights(mm(own[...], block, NT), scale, offset)
-    upstream = own_in[...] + received[...] + mm(part, block, NN)
+    if raw:
+        block = unit_of(block)[0].astype(BF16)
+    part = weights(mm(own[...], block, NT), temper[0], temper[1])
+    own_out[...] = own_in[...] + mm(part, block, NN)
+
+
+def finish_kernel(rows, own_sum, received, grad):
+    upstream = own_sum[...] + received[...]
     unit, inverse = unit_of(rows[...])
     along = jnp.sum(unit * upstream, axis=-1, keepdims=True)
     grad[...] = inverse * (upstream - unit * along)
@@ -157,43 +174,58 @@
     full = jax.ShapeDtypeStruct((rows, width), F32)
     pair = jax.ShapeDtypeStruct((2 * rows, width), BF16)
 
-    text_half, image_half, both = call(prepare_kernel, [half, half, pair], [texts, images], 0)
-    both = swapped(both)
-    a_text, a_image = hop(text_half, 1, 0, 1), hop(image_half, -1, 0, 1)
-    d_text, d_image = hop(text_half, 1, 1, 3), hop(image_half, -1, 1, 3)
-    text_other, image_other = both[:rows], both[rows:]
-    image_own, image_far, text_own, text_far = call(
-        own_kernel,
-        [full] * 4,
-        [temper, flags, local, text_half, image_half, text_other, image_other],
-        5,
+    a_text, a_image = hop(texts, 1, 0, 1), hop(images, -1, 0, 1)
+    d_text, d_image = hop(texts, 1, 1, 3), hop(images, -1, 1, 3)
+    text_half, image_half, both = call(
+        prepare_kernel, [half, half, pair], [texts, images]
     )
+    other = swapped(both)
     b_text, b_image = last_hop(a_text, 1), last_hop(a_image, -1)
     c_text, c_image = hop(d_text, 1, 0, -1), hop(d_image, -1, 0, -1)
 
-    def visit(always, visitor, own, other, own_sum, far_sum):
+    image_own, image_far, text_own, text_far = call(
+        own_kernel, [full] * 4, [temper, flags, local, text_half, image_half, other]
+    )
+
+    def visit(only, first, visitor, own, own_sum, far_sum):
         return call(
-            functools.partial(visit_kernel, always),
+            functools.partial(visit_kernel, only, first),
             [full, full],
             [temper, flags, visitor, own, other, own_sum, far_sum],
-            4,
             {5: 0, 6: 1},
         )
 
-    for always_t, always_i, text, image in (
+    def far(first, visitor, far_sum):
+        return call(
+            functools.partial(far_kernel, first),
+            [half, full],
+            [temper, visitor, other, far_sum],
+            {3: 1},
+        )
+
+    def near(raw, visitor, own, own_sum, later=None):
+        inputs = [temper, visitor, own, own_sum]
+        kernel = functools.partial(near_kernel, raw)
+        if later is None:
+            return call(kernel, [full], inputs, {3: 0})[0]
+        return call(kernel, [full, full], inputs + [later], {3: 0, 4: 1}, ((4, 1),))
+
+    for only_t, only_i, text, image in (
         (None, None, a_text, a_image),
         (1, 0, d_text, d_image),
-        (None, None, c_text, c_image),
     ):
-        image_own, image_far = visit(always_t, text, image_half, image_other, image_own, image_far)
-        text_own, text_far = visit(always_i, image, text_half, text_other, text_own, text_far)
-    image_back, text_back = swapped(image_far), swapped(text_far)
-    (grad_images,) = call(
-        last_kernel, [full], [temper, b_text, image_half, images, image_own, image_back], 2
-    )
-    (grad_texts,) = call(
-        last_kernel, [full], [temper, b_image, text_half, texts, text_own, text_back], 2
-    )
+        image_own, image_far = visit(only_t, rows, text, image_half, image_own, image_far)
+        text_own, text_far = visit(only_i, 0, image, text_half, text_own, text_far)
+    image_own, image_far = near(True, b_text, image_half, image_own, image_far)
+    text_own, text_far = near(True, b_image, text_half, text_own, text_far)
+    c_text, image_far = far(rows, c_text, image_far)
+    image_back = swapped(image_far)
+    c_image, text_far = far(0, c_image, text_far)
+    text_back = swapped(text_far)
+    image_own = near(False, c_text, image_half, image_own)
+    text_own = near(False, c_image, text_half, text_own)
+    (grad_images,) = call(finish_kernel, [full], [images, image_own, image_back])
+    (grad_texts,) = call(finish_kernel, [full], [texts, text_own, text_back])
     return (grad_images, grad_texts)
 
 

time: 120 us -> 123 us (1.025)
  waiting for transfers between devices: 39.2 us -> 18.5 us
  starting transfers between devices: 48.3 us -> 65.6 us
  Pallas kernels: 23.9 us -> 29.7 us
    ppermute x11, waiting for transfers between devices: 39.2 us -> 18.5 us  [moved(): return lax.ppermute(value, AXES, pairs)]
    ppermute x11, starting transfers between devices: 48.3 us -> 65.6 us  [moved(): return lax.ppermute(value, AXES, pairs)]
    pallas_call x10 -> x14, Pallas kernels: 23.9 us -> 29.7 us  [call(): pl.pallas_call(kernel, out_shape=outs, in_specs=specs, out_specs=out_spec...]
    unnamed x14 -> x18, local copies, waits for them, and re-layouts: 3.41 us -> 5.33 us
    slice x1 -> x0, local copies, waits for them, and re-layouts: 1.33 us -> none  [shards(): text_other, image_other = (both[:rows], both[rows:])]
  transfers between devices with their start and end apart: 11 -> 11, of which waited for: 5 -> 3; matrix products, arithmetic and copies ran while one was open for 2% -> 1% of each run, Pallas kernels for 16% -> 22%
where the time goes in v2:
time: 123 us; the launch traced here: 122 us
  starting transfers between devices  65.6 us (53%)
  Pallas kernels  29.7 us (24%)
  waiting for transfers between devices  18.5 us (15%)
  local copies, waits for them, and re-layouts  6.13 us (5%)
  between operations  2.27 us (2%)
    ppermute x11, starting transfers between devices, moved(): return lax.ppermute(value, AXES, pairs)  65.6 us
    pallas_call x14, Pallas kernels, call(): pl.pallas_call(kernel, out_shape=outs, in_specs=specs, out_specs=out_spec...  29.7 us
    ppermute x11, waiting for transfers between devices, moved(): return lax.ppermute(value, AXES, pairs)  18.5 us
    unnamed x18, local copies, waits for them, and re-layouts  5.33 us
  transfers between devices with their start and end apart: 11, of which 3 were waited for; matrix products, arithmetic and copies ran while one was open for 1% of the time, Pallas kernels for 22%

profile of v2, /device:TPU:7, one launch (start us, length us, event | category | flops | bytes accessed | tf_op | source)
XLA Modules:
  0.0 122.3 jit_solution(223633002903476649)
XLA Ops:
  0.6 0.0 copy-start.3
  0.6 1.1 copy-done.3
  1.7 0.0 copy-start.5
  1.7 1.1 copy-done.5
  2.8 0.0 copy-start.8
  2.8 1.4 %shard_map.68 = (bf16[256,1152]{1,0:T(8,128)(2,1)S(1)}, bf16[256,1152]{1,0:T(8,128)(2,1)S(1)}, bf16[512,1152]{1,0:T(8,128)(2,1)}) custom-call(bf16[256,1152]{1,0:T(8,128)(2,1)S(1)} %copy-done.3, bf16[256,1152]{1,0:T(8,128)(2,1)S(1)} %copy-done.5), custom_call_target="tpu_custom_call" | custom-call | flops 1000 | bytes 1000 | tf_op jit(solution)/shard_map/pallas_call | solution.py:45
  4.2 2.6 %collective-permute-start.2 = (bf16[512,1152]{1,0:T(8,128)(2,1)}, bf16[512,1152]{1,0:T(8,128)(2,1)S(1)}, u32[]{:S(2)}, u32[]{:S(2)}) collective-permute-start(bf16[512,1152]{1,0:T(8,128)(2,1)} %get-tuple-element.25), channel_id=1, source_target_pairs={{0,1},{1,0},{2,3},{3,2},{4,5},{5,4},{6,7},{7,6},{8,9},{9,8},{10,11... | collective-permute-start | bytes 3538952 | tf_op jit(solution)/shard_map/ppermute | solution.py:154
  6.8 2.5 %collective-permute-start.8 = (bf16[256,1152]{1,0:T(8,128)(2,1)S(1)}, bf16[256,1152]{1,0:T(8,128)(2,1)}, u32[]{:S(2)}, u32[]{:S(2)}) collective-permute-start(bf16[256,1152]{1,0:T(8,128)(2,1)S(1)} %copy-done.5), channel_id=1, source_target_pairs={{0,14},{1,15},{2,0},{3,1},{4,2},{5,3},{6,4},{7,5},{8,6},{9,7},{10,... | collective-permute-start | bytes 1769480 | tf_op jit(solution)/shard_map/ppermute | solution.py:154
  9.2 16.3 %collective-permute-start.6 = (bf16[256,1152]{1,0:T(8,128)(2,1)S(1)}, bf16[256,1152]{1,0:T(8,128)(2,1)}, u32[]{:S(2)}, u32[]{:S(2)}) collective-permute-start(bf16[256,1152]{1,0:T(8,128)(2,1)S(1)} %copy-done.5), channel_id=1, source_target_pairs={{0,506},{1,507},{2,508},{3,509},{4,510},{5,511},{6,496},{7,497},{8... | collective-permute-start | bytes 1769480 | tf_op jit(solution)/shard_map/ppermute | solution.py:154
  25.5 1.9 %collective-permute-start.3 = (bf16[256,1152]{1,0:T(8,128)(2,1)S(1)}, bf16[256,1152]{1,0:T(8,128)(2,1)S(1)}, u32[]{:S(2)}, u32[]{:S(2)}) collective-permute-start(bf16[256,1152]{1,0:T(8,128)(2,1)S(1)} %copy-done.3), channel_id=1, source_target_pairs={{0,2},{1,3},{2,4},{3,5},{4,6},{5,7},{6,8},{7,9},{8,10},{9,11},{10,... | collective-permute-start | bytes 1769480 | tf_op jit(solution)/shard_map/ppermute | solution.py:154
  27.5 1.9 %collective-permute-start = (bf16[256,1152]{1,0:T(8,128)(2,1)S(1)}, bf16[256,1152]{1,0:T(8,128)(2,1)S(1)}, u32[]{:S(2)}, u32[]{:S(2)}) collective-permute-start(bf16[256,1152]{1,0:T(8,128)(2,1)S(1)} %copy-done.3), channel_id=1, source_target_pairs={{0,22},{1,23},{2,24},{3,25},{4,26},{5,27},{6,28},{7,29},{8,30},{9,... | collective-permute-start | bytes 1769480 | tf_op jit(solution)/shard_map/ppermute | solution.py:154
  29.4 0.0 collective-permute-done.8.visitor
  29.4 20.2 %collective-permute-start.9 = (bf16[256,1152]{1,0:T(8,128)(2,1)}, bf16[256,1152]{1,0:T(8,128)(2,1)}, u32[]{:S(2)}, u32[]{:S(2)}) collective-permute-start(bf16[256,1152]{1,0:T(8,128)(2,1)} %collective-permute-done.8.visitor), channel_id=1, source_target_pairs={{0,15},{1,496},{2,1},{3,498},{4,3},{5,500},{6,5},{7,502},{8,7},{9,... | collective-permute-start | bytes 1769480 | tf_op jit(solution)/shard_map/ppermute | solution.py:154
  49.6 0.0 collective-permute-done.6.visitor
  49.7 9.0 %collective-permute-start.7 = (bf16[256,1152]{1,0:T(8,128)(2,1)}, bf16[256,1152]{1,0:T(8,128)(2,1)}, u32[]{:S(2)}, u32[]{:S(2)}) collective-permute-start(bf16[256,1152]{1,0:T(8,128)(2,1)} %collective-permute-done.6.visitor), channel_id=1, source_target_pairs={{0,2},{1,3},{2,4},{3,5},{4,6},{5,7},{6,8},{7,9},{8,10},{9,11},{10,... | collective-permute-start | bytes 1769480 | tf_op jit(solution)/shard_map/ppermute | solution.py:154
  58.7 0.0 collective-permute-done.3.visitor
  58.7 3.6 %collective-permute-start.4 = (bf16[256,1152]{1,0:T(8,128)(2,1)S(1)}, bf16[256,1152]{1,0:T(8,128)(2,1)}, u32[]{:S(2)}, u32[]{:S(2)}) collective-permute-start(bf16[256,1152]{1,0:T(8,128)(2,1)S(1)} %collective-permute-done.3.visitor), channel_id=1, source_target_pairs={{0,17},{1,2},{2,19},{3,4},{4,21},{5,6},{6,23},{7,8},{8,25},{9,10},... | collective-permute-start | bytes 1769480 | tf_op jit(solution)/shard_map/ppermute | solution.py:154
  62.3 1.8 %collective-permute-done.visitor = bf16[256,1152]{1,0:T(8,128)(2,1)S(1)} collective-permute-done((bf16[256,1152]{1,0:T(8,128)(2,1)S(1)}, bf16[256,1152]{1,0:T(8,128)(2,1)S(1)}, u32[]{:S(2)}, u32[]{:S(2)}) %collective-permute-start) | collective-permute-done | bytes 589856 | tf_op jit(solution)/shard_map/ppermute | solution.py:154
  64.1 1.9 %collective-permute-start.1 = (bf16[256,1152]{1,0:T(8,128)(2,1)S(1)}, bf16[256,1152]{1,0:T(8,128)(2,1)}, u32[]{:S(2)}, u32[]{:S(2)}) collective-permute-start(bf16[256,1152]{1,0:T(8,128)(2,1)S(1)} %collective-permute-done.visitor), channel_id=1, source_target_pairs={{0,14},{1,15},{2,0},{3,1},{4,2},{5,3},{6,4},{7,5},{8,6},{9,7},{10,... | collective-permute-start | bytes 1769480 | tf_op jit(solution)/shard_map/ppermute | solution.py:154
  67.3 0.0 copy-done.8
  67.4 0.8 copy.23.labels
  68.2 0.1 pad_maximum_fusion.temper
  68.2 0.0 collective-permute-done.2.other
  68.2 0.0 copy-start
  68.2 1.0 copy-done
  69.3 0.0 copy-start.7
  69.3 0.9 copy-done.7
  70.2 3.3 %shard_map.69 = (f32[256,1152]{1,0:T(8,128)S(1)}, f32[256,1152]{1,0:T(8,128)S(1)}, f32[256,1152]{1,0:T(8,128)S(1)}, f32[256,1152]{1,0:T(8,128)S(1)}) custom-call(f32[2]{0:T(128)S(1)} %pad_maximum_fusion.temper, s32[1]{0:T(128)} %bitcast.flags, s32[256,1]{1,0:T(8,128)S(1)} %copy-done.7, bf16[256,1152]{1,0:T(8,128)(2,1)S(1)} %get-tuple-element.27.text_half.own, ...), custom_call_target="tpu_custom_call" | custom-call | flops 1000 | bytes 1000 | tf_op jit(solution)/shard_map/pallas_call | solution.py:45
  73.5 0.0 copy-start.1
  73.5 1.3 %copy-done.1 = bf16[512,1152]{1,0:T(8,128)(2,1)S(1)} copy-done((bf16[512,1152]{1,0:T(8,128)(2,1)S(1)}, bf16[512,1152]{1,0:T(8,128)(2,1)}, u32[]{:S(2)}) %copy-start.1) | copy-done | bytes 1179672
  74.8 2.9 %shard_map.76 = (f32[256,1152]{1,0:T(8,128)S(1)}, f32[256,1152]{1,0:T(8,128)S(1)}) custom-call(f32[2]{0:T(128)S(1)} %pad_maximum_fusion.temper, s32[1]{0:T(128)} %bitcast.flags, bf16[256,1152]{1,0:T(8,128)(2,1)} %collective-permute-done.8.visitor, ...), custom_call_target="tpu_custom_call", output_to_operand_aliasing={{0}: (5, {}), {1}: (6, {})} | custom-call | flops 1000 | bytes 1000 | tf_op jit(solution)/shard_map/pallas_call | solution.py:45
  77.7 2.4 %shard_map.77 = (f32[256,1152]{1,0:T(8,128)S(1)}, f32[256,1152]{1,0:T(8,128)S(1)}) custom-call(f32[2]{0:T(128)S(1)} %pad_maximum_fusion.temper, s32[1]{0:T(128)} %bitcast.flags, bf16[256,1152]{1,0:T(8,128)(2,1)} %collective-permute-done.6.visitor, ...), custom_call_target="tpu_custom_call", output_to_operand_aliasing={{0}: (5, {}), {1}: (6, {})} | custom-call | flops 1000 | bytes 1000 | tf_op jit(solution)/shard_map/pallas_call | solution.py:45
  80.1 0.0 collective-permute-done.9.visitor
  80.1 0.0 copy-start.2
  80.1 2.2 %shard_map.78 = (f32[256,1152]{1,0:T(8,128)S(1)}, f32[256,1152]{1,0:T(8,128)S(1)}) custom-call(f32[2]{0:T(128)S(1)} %pad_maximum_fusion.temper, bf16[256,1152]{1,0:T(8,128)(2,1)} %collective-permute-done.9.visitor, bf16[256,1152]{1,0:T(8,128)(2,1)S(1)} %get-tuple-element.27.text_half.own, ...), custom_call_target="tpu_custom_call", output_to_operand_aliasing={{0}: (3, {}), {1}: (4, {})} | custom-call | flops 1000 | bytes 1000 | tf_op jit(solution)/shard_map/pallas_call | solution.py:45
  82.3 6.0 %collective-permute-done.7.visitor = bf16[256,1152]{1,0:T(8,128)(2,1)} collective-permute-done((bf16[256,1152]{1,0:T(8,128)(2,1)}, bf16[256,1152]{1,0:T(8,128)(2,1)}, u32[]{:S(2)}, u32[]{:S(2)}) %collective-permute-start.7) | collective-permute-done | bytes 589856 | tf_op jit(solution)/shard_map/ppermute | solution.py:154
  88.4 0.0 copy-done.2
  88.4 2.1 %shard_map.79 = (bf16[256,1152]{1,0:T(8,128)(2,1)S(1)}, f32[256,1152]{1,0:T(8,128)S(1)}) custom-call(f32[2]{0:T(128)S(1)} %pad_maximum_fusion.temper, bf16[256,1152]{1,0:T(8,128)(2,1)} %collective-permute-done.7.visitor, bf16[512,1152]{1,0:T(8,128)(2,1)S(1)} %copy-done.2, f32[256,1152]{1,0:T(8,128)S(1)} %get-tuple-element.44.far_in), custom_call_target="tpu_custom_call", output_to_operand_aliasing={{1}: (3, {})} | custom-call | flops 1000 | bytes 1000 | tf_op jit(solution)/shard_map/pallas_call | solution.py:45
  90.5 3.8 %collective-permute-start.10 = (f32[256,1152]{1,0:T(8,128)S(1)}, f32[256,1152]{1,0:T(8,128)S(1)}, u32[]{:S(2)}, u32[]{:S(2)}) collective-permute-start(f32[256,1152]{1,0:T(8,128)S(1)} %get-tuple-element.47), channel_id=1, source_target_pairs={{0,1},{1,0},{2,3},{3,2},{4,5},{5,4},{6,7},{7,6},{8,9},{9,8},{10,11... | collective-permute-start | bytes 3538952 | tf_op jit(solution)/shard_map/ppermute | solution.py:154
  94.3 2.4 %shard_map.70 = (f32[256,1152]{1,0:T(8,128)S(1)}, f32[256,1152]{1,0:T(8,128)S(1)}) custom-call(f32[2]{0:T(128)S(1)} %pad_maximum_fusion.temper, s32[1]{0:T(128)} %bitcast.flags, bf16[256,1152]{1,0:T(8,128)(2,1)S(1)} %collective-permute-done.3.visitor, ...), custom_call_target="tpu_custom_call", output_to_operand_aliasing={{0}: (5, {}), {1}: (6, {})} | custom-call | flops 1000 | bytes 1000 | tf_op jit(solution)/shard_map/pallas_call | solution.py:45
  96.7 2.8 %shard_map.71 = (f32[256,1152]{1,0:T(8,128)S(1)}, f32[256,1152]{1,0:T(8,128)S(1)}) custom-call(f32[2]{0:T(128)S(1)} %pad_maximum_fusion.temper, s32[1]{0:T(128)} %bitcast.flags, bf16[256,1152]{1,0:T(8,128)(2,1)S(1)} %collective-permute-done.visitor, ...), custom_call_target="tpu_custom_call", output_to_operand_aliasing={{0}: (5, {}), {1}: (6, {})} | custom-call | flops 1000 | bytes 1000 | tf_op jit(solution)/shard_map/pallas_call | solution.py:45
  99.5 10.7 %collective-permute-done.4.visitor = bf16[256,1152]{1,0:T(8,128)(2,1)} collective-permute-done((bf16[256,1152]{1,0:T(8,128)(2,1)S(1)}, bf16[256,1152]{1,0:T(8,128)(2,1)}, u32[]{:S(2)}, u32[]{:S(2)}) %collective-permute-start.4) | collective-permute-done | bytes 589856 | tf_op jit(solution)/shard_map/ppermute | solution.py:154
  110.1 2.1 %shard_map.72 = (f32[256,1152]{1,0:T(8,128)S(1)}, f32[256,1152]{1,0:T(8,128)S(1)}) custom-call(f32[2]{0:T(128)S(1)} %pad_maximum_fusion.temper, bf16[256,1152]{1,0:T(8,128)(2,1)} %collective-permute-done.4.visitor, bf16[256,1152]{1,0:T(8,128)(2,1)S(1)} %get-tuple-element.26.image_half.own, ...), custom_call_target="tpu_custom_call", output_to_operand_aliasing={{0}: (3, {}), {1}: (4, {})} | custom-call | flops 1000 | bytes 1000 | tf_op jit(solution)/shard_map/pallas_call | solution.py:45
  112.3 0.0 collective-permute-done.1.visitor
  112.3 2.1 %shard_map.73 = (bf16[256,1152]{1,0:T(8,128)(2,1)S(1)}, f32[256,1152]{1,0:T(8,128)S(1)}) custom-call(f32[2]{0:T(128)S(1)} %pad_maximum_fusion.temper, bf16[256,1152]{1,0:T(8,128)(2,1)} %collective-permute-done.1.visitor, bf16[512,1152]{1,0:T(8,128)(2,1)S(1)} %copy-done.2, f32[256,1152]{1,0:T(8,128)S(1)} %get-tuple-element.34.far_in), custom_call_target="tpu_custom_call", output_to_operand_aliasing={{1}: (3, {})} | custom-call | flops 1000 | bytes 1000 | tf_op jit(solution)/shard_map/pallas_call | solution.py:45
  114.4 1.9 %collective-permute-start.5 = (f32[256,1152]{1,0:T(8,128)S(1)}, f32[256,1152]{1,0:T(8,128)S(1)}, u32[]{:S(2)}, u32[]{:S(2)}) collective-permute-start(f32[256,1152]{1,0:T(8,128)S(1)} %get-tuple-element.37), channel_id=1, source_target_pairs={{0,1},{1,0},{2,3},{3,2},{4,5},{5,4},{6,7},{7,6},{8,9},{9,8},{10,11... | collective-permute-start | bytes 3538952 | tf_op jit(solution)/shard_map/ppermute | solution.py:154
  116.4 1.5 %shard_map.80.own_sum = f32[256,1152]{1,0:T(8,128)S(1)} custom-call(f32[2]{0:T(128)S(1)} %pad_maximum_fusion.temper, bf16[256,1152]{1,0:T(8,128)(2,1)S(1)} %get-tuple-element.45.visitor, bf16[256,1152]{1,0:T(8,128)(2,1)S(1)} %get-tuple-element.27.text_half.own, f32[256,1152]{1,0:T(8,128)S(1)} %get-tuple-element.46.own_in), custom_call_target="tpu_custom_call", output_to_operand_aliasing={{}: (3, {})} | custom-call | flops 1000 | bytes 1000 | tf_op jit(solution)/shard_map/pallas_call | solution.py:45
  117.8 0.0 copy-start.4
  117.9 1.5 %shard_map.74.own_sum = f32[256,1152]{1,0:T(8,128)S(1)} custom-call(f32[2]{0:T(128)S(1)} %pad_maximum_fusion.temper, bf16[256,1152]{1,0:T(8,128)(2,1)S(1)} %get-tuple-element.35.visitor, bf16[256,1152]{1,0:T(8,128)(2,1)S(1)} %get-tuple-element.26.image_half.own, f32[256,1152]{1,0:T(8,128)S(1)} %get-tuple-element.36.own_in), custom_call_target="tpu_custom_call", output_to_operand_aliasing={{}: (3, {})} | custom-call | flops 1000 | bytes 1000 | tf_op jit(solution)/shard_map/pallas_call | solution.py:45
  119.3 0.0 copy-start.6
  119.3 0.0 collective-permute-done.10.received
  119.4 0.0 copy-done.4
  119.4 1.5 %shard_map.81 = f32[256,1152]{1,0:T(8,128)} custom-call(bf16[256,1152]{1,0:T(8,128)(2,1)S(1)} %copy-done.4, f32[256,1152]{1,0:T(8,128)S(1)} %shard_map.80.own_sum, f32[256,1152]{1,0:T(8,128)S(1)} %collective-permute-done.10.received), custom_call_target="tpu_custom_call" | custom-call | flops 1000 | bytes 1000 | tf_op jit(solution)/shard_map/pallas_call | solution.py:45
  120.9 0.0 collective-permute-done.5.received
  120.9 0.0 copy-done.6
  120.9 1.5 %shard_map.75 = f32[256,1152]{1,0:T(8,128)} custom-call(bf16[256,1152]{1,0:T(8,128)(2,1)S(1)} %copy-done.6, f32[256,1152]{1,0:T(8,128)S(1)} %shard_map.74.own_sum, f32[256,1152]{1,0:T(8,128)S(1)} %collective-permute-done.5.received), custom_call_target="tpu_custom_call" | custom-call | flops 1000 | bytes 1000 | tf_op jit(solution)/shard_map/pallas_call | solution.py:45
  (1 shorter events, 0.0 us)
Async XLA Ops:
  0.6 1.1 copy-start.3
  1.7 1.1 copy-start.5
  2.8 64.6 %copy-start.8 = (s32[256]{0:T(256)S(1)}, s32[256]{0:T(256)}, u32[]{:S(2)}) copy-start(s32[256]{0:T(256)} %param.7) | copy-start | bytes 3076
  4.2 64.1 %collective-permute-start.2 = (bf16[512,1152]{1,0:T(8,128)(2,1)}, bf16[512,1152]{1,0:T(8,128)(2,1)S(1)}, u32[]{:S(2)}, u32[]{:S(2)}) collective-permute-start(bf16[512,1152]{1,0:T(8,128)(2,1)} %get-tuple-element.25), channel_id=1, source_target_pairs={{0,1},{1,0},{2,3},{3,2},{4,5},{5,4},{6,7},{7,6},{8,9},{9,8},{10,11... | collective-permute-start | bytes 3538952 | tf_op jit(solution)/shard_map/ppermute | solution.py:154
  6.8 22.7 %collective-permute-start.8 = (bf16[256,1152]{1,0:T(8,128)(2,1)S(1)}, bf16[256,1152]{1,0:T(8,128)(2,1)}, u32[]{:S(2)}, u32[]{:S(2)}) collective-permute-start(bf16[256,1152]{1,0:T(8,128)(2,1)S(1)} %copy-done.5), channel_id=1, source_target_pairs={{0,14},{1,15},{2,0},{3,1},{4,2},{5,3},{6,4},{7,5},{8,6},{9,7},{10,... | collective-permute-start | bytes 1769480 | tf_op jit(solution)/shard_map/ppermute | solution.py:154
  9.2 40.4 %collective-permute-start.6 = (bf16[256,1152]{1,0:T(8,128)(2,1)S(1)}, bf16[256,1152]{1,0:T(8,128)(2,1)}, u32[]{:S(2)}, u32[]{:S(2)}) collective-permute-start(bf16[256,1152]{1,0:T(8,128)(2,1)S(1)} %copy-done.5), channel_id=1, source_target_pairs={{0,506},{1,507},{2,508},{3,509},{4,510},{5,511},{6,496},{7,497},{8... | collective-permute-start | bytes 1769480 | tf_op jit(solution)/shard_map/ppermute | solution.py:154
  25.5 33.1 %collective-permute-start.3 = (bf16[256,1152]{1,0:T(8,128)(2,1)S(1)}, bf16[256,1152]{1,0:T(8,128)(2,1)S(1)}, u32[]{:S(2)}, u32[]{:S(2)}) collective-permute-start(bf16[256,1152]{1,0:T(8,128)(2,1)S(1)} %copy-done.3), channel_id=1, source_target_pairs={{0,2},{1,3},{2,4},{3,5},{4,6},{5,7},{6,8},{7,9},{8,10},{9,11},{10,... | collective-permute-start | bytes 1769480 | tf_op jit(solution)/shard_map/ppermute | solution.py:154
  27.5 36.6 %collective-permute-start = (bf16[256,1152]{1,0:T(8,128)(2,1)S(1)}, bf16[256,1152]{1,0:T(8,128)(2,1)S(1)}, u32[]{:S(2)}, u32[]{:S(2)}) collective-permute-start(bf16[256,1152]{1,0:T(8,128)(2,1)S(1)} %copy-done.3), channel_id=1, source_target_pairs={{0,22},{1,23},{2,24},{3,25},{4,26},{5,27},{6,28},{7,29},{8,30},{9,... | collective-permute-start | bytes 1769480 | tf_op jit(solution)/shard_map/ppermute | solution.py:154
  29.4 50.7 %collective-permute-start.9 = (bf16[256,1152]{1,0:T(8,128)(2,1)}, bf16[256,1152]{1,0:T(8,128)(2,1)}, u32[]{:S(2)}, u32[]{:S(2)}) collective-permute-start(bf16[256,1152]{1,0:T(8,128)(2,1)} %collective-permute-done.8.visitor), channel_id=1, source_target_pairs={{0,15},{1,496},{2,1},{3,498},{4,3},{5,500},{6,5},{7,502},{8,7},{9,... | collective-permute-start | bytes 1769480 | tf_op jit(solution)/shard_map/ppermute | solution.py:154
  49.7 38.7 %collective-permute-start.7 = (bf16[256,1152]{1,0:T(8,128)(2,1)}, bf16[256,1152]{1,0:T(8,128)(2,1)}, u32[]{:S(2)}, u32[]{:S(2)}) collective-permute-start(bf16[256,1152]{1,0:T(8,128)(2,1)} %collective-permute-done.6.visitor), channel_id=1, source_target_pairs={{0,2},{1,3},{2,4},{3,5},{4,6},{5,7},{6,8},{7,9},{8,10},{9,11},{10,... | collective-permute-start | bytes 1769480 | tf_op jit(solution)/shard_map/ppermute | solution.py:154
  58.7 51.5 %collective-permute-start.4 = (bf16[256,1152]{1,0:T(8,128)(2,1)S(1)}, bf16[256,1152]{1,0:T(8,128)(2,1)}, u32[]{:S(2)}, u32[]{:S(2)}) collective-permute-start(bf16[256,1152]{1,0:T(8,128)(2,1)S(1)} %collective-permute-done.3.visitor), channel_id=1, source_target_pairs={{0,17},{1,2},{2,19},{3,4},{4,21},{5,6},{6,23},{7,8},{8,25},{9,10},... | collective-permute-start | bytes 1769480 | tf_op jit(solution)/shard_map/ppermute | solution.py:154
  64.1 48.2 %collective-permute-start.1 = (bf16[256,1152]{1,0:T(8,128)(2,1)S(1)}, bf16[256,1152]{1,0:T(8,128)(2,1)}, u32[]{:S(2)}, u32[]{:S(2)}) collective-permute-start(bf16[256,1152]{1,0:T(8,128)(2,1)S(1)} %collective-permute-done.visitor), channel_id=1, source_target_pairs={{0,14},{1,15},{2,0},{3,1},{4,2},{5,3},{6,4},{7,5},{8,6},{9,7},{10,... | collective-permute-start | bytes 1769480 | tf_op jit(solution)/shard_map/ppermute | solution.py:154
  68.2 1.0 copy-start
  69.3 0.9 copy-start.7
  73.5 1.3 %copy-start.1 = (bf16[512,1152]{1,0:T(8,128)(2,1)S(1)}, bf16[512,1152]{1,0:T(8,128)(2,1)}, u32[]{:S(2)}) copy-start(bf16[512,1152]{1,0:T(8,128)(2,1)} %copy-done) | copy-start | bytes 3538948
  80.1 8.3 %copy-start.2 = (bf16[512,1152]{1,0:T(8,128)(2,1)S(1)}, bf16[512,1152]{1,0:T(8,128)(2,1)}, u32[]{:S(2)}) copy-start(bf16[512,1152]{1,0:T(8,128)(2,1)} %copy-done) | copy-start | bytes 3538948
  90.5 28.8 %collective-permute-start.10 = (f32[256,1152]{1,0:T(8,128)S(1)}, f32[256,1152]{1,0:T(8,128)S(1)}, u32[]{:S(2)}, u32[]{:S(2)}) collective-permute-start(f32[256,1152]{1,0:T(8,128)S(1)} %get-tuple-element.47), channel_id=1, source_target_pairs={{0,1},{1,0},{2,3},{3,2},{4,5},{5,4},{6,7},{7,6},{8,9},{9,8},{10,11... | collective-permute-start | bytes 3538952 | tf_op jit(solution)/shard_map/ppermute | solution.py:154
  114.4 6.4 %collective-permute-start.5 = (f32[256,1152]{1,0:T(8,128)S(1)}, f32[256,1152]{1,0:T(8,128)S(1)}, u32[]{:S(2)}, u32[]{:S(2)}) collective-permute-start(f32[256,1152]{1,0:T(8,128)S(1)} %get-tuple-element.37), channel_id=1, source_target_pairs={{0,1},{1,0},{2,3},{3,2},{4,5},{5,4},{6,7},{7,6},{8,9},{9,8},{10,11... | collective-permute-start | bytes 3538952 | tf_op jit(solution)/shard_map/ppermute | solution.py:154
  117.8 1.5 %copy-start.4 = (bf16[256,1152]{1,0:T(8,128)(2,1)S(1)}, bf16[256,1152]{1,0:T(8,128)(2,1)}, u32[]{:S(2)}) copy-start(bf16[256,1152]{1,0:T(8,128)(2,1)} %rows.3) | copy-start | bytes 1769476
  119.3 1.5 %copy-start.6 = (bf16[256,1152]{1,0:T(8,128)(2,1)S(1)}, bf16[256,1152]{1,0:T(8,128)(2,1)}, u32[]{:S(2)}) copy-start(bf16[256,1152]{1,0:T(8,128)(2,1)} %rows.2) | copy-start | bytes 1769476

commit v3 on v1

v3 whole, which is shorter than its diff:
```python
import functools

import jax
import jax.numpy as jnp
from jax import lax
from jax.experimental import pallas as pl
from jax.experimental.pallas import tpu as pltpu
from jax.sharding import PartitionSpec as P

EPS = 1e-06
AXES = ("wide", "narrow")
NT = (((1,), (1,)), ((), ()))
NN = (((1,), (0,)), ((), ()))
VMEM_LIMIT = 48 * 1024 * 1024
F32 = jnp.float32
BF16 = jnp.bfloat16


def mm(a, b, dims):
    return lax.dot_general(a, b, dims, preferred_element_type=F32)


def unit_of(rows):
    floats = rows.astype(F32)
    inverse = lax.rsqrt(jnp.sum(floats * floats, axis=-1, keepdims=True) + EPS)
    return floats * inverse, inverse


def half_of(rows):
    return unit_of(rows)[0].astype(BF16)


def call(kernel, outs, inputs, scratch=(), aliases=None):
    specs = [
        pl.BlockSpec(memory_space=pltpu.SMEM if x.ndim == 1 else pltpu.VMEM) for x in inputs
    ]
    return pl.pallas_call(
        kernel,
        out_shape=outs,
        in_specs=specs,
        out_specs=[pl.BlockSpec(memory_space=pltpu.VMEM) for _ in outs],
        scratch_shapes=list(scratch),
        input_output_aliases=aliases or {},
        compiler_params=pltpu.CompilerParams(vmem_limit_bytes=VMEM_LIMIT),
        cost_estimate=pl.CostEstimate(flops=1000, bytes_accessed=1000, transcendentals=0),
    )(*inputs)


def weigh(temper, resident, visitors, first, weighted, count, positive=None):
    scale, offset = temper[0], temper[1]
    rows = resident.shape[0]
    for k in range(count):
        block = visitors[pl.ds(pl.multiple_of(first + k * rows, rows), rows), :]
        scores = mm(resident, block, NT)
        residual = jax.nn.sigmoid(scale * scores + offset)
        if k == 0 and positive is not None:
            residual = residual - positive
        weighted[:, k * rows : (k + 1) * rows] = (scale * residual).astype(BF16)


def gather(weighted, visitors, first, count, out, before=None):
    rows, width = out.shape
    step = width // 3
    left = weighted[:, : count * rows]
    for at in range(0, width, step):
        block = visitors[pl.ds(pl.multiple_of(first, rows), count * rows), at : at + step]
        part = mm(left, block, NN)
        if before is not None:
            part = before[:, at : at + step] + part
        out[:, at : at + step] = part


def early_kernel(
    temper, flags, column, row, texts, images, other,
    a_text, a_image, d_text, d_image,
    text_half, image_half, text_other, image_other,
    image_near, image_far, text_near, text_far,
    texts_met, images_met, image_weights, image_far_weights, text_weights, text_far_weights,
):
    rows = texts.shape[0]
    square = (rows, rows)
    text, image = half_of(texts[...]), half_of(images[...])
    text_half[...] = text
    image_half[...] = image
    text_other[...] = half_of(other[:rows])
    image_other[...] = half_of(other[rows:])

    def stream(core, own, one, three, near, far, positive, near_sum, far_sum, visitors, *tables):
        visitors[:rows] = own
        visitors[rows : 2 * rows] = half_of(one[...])
        visitors[2 * rows :] = half_of(three[...])
        weigh(temper, near, visitors, 0, tables[0], 3, positive.astype(F32))
        gather(tables[0], visitors, 0, 3, near_sum)
        first = core * rows
        weigh(temper, far, visitors, first, tables[1], 2)
        gather(tables[1], visitors, first, 2, far_sum)

    target = lax.broadcasted_iota(jnp.int32, square, 1)
    stream(
        flags[0], text, a_text, d_text, image, image_other[...],
        column[...] == target, image_near, image_far,
        texts_met, image_weights, image_far_weights,
    )
    target = lax.broadcasted_iota(jnp.int32, square, 0)
    stream(
        1 - flags[0], image, a_image, d_image, text, text_other[...],
        row[...] == target, text_near, text_far,
        images_met, text_weights, text_far_weights,
    )


def far_kernel(temper, c_block, other, far_in, half, far_out, weighted):
    half[...] = half_of(c_block[...])
    weigh(temper, other[...], half, 0, weighted, 1)
    gather(weighted, half, 0, 1, far_out, far_in)


def near_kernel(
    temper, b_text, c_text, image_half, image_in, b_image, c_image, text_half, text_in,
    image_out, text_out, texts_met, images_met, image_weights, text_weights,
):
    rows = b_text.shape[0]
    for last, half, own, before, out, visitors, weighted in (
        (b_text, c_text, image_half, image_in, image_out, texts_met, image_weights),
        (b_image, c_image, text_half, text_in, text_out, images_met, text_weights),
    ):
        visitors[:rows] = half_of(last[...])
        visitors[rows:] = half[...]
        weigh(temper, own[...], visitors, 0, weighted, 2)
        gather(weighted, visitors, 0, 2, out, before)


def finish_kernel(rows, near, received, grad):
    upstream = near[...] + received[...]
    unit, inverse = unit_of(rows[...])
    along = jnp.sum(unit * upstream, axis=-1, keepdims=True)
    grad[...] = inverse * (upstream - unit * along)


def shards(images, texts, labels, log_scale, bias):
    n_wide, n_narrow = lax.axis_size("wide"), lax.axis_size("narrow")
    wide, narrow = lax.axis_index("wide"), lax.axis_index("narrow")
    rows, width = images.shape
    core = narrow % 2

    def moved(value, place):
        pairs = []
        for w in range(n_wide):
            for n in range(n_narrow):
                a, b = place(w, n)
                pairs.append((w * n_narrow + n, a % n_wide * n_narrow + b % n_narrow))
        return lax.ppermute(value, AXES, pairs)

    def hop(value, sign, w_step, chips):
        return moved(value, lambda w, n: (w + sign * w_step, n + 2 * sign * chips))

    def last_hop(value, sign):
        def place(w, n):
            even = n % 2 == (0 if sign > 0 else 1)
            m = n + 1 - 2 * (n % 2)
            return (w + sign, m) if even else (w, m + 2 * sign)

        return moved(value, place)

    def swapped(value):
        return moved(value, lambda w, n: (w, n + 1 - 2 * (n % 2)))

    temper = jnp.stack([jnp.exp(log_scale[0]), bias[0]])
    flags = core.reshape(1).astype(jnp.int32)
    local = labels - (wide * n_narrow + narrow) * rows
    half = jax.ShapeDtypeStruct((rows, width), BF16)
    full = jax.ShapeDtypeStruct((rows, width), F32)

    def table(kind, blocks):
        shape = (blocks * rows, width) if kind == "v" else (rows, blocks * rows)
        return pltpu.VMEM(shape, BF16)

    a_text, a_image = hop(texts, 1, 0, 1), hop(images, -1, 0, 1)
    d_text, d_image = hop(texts, 1, 1, 3), hop(images, -1, 1, 3)
    other = swapped(jnp.concatenate([texts, images]))
    a_text, a_image, other = lax.optimization_barrier((a_text, a_image, other))
    b_text, b_image = last_hop(a_text, 1), last_hop(a_image, -1)
    d_text, d_image = lax.optimization_barrier((d_text, d_image))
    c_text, c_image = hop(d_text, 1, 0, -1), hop(d_image, -1, 0, -1)

    (text_half, image_half, text_other, image_other, image_near, image_far, text_near, text_far) = (
        call(
            early_kernel,
            [half] * 4 + [full] * 4,
            [
                temper, flags, local.reshape(rows, 1), local.reshape(1, rows),
                texts, images, other, a_text, a_image, d_text, d_image,
            ],
            [table("v", 3)] * 2 + [table("w", 3), table("w", 2)] * 2,
        )
    )

    def far(block, other, far_sum):
        return call(
            far_kernel, [half, full], [temper, block, other, far_sum], [table("w", 1)], {3: 1}
        )

    b_text, b_image, image_far, text_far = lax.optimization_barrier(
        (b_text, b_image, image_far, text_far)
    )
    c_text, image_far = far(c_text, image_other, image_far)
    image_back = swapped(image_far)
    c_image, text_far = far(c_image, text_other, text_far)
    text_back = swapped(text_far)
    image_near, text_near = call(
        near_kernel,
        [full, full],
        [temper, b_text, c_text, image_half, image_near, b_image, c_image, text_half, text_near],
        [table("v", 2)] * 2 + [table("w", 2)] * 2,
        {4: 0, 8: 1},
    )
    (grad_images,) = call(finish_kernel, [full], [images, image_near, image_back])
    (grad_texts,) = call(finish_kernel, [full], [texts, text_near, text_back])
    return (grad_images, grad_texts)


def solution(mesh):
    return jax.shard_map(
        shards,
        mesh=mesh,
        in_specs=(P(AXES, None), P(AXES, None), P(AXES), P(), P()),
        out_specs=(P(AXES, None), P(AXES, None)),
        check_vma=False,
    )
```

time: 120 us -> 110 us (0.917)
  waiting for transfers between devices: 39.2 us -> 23.2 us
  starting transfers between devices: 48.3 us -> 59.2 us
  local copies, waits for them, and re-layouts: 5.55 us -> 1.74 us
  Pallas kernels: 23.9 us -> 21.2 us
  other arithmetic: 0.08 us -> 1.5 us
    ppermute x11, waiting for transfers between devices: 39.2 us -> 23.2 us  [moved(): return lax.ppermute(value, AXES, pairs)]
    ppermute x11, starting transfers between devices: 48.3 us -> 59.2 us  [moved(): return lax.ppermute(value, AXES, pairs)]
    pallas_call x10 -> x6, Pallas kernels: 23.9 us -> 21.2 us  [call(): pl.pallas_call(kernel, out_shape=outs, in_specs=specs, out_specs=[pl.Bloc...]
    unnamed x14 -> x16, local copies, waits for them, and re-layouts: 3.41 us -> 0.94 us
    concatenate x0 -> x1, other arithmetic: none -> 1.43 us  [shards(): other = swapped(jnp.concatenate([texts, images]))]
    slice x1 -> x0, local copies, waits for them, and re-layouts: 1.33 us -> none  [shards(): text_other, image_other = (both[:rows], both[rows:])]
  transfers between devices with their start and end apart: 11 -> 11, of which waited for: 5 -> 1; matrix products, arithmetic and copies ran while one was open for 2% -> 1% of each run, Pallas kernels for 16% -> 18%
where the time goes in v3:
time: 110 us; the launch traced here: 109 us
  starting transfers between devices  59.2 us (54%)
  waiting for transfers between devices  23.2 us (21%)
  Pallas kernels  21.2 us (19%)
  between operations  2.25 us (2%)
  local copies, waits for them, and re-layouts  1.74 us (2%)
  other arithmetic  1.5 us (1%)
    ppermute x11, starting transfers between devices, moved(): return lax.ppermute(value, AXES, pairs)  59.2 us
    ppermute x11, waiting for transfers between devices, moved(): return lax.ppermute(value, AXES, pairs)  23.2 us
    pallas_call x6, Pallas kernels, call(): pl.pallas_call(kernel, out_shape=outs, in_specs=specs, out_specs=[pl.Bloc...  21.2 us
  transfers between devices with their start and end apart: 11, of which 1 were waited for; matrix products, arithmetic and copies ran while one was open for 1% of the time, Pallas kernels for 18%

profile of v3, /device:TPU:7, one launch (start us, length us, event | category | flops | bytes accessed | tf_op | source)
XLA Modules:
  0.0 109.1 jit_solution(508626816839303104)
XLA Ops:
  0.6 0.0 copy-start.1
  0.6 0.0 copy-start
  0.6 0.0 copy-start.7
  0.7 1.4 %pad_maximum_fusion = bf16[512,1152]{1,0:T(8,128)(2,1)S(1)} fusion(bf16[256,1152]{1,0:T(8,128)(2,1)} %rows.2, bf16[256,1152]{1,0:T(8,128)(2,1)} %rows.3), kind=kLoop, calls=%fused_computation | loop fusion | flops 2359296 | bytes 2359296 | tf_op jit(solution)/shard_map/concatenate | solution.py:180
  2.1 2.6 %collective-permute-start.2 = (bf16[512,1152]{1,0:T(8,128)(2,1)S(1)}, bf16[512,1152]{1,0:T(8,128)(2,1)S(1)}, u32[]{:S(2)}, u32[]{:S(2)}) collective-permute-start(bf16[512,1152]{1,0:T(8,128)(2,1)S(1)} %pad_maximum_fusion), channel_id=1, source_target_pairs={{0,1},{1,0},{2,3},{3,2},{4,5},{5,4},{6,7},{7,6},{8,9},{9,8},{10,11... | collective-permute-start | bytes 3538952 | tf_op jit(solution)/shard_map/ppermute | solution.py:152
  4.7 0.0 copy-done
  4.7 3.1 %collective-permute-start = (bf16[256,1152]{1,0:T(8,128)(2,1)S(1)}, bf16[256,1152]{1,0:T(8,128)(2,1)S(1)}, u32[]{:S(2)}, u32[]{:S(2)}) collective-permute-start(bf16[256,1152]{1,0:T(8,128)(2,1)S(1)} %copy-done), channel_id=1, source_target_pairs={{0,2},{1,3},{2,4},{3,5},{4,6},{5,7},{6,8},{7,9},{8,10},{9,11},{10,... | collective-permute-start | bytes 1769480 | tf_op jit(solution)/shard_map/ppermute | solution.py:152
  7.8 0.0 copy-done.1
  7.8 2.2 %collective-permute-start.1 = (bf16[256,1152]{1,0:T(8,128)(2,1)S(1)}, bf16[256,1152]{1,0:T(8,128)(2,1)}, u32[]{:S(2)}, u32[]{:S(2)}) collective-permute-start(bf16[256,1152]{1,0:T(8,128)(2,1)S(1)} %copy-done.1), channel_id=1, source_target_pairs={{0,14},{1,15},{2,0},{3,1},{4,2},{5,3},{6,4},{7,5},{8,6},{9,7},{10,... | collective-permute-start | bytes 1769480 | tf_op jit(solution)/shard_map/ppermute | solution.py:152
  10.0 5.5 %collective-permute-start.5 = (bf16[256,1152]{1,0:T(8,128)(2,1)S(1)}, bf16[256,1152]{1,0:T(8,128)(2,1)S(1)}, u32[]{:S(2)}, u32[]{:S(2)}) collective-permute-start(bf16[256,1152]{1,0:T(8,128)(2,1)S(1)} %copy-done), channel_id=1, source_target_pairs={{0,22},{1,23},{2,24},{3,25},{4,26},{5,27},{6,28},{7,29},{8,30},{9,... | collective-permute-start | bytes 1769480 | tf_op jit(solution)/shard_map/ppermute | solution.py:152
  15.5 12.8 %collective-permute-start.6 = (bf16[256,1152]{1,0:T(8,128)(2,1)S(1)}, bf16[256,1152]{1,0:T(8,128)(2,1)}, u32[]{:S(2)}, u32[]{:S(2)}) collective-permute-start(bf16[256,1152]{1,0:T(8,128)(2,1)S(1)} %copy-done.1), channel_id=1, source_target_pairs={{0,506},{1,507},{2,508},{3,509},{4,510},{5,511},{6,496},{7,497},{8... | collective-permute-start | bytes 1769480 | tf_op jit(solution)/shard_map/ppermute | solution.py:152
  28.3 0.0 collective-permute-done.a_text
  28.3 0.0 collective-permute-done.1.a_image
  28.3 0.0 collective-permute-done.2.other
  28.4 0.0 copy-start.6
  28.4 2.6 %collective-permute-start.3 = (bf16[256,1152]{1,0:T(8,128)(2,1)S(1)}, bf16[256,1152]{1,0:T(8,128)(2,1)S(1)}, u32[]{:S(2)}, u32[]{:S(2)}) collective-permute-start(bf16[256,1152]{1,0:T(8,128)(2,1)S(1)} %collective-permute-done.a_text), channel_id=1, source_target_pairs={{0,17},{1,2},{2,19},{3,4},{4,21},{5,6},{6,23},{7,8},{8,25},{9,10},... | collective-permute-start | bytes 1769480 | tf_op jit(solution)/shard_map/ppermute | solution.py:152
  31.0 19.3 %collective-permute-start.4 = (bf16[256,1152]{1,0:T(8,128)(2,1)}, bf16[256,1152]{1,0:T(8,128)(2,1)S(1)}, u32[]{:S(2)}, u32[]{:S(2)}) collective-permute-start(bf16[256,1152]{1,0:T(8,128)(2,1)} %collective-permute-done.1.a_image), channel_id=1, source_target_pairs={{0,15},{1,496},{2,1},{3,498},{4,3},{5,500},{6,5},{7,502},{8,7},{9,... | collective-permute-start | bytes 1769480 | tf_op jit(solution)/shard_map/ppermute | solution.py:152
  50.3 23.2 %collective-permute-done.5.d_text = bf16[256,1152]{1,0:T(8,128)(2,1)S(1)} collective-permute-done((bf16[256,1152]{1,0:T(8,128)(2,1)S(1)}, bf16[256,1152]{1,0:T(8,128)(2,1)S(1)}, u32[]{:S(2)}, u32[]{:S(2)}) %collective-permute-start.5) | collective-permute-done | bytes 589856 | tf_op jit(solution)/shard_map/ppermute | solution.py:152
  73.5 0.0 collective-permute-done.6.d_image
  73.5 0.0 copy-done.6
  73.5 1.9 %collective-permute-start.8 = (bf16[256,1152]{1,0:T(8,128)(2,1)}, bf16[256,1152]{1,0:T(8,128)(2,1)}, u32[]{:S(2)}, u32[]{:S(2)}) collective-permute-start(bf16[256,1152]{1,0:T(8,128)(2,1)} %collective-permute-done.6.d_image), channel_id=1, source_target_pairs={{0,2},{1,3},{2,4},{3,5},{4,6},{5,7},{6,8},{7,9},{8,10},{9,11},{10,... | collective-permute-start | bytes 1769480 | tf_op jit(solution)/shard_map/ppermute | solution.py:152
  75.5 3.4 %collective-permute-start.7 = (bf16[256,1152]{1,0:T(8,128)(2,1)S(1)}, bf16[256,1152]{1,0:T(8,128)(2,1)}, u32[]{:S(2)}, u32[]{:S(2)}) collective-permute-start(bf16[256,1152]{1,0:T(8,128)(2,1)S(1)} %collective-permute-done.5.d_text), channel_id=1, source_target_pairs={{0,14},{1,15},{2,0},{3,1},{4,2},{5,3},{6,4},{7,5},{8,6},{9,7},{10,... | collective-permute-start | bytes 1769480 | tf_op jit(solution)/shard_map/ppermute | solution.py:152
  78.8 0.0 copy-done.7
  78.9 0.8 copy.11.column
  81.0 0.1 pad_maximum_fusion.1.temper
  81.1 0.0 copy-start.5
  81.1 0.9 copy-done.5
  82.0 8.8 %shard_map.68 = (bf16[256,1152]{1,0:T(8,128)(2,1)S(1)}, bf16[256,1152]{1,0:T(8,128)(2,1)S(1)}, bf16[256,1152]{1,0:T(8,128)(2,1)S(1)}, bf16[256,1152]{1,0:T(8,128...) custom-call(f32[2]{0:T(128)S(1)} %pad_maximum_fusion.1.temper, ...), custom_call_target="tpu_custom_call" | custom-call | flops 1000 | bytes 1000 | tf_op jit(solution)/shard_map/pallas_call | solution.py:37
  90.8 0.0 collective-permute-done.3.b_text
  90.8 0.0 collective-permute-done.4.b_image
  90.8 0.0 collective-permute-done.8.c_block
  90.8 0.0 copy-start.4
  90.8 3.7 %shard_map.70 = (bf16[256,1152]{1,0:T(8,128)(2,1)S(1)}, f32[256,1152]{1,0:T(8,128)}) custom-call(f32[2]{0:T(128)S(1)} %pad_maximum_fusion.1.temper, bf16[256,1152]{1,0:T(8,128)(2,1)} %collective-permute-done.8.c_block, bf16[256,1152]{1,0:T(8,128)(2,1)S(1)} %get-tuple-element.39.other, ...), custom_call_target="tpu_custom_call", output_to_operand_aliasing={{1}: (3, {})} | custom-call | flops 1000 | bytes 1000 | tf_op jit(solution)/shard_map/pallas_call | solution.py:37
  94.5 3.9 %collective-permute-start.10 = (f32[256,1152]{1,0:T(8,128)}, f32[256,1152]{1,0:T(8,128)S(1)}, u32[]{:S(2)}, u32[]{:S(2)}) collective-permute-start(f32[256,1152]{1,0:T(8,128)} %get-tuple-element.47), channel_id=1, source_target_pairs={{0,1},{1,0},{2,3},{3,2},{4,5},{5,4},{6,7},{7,6},{8,9},{9,8},{10,11... | collective-permute-start | bytes 3538952 | tf_op jit(solution)/shard_map/ppermute | solution.py:152
  98.4 0.0 collective-permute-done.7.c_block
  98.4 0.0 copy-done.4
  98.4 0.0 copy-start.2
  98.4 0.0 copy-start.3
  98.4 2.4 %shard_map.69 = (bf16[256,1152]{1,0:T(8,128)(2,1)S(1)}, f32[256,1152]{1,0:T(8,128)S(1)}) custom-call(f32[2]{0:T(128)S(1)} %pad_maximum_fusion.1.temper, bf16[256,1152]{1,0:T(8,128)(2,1)} %collective-permute-done.7.c_block, bf16[256,1152]{1,0:T(8,128)(2,1)S(1)} %get-tuple-element.33.other, f32[256,1152]{1,0:T(8,128)S(1)} %copy-done.4), custom_call_target="tpu_custom_call", output_to_operand_aliasing={{1}: (3, {})} | custom-call | flops 1000 | bytes 1000 | tf_op jit(solution)/shard_map/pallas_call | solution.py:37
  100.8 1.9 %collective-permute-start.9 = (f32[256,1152]{1,0:T(8,128)S(1)}, f32[256,1152]{1,0:T(8,128)S(1)}, u32[]{:S(2)}, u32[]{:S(2)}) collective-permute-start(f32[256,1152]{1,0:T(8,128)S(1)} %get-tuple-element.45), channel_id=1, source_target_pairs={{0,1},{1,0},{2,3},{3,2},{4,5},{5,4},{6,7},{7,6},{8,9},{9,8},{10,11... | collective-permute-start | bytes 3538952 | tf_op jit(solution)/shard_map/ppermute | solution.py:152
  102.8 0.0 copy-done.2
  102.8 0.0 copy-done.3
  102.8 3.3 %shard_map.71 = (f32[256,1152]{1,0:T(8,128)S(1)}, f32[256,1152]{1,0:T(8,128)S(1)}) custom-call(f32[2]{0:T(128)S(1)} %pad_maximum_fusion.1.temper, bf16[256,1152]{1,0:T(8,128)(2,1)S(1)} %collective-permute-done.3.b_text, bf16[256,1152]{1,0:T(8,128)(2,1)S(1)} %get-tuple-element.35.c_text, ...), custom_call_target="tpu_custom_call", output_to_operand_aliasing={{0}: (4, {}), {1}: (8, {})} | custom-call | flops 1000 | bytes 1000 | tf_op jit(solution)/shard_map/pallas_call | solution.py:37
  106.1 0.0 collective-permute-done.10.received
  106.1 1.5 %shard_map.73 = f32[256,1152]{1,0:T(8,128)} custom-call(bf16[256,1152]{1,0:T(8,128)(2,1)S(1)} %copy-done, f32[256,1152]{1,0:T(8,128)S(1)} %get-tuple-element.46.near, f32[256,1152]{1,0:T(8,128)S(1)} %collective-permute-done.10.received), custom_call_target="tpu_custom_call" | custom-call | flops 1000 | bytes 1000 | tf_op jit(solution)/shard_map/pallas_call | solution.py:37
  107.6 0.0 collective-permute-done.9.received
  107.6 1.5 %shard_map.72 = f32[256,1152]{1,0:T(8,128)} custom-call(bf16[256,1152]{1,0:T(8,128)(2,1)S(1)} %copy-done.1, f32[256,1152]{1,0:T(8,128)S(1)} %get-tuple-element.44.near, f32[256,1152]{1,0:T(8,128)S(1)} %collective-permute-done.9.received), custom_call_target="tpu_custom_call" | custom-call | flops 1000 | bytes 1000 | tf_op jit(solution)/shard_map/pallas_call | solution.py:37
  (1 shorter events, 0.0 us)
Async XLA Ops:
  0.6 7.2 %copy-start.1 = (bf16[256,1152]{1,0:T(8,128)(2,1)S(1)}, bf16[256,1152]{1,0:T(8,128)(2,1)}, u32[]{:S(2)}) copy-start(bf16[256,1152]{1,0:T(8,128)(2,1)} %rows.2) | copy-start | bytes 1769476
  0.6 4.0 %copy-start = (bf16[256,1152]{1,0:T(8,128)(2,1)S(1)}, bf16[256,1152]{1,0:T(8,128)(2,1)}, u32[]{:S(2)}) copy-start(bf16[256,1152]{1,0:T(8,128)(2,1)} %rows.3) | copy-start | bytes 1769476
  0.6 78.2 %copy-start.7 = (s32[256]{0:T(256)S(1)}, s32[256]{0:T(256)}, u32[]{:S(2)}) copy-start(s32[256]{0:T(256)} %param.7) | copy-start | bytes 3076
  2.1 26.3 %collective-permute-start.2 = (bf16[512,1152]{1,0:T(8,128)(2,1)S(1)}, bf16[512,1152]{1,0:T(8,128)(2,1)S(1)}, u32[]{:S(2)}, u32[]{:S(2)}) collective-permute-start(bf16[512,1152]{1,0:T(8,128)(2,1)S(1)} %pad_maximum_fusion), channel_id=1, source_target_pairs={{0,1},{1,0},{2,3},{3,2},{4,5},{5,4},{6,7},{7,6},{8,9},{9,8},{10,11... | collective-permute-start | bytes 3538952 | tf_op jit(solution)/shard_map/ppermute | solution.py:152
  4.7 23.6 %collective-permute-start = (bf16[256,1152]{1,0:T(8,128)(2,1)S(1)}, bf16[256,1152]{1,0:T(8,128)(2,1)S(1)}, u32[]{:S(2)}, u32[]{:S(2)}) collective-permute-start(bf16[256,1152]{1,0:T(8,128)(2,1)S(1)} %copy-done), channel_id=1, source_target_pairs={{0,2},{1,3},{2,4},{3,5},{4,6},{5,7},{6,8},{7,9},{8,10},{9,11},{10,... | collective-permute-start | bytes 1769480 | tf_op jit(solution)/shard_map/ppermute | solution.py:152
  7.8 20.5 %collective-permute-start.1 = (bf16[256,1152]{1,0:T(8,128)(2,1)S(1)}, bf16[256,1152]{1,0:T(8,128)(2,1)}, u32[]{:S(2)}, u32[]{:S(2)}) collective-permute-start(bf16[256,1152]{1,0:T(8,128)(2,1)S(1)} %copy-done.1), channel_id=1, source_target_pairs={{0,14},{1,15},{2,0},{3,1},{4,2},{5,3},{6,4},{7,5},{8,6},{9,7},{10,... | collective-permute-start | bytes 1769480 | tf_op jit(solution)/shard_map/ppermute | solution.py:152
  10.0 63.5 %collective-permute-start.5 = (bf16[256,1152]{1,0:T(8,128)(2,1)S(1)}, bf16[256,1152]{1,0:T(8,128)(2,1)S(1)}, u32[]{:S(2)}, u32[]{:S(2)}) collective-permute-start(bf16[256,1152]{1,0:T(8,128)(2,1)S(1)} %copy-done), channel_id=1, source_target_pairs={{0,22},{1,23},{2,24},{3,25},{4,26},{5,27},{6,28},{7,29},{8,30},{9,... | collective-permute-start | bytes 1769480 | tf_op jit(solution)/shard_map/ppermute | solution.py:152
  15.5 58.0 %collective-permute-start.6 = (bf16[256,1152]{1,0:T(8,128)(2,1)S(1)}, bf16[256,1152]{1,0:T(8,128)(2,1)}, u32[]{:S(2)}, u32[]{:S(2)}) collective-permute-start(bf16[256,1152]{1,0:T(8,128)(2,1)S(1)} %copy-done.1), channel_id=1, source_target_pairs={{0,506},{1,507},{2,508},{3,509},{4,510},{5,511},{6,496},{7,497},{8... | collective-permute-start | bytes 1769480 | tf_op jit(solution)/shard_map/ppermute | solution.py:152
  28.4 45.2 %copy-start.6 = (bf16[512,1152]{1,0:T(8,128)(2,1)}, bf16[512,1152]{1,0:T(8,128)(2,1)S(1)}, u32[]{:S(2)}) copy-start(bf16[512,1152]{1,0:T(8,128)(2,1)S(1)} %collective-permute-done.2.other) | copy-start | bytes 3538948
  28.4 62.4 %collective-permute-start.3 = (bf16[256,1152]{1,0:T(8,128)(2,1)S(1)}, bf16[256,1152]{1,0:T(8,128)(2,1)S(1)}, u32[]{:S(2)}, u32[]{:S(2)}) collective-permute-start(bf16[256,1152]{1,0:T(8,128)(2,1)S(1)} %collective-permute-done.a_text), channel_id=1, source_target_pairs={{0,17},{1,2},{2,19},{3,4},{4,21},{5,6},{6,23},{7,8},{8,25},{9,10},... | collective-permute-start | bytes 1769480 | tf_op jit(solution)/shard_map/ppermute | solution.py:152
  31.0 59.8 %collective-permute-start.4 = (bf16[256,1152]{1,0:T(8,128)(2,1)}, bf16[256,1152]{1,0:T(8,128)(2,1)S(1)}, u32[]{:S(2)}, u32[]{:S(2)}) collective-permute-start(bf16[256,1152]{1,0:T(8,128)(2,1)} %collective-permute-done.1.a_image), channel_id=1, source_target_pairs={{0,15},{1,496},{2,1},{3,498},{4,3},{5,500},{6,5},{7,502},{8,7},{9,... | collective-permute-start | bytes 1769480 | tf_op jit(solution)/shard_map/ppermute | solution.py:152
  73.5 17.2 %collective-permute-start.8 = (bf16[256,1152]{1,0:T(8,128)(2,1)}, bf16[256,1152]{1,0:T(8,128)(2,1)}, u32[]{:S(2)}, u32[]{:S(2)}) collective-permute-start(bf16[256,1152]{1,0:T(8,128)(2,1)} %collective-permute-done.6.d_image), channel_id=1, source_target_pairs={{0,2},{1,3},{2,4},{3,5},{4,6},{5,7},{6,8},{7,9},{8,10},{9,11},{10,... | collective-permute-start | bytes 1769480 | tf_op jit(solution)/shard_map/ppermute | solution.py:152
  75.5 23.0 %collective-permute-start.7 = (bf16[256,1152]{1,0:T(8,128)(2,1)S(1)}, bf16[256,1152]{1,0:T(8,128)(2,1)}, u32[]{:S(2)}, u32[]{:S(2)}) collective-permute-start(bf16[256,1152]{1,0:T(8,128)(2,1)S(1)} %collective-permute-done.5.d_text), channel_id=1, source_target_pairs={{0,14},{1,15},{2,0},{3,1},{4,2},{5,3},{6,4},{7,5},{8,6},{9,7},{10,... | collective-permute-start | bytes 1769480 | tf_op jit(solution)/shard_map/ppermute | solution.py:152
  81.1 0.9 copy-start.5
  90.8 7.6 %copy-start.4 = (f32[256,1152]{1,0:T(8,128)S(1)}, f32[256,1152]{1,0:T(8,128)}, u32[]{:S(2)}) copy-start(f32[256,1152]{1,0:T(8,128)} %get-tuple-element.34.far_in) | copy-start | bytes 3538948
  94.5 11.6 %collective-permute-start.10 = (f32[256,1152]{1,0:T(8,128)}, f32[256,1152]{1,0:T(8,128)S(1)}, u32[]{:S(2)}, u32[]{:S(2)}) collective-permute-start(f32[256,1152]{1,0:T(8,128)} %get-tuple-element.47), channel_id=1, source_target_pairs={{0,1},{1,0},{2,3},{3,2},{4,5},{5,4},{6,7},{7,6},{8,9},{9,8},{10,11... | collective-permute-start | bytes 3538952 | tf_op jit(solution)/shard_map/ppermute | solution.py:152
  98.4 4.3 %copy-start.2 = (f32[256,1152]{1,0:T(8,128)S(1)}, f32[256,1152]{1,0:T(8,128)}, u32[]{:S(2)}) copy-start(f32[256,1152]{1,0:T(8,128)} %get-tuple-element.37.image_in) | copy-start | bytes 3538948
  98.4 4.3 %copy-start.3 = (f32[256,1152]{1,0:T(8,128)S(1)}, f32[256,1152]{1,0:T(8,128)}, u32[]{:S(2)}) copy-start(f32[256,1152]{1,0:T(8,128)} %get-tuple-element.43.text_in) | copy-start | bytes 3538948
  100.8 6.8 %collective-permute-start.9 = (f32[256,1152]{1,0:T(8,128)S(1)}, f32[256,1152]{1,0:T(8,128)S(1)}, u32[]{:S(2)}, u32[]{:S(2)}) collective-permute-start(f32[256,1152]{1,0:T(8,128)S(1)} %get-tuple-element.45), channel_id=1, source_target_pairs={{0,1},{1,0},{2,3},{3,2},{4,5},{5,4},{6,7},{7,6},{8,9},{9,8},{10,11... | collective-permute-start | bytes 3538952 | tf_op jit(solution)/shard_map/ppermute | solution.py:152

commit v4 on v3

v4 whole, which is shorter than its diff:
```python
import functools

import jax
import jax.numpy as jnp
from jax import lax
from jax.experimental import pallas as pl
from jax.experimental.pallas import tpu as pltpu
from jax.sharding import PartitionSpec as P

EPS = 1e-06
AXES = ("wide", "narrow")
NT = (((1,), (1,)), ((), ()))
NN = (((1,), (0,)), ((), ()))
VMEM_LIMIT = 20 * 1024 * 1024
F32 = jnp.float32
BF16 = jnp.bfloat16


def mm(a, b, dims):
    return lax.dot_general(a, b, dims, preferred_element_type=F32)


def unit_of(rows):
    floats = rows.astype(F32)
    inverse = lax.rsqrt(jnp.sum(floats * floats, axis=-1, keepdims=True) + EPS)
    return floats * inverse, inverse


def half_of(rows):
    return unit_of(rows)[0].astype(BF16)


def call(kernel, outs, inputs, aliases=None):
    specs = [
        pl.BlockSpec(memory_space=pltpu.SMEM if x.ndim == 1 else pltpu.VMEM) for x in inputs
    ]
    return pl.pallas_call(
        kernel,
        out_shape=outs,
        in_specs=specs,
        out_specs=[pl.BlockSpec(memory_space=pltpu.VMEM) for _ in outs],
        input_output_aliases=aliases or {},
        compiler_params=pltpu.CompilerParams(vmem_limit_bytes=VMEM_LIMIT),
        cost_estimate=pl.CostEstimate(flops=1000, bytes_accessed=1000, transcendentals=0),
    )(*inputs)


def weigh(temper, resident, block, positive=None):
    scale, offset = temper[0], temper[1]
    residual = jax.nn.sigmoid(scale * mm(resident, block, NT) + offset)
    if positive is not None:
        residual = residual - positive.astype(F32)
    return (scale * residual).astype(BF16)


def own_kernel(
    temper, flags, column, row, texts, images, other,
    text_half, image_half, text_other, image_other,
    image_near, image_far, text_near, text_far,
):
    rows = texts.shape[0]
    text, image = half_of(texts[...]), half_of(images[...])
    text_half[...] = text
    image_half[...] = image
    text_other[...] = half_of(other[:rows])
    image_other[...] = half_of(other[rows:])
    target = lax.broadcasted_iota(jnp.int32, (rows, rows), 1)
    image_near[...] = mm(weigh(temper, image, text, column[...] == target), text, NN)
    target = lax.broadcasted_iota(jnp.int32, (rows, rows), 0)
    text_near[...] = mm(weigh(temper, text, image, row[...] == target), image, NN)

    @pl.when(flags[0] == 0)
    def _():
        image_far[...] = mm(weigh(temper, image_other[...], text), text, NN)
        text_far[...] = jnp.zeros(text_far.shape, F32)

    @pl.when(flags[0] == 1)
    def _():
        text_far[...] = mm(weigh(temper, text_other[...], image), image, NN)
        image_far[...] = jnp.zeros(image_far.shape, F32)


def both_kernel(
    temper, text, image, image_half, image_other, text_half, text_other,
    image_near_in, image_far_in, text_near_in, text_far_in,
    image_near, image_far, text_near, text_far,
):
    for visitor, own, other, near_in, far_in, near, far in (
        (text, image_half, image_other, image_near_in, image_far_in, image_near, image_far),
        (image, text_half, text_other, text_near_in, text_far_in, text_near, text_far),
    ):
        block = half_of(visitor[...])
        near[...] = near_in[...] + mm(weigh(temper, own[...], block), block, NN)
        far[...] = far_in[...] + mm(weigh(temper, other[...], block), block, NN)


def side_kernel(
    temper, flags, d_text, d_image, b_text, b_image,
    image_half, image_other, text_half, text_other,
    image_near_in, image_far_in, text_near_in, text_far_in,
    image_near, image_far, text_near, text_far,
):
    for core, three, last, own, other, near_in, far_in, near, far in (
        (1, d_text, b_text, image_half, image_other,
         image_near_in, image_far_in, image_near, image_far),
        (0, d_image, b_image, text_half, text_other,
         text_near_in, text_far_in, text_near, text_far),
    ):
        block, final = half_of(three[...]), half_of(last[...])
        part = mm(weigh(temper, own[...], block), block, NN)
        near[...] = near_in[...] + part + mm(weigh(temper, own[...], final), final, NN)

        @pl.when(flags[0] == core)
        def _():
            far[...] = far_in[...] + mm(weigh(temper, other[...], block), block, NN)

        @pl.when(flags[0] != core)
        def _():
            far[...] = far_in[...]


def far_kernel(temper, c_block, other, far_in, half, far):
    block = half_of(c_block[...])
    half[...] = block
    far[...] = far_in[...] + mm(weigh(temper, other[...], block), block, NN)


def near_kernel(
    temper, c_text, image_half, image_in, c_image, text_half, text_in, image_out, text_out
):
    for visitor, own, before, out in (
        (c_text, image_half, image_in, image_out),
        (c_image, text_half, text_in, text_out),
    ):
        block = visitor[...]
        out[...] = before[...] + mm(weigh(temper, own[...], block), block, NN)


def finish_kernel(rows, near, received, grad):
    upstream = near[...] + received[...]
    unit, inverse = unit_of(rows[...])
    along = jnp.sum(unit * upstream, axis=-1, keepdims=True)
    grad[...] = inverse * (upstream - unit * along)


def shards(images, texts, labels, log_scale, bias):
    n_wide, n_narrow = lax.axis_size("wide"), lax.axis_size("narrow")
    wide, narrow = lax.axis_index("wide"), lax.axis_index("narrow")
    rows, width = images.shape
    core = narrow % 2

    def moved(value, place):
        pairs = []
        for w in range(n_wide):
            for n in range(n_narrow):
                a, b = place(w, n)
                pairs.append((w * n_narrow + n, a % n_wide * n_narrow + b % n_narrow))
        return lax.ppermute(value, AXES, pairs)

    def hop(value, sign, w_step, chips):
        return moved(value, lambda w, n: (w + sign * w_step, n + 2 * sign * chips))

    def last_hop(value, sign):
        def place(w, n):
            even = n % 2 == (0 if sign > 0 else 1)
            m = n + 1 - 2 * (n % 2)
            return (w + sign, m) if even else (w, m + 2 * sign)

        return moved(value, place)

    def swapped(value):
        return moved(value, lambda w, n: (w, n + 1 - 2 * (n % 2)))

    temper = jnp.stack([jnp.exp(log_scale[0]), bias[0]])
    flags = core.reshape(1).astype(jnp.int32)
    local = labels - (wide * n_narrow + narrow) * rows
    half = jax.ShapeDtypeStruct((rows, width), BF16)
    full = jax.ShapeDtypeStruct((rows, width), F32)

    a_text, a_image = hop(texts, 1, 0, 1), hop(images, -1, 0, 1)
    d_text, d_image = hop(texts, 1, 1, 3), hop(images, -1, 1, 3)
    other = swapped(jnp.concatenate([texts, images]))

    (text_half, image_half, text_other, image_other, *sums) = call(
        own_kernel,
        [half] * 4 + [full] * 4,
        [temper, flags, local.reshape(rows, 1), local.reshape(1, rows), texts, images, other],
    )
    residents = [image_half, image_other, text_half, text_other]
    a_text, a_image, *sums = lax.optimization_barrier((a_text, a_image, *sums))
    b_text, b_image = last_hop(a_text, 1), last_hop(a_image, -1)
    sums = call(
        both_kernel,
        [full] * 4,
        [temper, a_text, a_image, *residents, *sums],
        {7: 0, 8: 1, 9: 2, 10: 3},
    )
    d_text, d_image, *sums = lax.optimization_barrier((d_text, d_image, *sums))
    c_text, c_image = hop(d_text, 1, 0, -1), hop(d_image, -1, 0, -1)
    image_near, image_far, text_near, text_far = call(
        side_kernel,
        [full] * 4,
        [temper, flags, d_text, d_image, b_text, b_image, *residents, *sums],
        {10: 0, 11: 1, 12: 2, 13: 3},
    )

    def far(block, other, far_sum):
        return call(far_kernel, [half, full], [temper, block, other, far_sum], {3: 1})

    c_text, image_far = far(c_text, image_other, image_far)
    image_back = swapped(image_far)
    c_image, text_far = far(c_image, text_other, text_far)
    text_back = swapped(text_far)
    image_near, text_near = call(
        near_kernel,
        [full, full],
        [temper, c_text, image_half, image_near, c_image, text_half, text_near],
        {3: 0, 6: 1},
    )
    (grad_images,) = call(finish_kernel, [full], [images, image_near, image_back])
    (grad_texts,) = call(finish_kernel, [full], [texts, text_near, text_back])
    return (grad_images, grad_texts)


def solution(mesh):
    return jax.shard_map(
        shards,
        mesh=mesh,
        in_specs=(P(AXES, None), P(AXES, None), P(AXES), P(), P()),
        out_specs=(P(AXES, None), P(AXES, None)),
        check_vma=False,
    )
```

time: 110 us -> 111 us (level)
  the two profiles are of different devices: /device:TPU:7 before, /device:TPU:1 now
where the time goes in v4:
time: 111 us
  starting transfers between devices  60.9 us (55%)
  waiting for transfers between devices  21.6 us (19%)
  Pallas kernels  21.6 us (19%)
  other arithmetic  2.52 us (2%)
  between operations  2.2 us (2%)
  local copies, waits for them, and re-layouts  1.72 us (2%)
    ppermute x11, starting transfers between devices, moved(): return lax.ppermute(value, AXES, pairs)  60.9 us
    pallas_call x8, Pallas kernels, call(): pl.pallas_call(kernel, out_shape=outs, in_specs=specs, out_specs=[pl.Bloc...  21.6 us
    ppermute x11, waiting for transfers between devices, moved(): return lax.ppermute(value, AXES, pairs)  21.6 us
    concatenate x1, other arithmetic, shards(): other = swapped(jnp.concatenate([texts, images]))  2.44 us
  transfers between devices with their start and end apart: 11, of which 4 were waited for; matrix products, arithmetic and copies ran while one was open for 1% of the time, Pallas kernels for 18%

profile of v4, /device:TPU:1, one launch (start us, length us, event | category | flops | bytes accessed | tf_op | source)
XLA Modules:
  0.0 110.5 jit_solution(5766654351732979340)
XLA Ops:
  0.6 0.0 copy-start.1
  0.6 0.0 copy-start
  0.6 0.0 copy-start.3
  0.7 2.4 %pad_maximum_fusion = bf16[512,1152]{1,0:T(8,128)(2,1)} fusion(bf16[256,1152]{1,0:T(8,128)(2,1)} %rows.2, bf16[256,1152]{1,0:T(8,128)(2,1)} %rows.3), kind=kLoop, calls=%fused_computation | loop fusion | flops 2359296 | bytes 2359296 | tf_op jit(solution)/shard_map/concatenate | solution.py:182
  3.1 8.8 %collective-permute-start.4 = (bf16[512,1152]{1,0:T(8,128)(2,1)}, bf16[512,1152]{1,0:T(8,128)(2,1)S(1)}, u32[]{:S(2)}, u32[]{:S(2)}) collective-permute-start(bf16[512,1152]{1,0:T(8,128)(2,1)} %pad_maximum_fusion), channel_id=1, source_target_pairs={{0,1},{1,0},{2,3},{3,2},{4,5},{5,4},{6,7},{7,6},{8,9},{9,8},{10,11... | collective-permute-start | bytes 3538952 | tf_op jit(solution)/shard_map/ppermute | solution.py:158
  11.9 0.0 copy-done
  11.9 1.9 %collective-permute-start.2 = (bf16[256,1152]{1,0:T(8,128)(2,1)S(1)}, bf16[256,1152]{1,0:T(8,128)(2,1)}, u32[]{:S(2)}, u32[]{:S(2)}) collective-permute-start(bf16[256,1152]{1,0:T(8,128)(2,1)S(1)} %copy-done), channel_id=1, source_target_pairs={{0,2},{1,3},{2,4},{3,5},{4,6},{5,7},{6,8},{7,9},{8,10},{9,11},{10,... | collective-permute-start | bytes 1769480 | tf_op jit(solution)/shard_map/ppermute | solution.py:158
  13.8 0.0 copy-done.1
  13.8 5.5 %collective-permute-start.3 = (bf16[256,1152]{1,0:T(8,128)(2,1)S(1)}, bf16[256,1152]{1,0:T(8,128)(2,1)}, u32[]{:S(2)}, u32[]{:S(2)}) collective-permute-start(bf16[256,1152]{1,0:T(8,128)(2,1)S(1)} %copy-done.1), channel_id=1, source_target_pairs={{0,14},{1,15},{2,0},{3,1},{4,2},{5,3},{6,4},{7,5},{8,6},{9,7},{10,... | collective-permute-start | bytes 1769480 | tf_op jit(solution)/shard_map/ppermute | solution.py:158
  19.3 1.9 %collective-permute-start = (bf16[256,1152]{1,0:T(8,128)(2,1)S(1)}, bf16[256,1152]{1,0:T(8,128)(2,1)S(1)}, u32[]{:S(2)}, u32[]{:S(2)}) collective-permute-start(bf16[256,1152]{1,0:T(8,128)(2,1)S(1)} %copy-done), channel_id=1, source_target_pairs={{0,22},{1,23},{2,24},{3,25},{4,26},{5,27},{6,28},{7,29},{8,30},{9,... | collective-permute-start | bytes 1769480 | tf_op jit(solution)/shard_map/ppermute | solution.py:158
  21.2 7.6 %collective-permute-start.1 = (bf16[256,1152]{1,0:T(8,128)(2,1)S(1)}, bf16[256,1152]{1,0:T(8,128)(2,1)S(1)}, u32[]{:S(2)}, u32[]{:S(2)}) collective-permute-start(bf16[256,1152]{1,0:T(8,128)(2,1)S(1)} %copy-done.1), channel_id=1, source_target_pairs={{0,506},{1,507},{2,508},{3,509},{4,510},{5,511},{6,496},{7,497},{8... | collective-permute-start | bytes 1769480 | tf_op jit(solution)/shard_map/ppermute | solution.py:158
  28.8 0.0 copy-done.3
  28.9 0.8 copy.19.column
  31.0 0.1 pad_maximum_fusion.1.temper
  31.1 0.0 collective-permute-done.4.other
  31.1 0.0 copy-start.2
  31.1 0.9 copy-done.2
  32.0 3.5 %shard_map.68 = (bf16[256,1152]{1,0:T(8,128)(2,1)S(1)}, bf16[256,1152]{1,0:T(8,128)(2,1)S(1)}, bf16[256,1152]{1,0:T(8,128)(2,1)S(1)}, bf16[256,1152]{1,0:T(8,128...) custom-call(f32[2]{0:T(128)S(1)} %pad_maximum_fusion.1.temper, ...), custom_call_target="tpu_custom_call" | custom-call | flops 1000 | bytes 1000 | tf_op jit(solution)/shard_map/pallas_call | solution.py:37
  35.5 0.0 collective-permute-done.2.text
  35.5 13.9 %collective-permute-done.3.image = bf16[256,1152]{1,0:T(8,128)(2,1)} collective-permute-done((bf16[256,1152]{1,0:T(8,128)(2,1)S(1)}, bf16[256,1152]{1,0:T(8,128)(2,1)}, u32[]{:S(2)}, u32[]{:S(2)}) %collective-permute-start.3) | collective-permute-done | bytes 589856 | tf_op jit(solution)/shard_map/ppermute | solution.py:158
  49.4 1.9 %collective-permute-start.6 = (bf16[256,1152]{1,0:T(8,128)(2,1)}, bf16[256,1152]{1,0:T(8,128)(2,1)S(1)}, u32[]{:S(2)}, u32[]{:S(2)}) collective-permute-start(bf16[256,1152]{1,0:T(8,128)(2,1)} %collective-permute-done.2.text), channel_id=1, source_target_pairs={{0,17},{1,2},{2,19},{3,4},{4,21},{5,6},{6,23},{7,8},{8,25},{9,10},... | collective-permute-start | bytes 1769480 | tf_op jit(solution)/shard_map/ppermute | solution.py:158
  51.3 12.0 %collective-permute-start.7 = (bf16[256,1152]{1,0:T(8,128)(2,1)}, bf16[256,1152]{1,0:T(8,128)(2,1)S(1)}, u32[]{:S(2)}, u32[]{:S(2)}) collective-permute-start(bf16[256,1152]{1,0:T(8,128)(2,1)} %collective-permute-done.3.image), channel_id=1, source_target_pairs={{0,15},{1,496},{2,1},{3,498},{4,3},{5,500},{6,5},{7,502},{8,7},{9,... | collective-permute-start | bytes 1769480 | tf_op jit(solution)/shard_map/ppermute | solution.py:158
  63.3 4.0 %shard_map.69 = (f32[256,1152]{1,0:T(8,128)S(1)}, f32[256,1152]{1,0:T(8,128)S(1)}, f32[256,1152]{1,0:T(8,128)S(1)}, f32[256,1152]{1,0:T(8,128)S(1)}) custom-call(f32[2]{0:T(128)S(1)} %pad_maximum_fusion.1.temper, bf16[256,1152]{1,0:T(8,128)(2,1)} %collective-permute-done.2.text, ...), custom_call_target="tpu_custom_call", output_to_operand_aliasing={{0}: (7, {}), {1}: (8, {}), {2}: (9, {}), {3}: (10, {})} | custom-call | flops 1000 | bytes 1000 | tf_op jit(solution)/shard_map/pallas_call | solution.py:37
  67.3 3.5 %collective-permute-done.d_text = bf16[256,1152]{1,0:T(8,128)(2,1)S(1)} collective-permute-done((bf16[256,1152]{1,0:T(8,128)(2,1)S(1)}, bf16[256,1152]{1,0:T(8,128)(2,1)S(1)}, u32[]{:S(2)}, u32[]{:S(2)}) %collective-permute-start) | collective-permute-done | bytes 589856 | tf_op jit(solution)/shard_map/ppermute | solution.py:158
  70.8 0.0 collective-permute-done.1.d_image
  70.8 1.9 %collective-permute-start.8 = (bf16[256,1152]{1,0:T(8,128)(2,1)S(1)}, bf16[256,1152]{1,0:T(8,128)(2,1)S(1)}, u32[]{:S(2)}, u32[]{:S(2)}) collective-permute-start(bf16[256,1152]{1,0:T(8,128)(2,1)S(1)} %collective-permute-done.1.d_image), channel_id=1, source_target_pairs={{0,2},{1,3},{2,4},{3,5},{4,6},{5,7},{6,8},{7,9},{8,10},{9,11},{10,... | collective-permute-start | bytes 1769480 | tf_op jit(solution)/shard_map/ppermute | solution.py:158
  72.8 5.5 %collective-permute-start.5 = (bf16[256,1152]{1,0:T(8,128)(2,1)S(1)}, bf16[256,1152]{1,0:T(8,128)(2,1)S(1)}, u32[]{:S(2)}, u32[]{:S(2)}) collective-permute-start(bf16[256,1152]{1,0:T(8,128)(2,1)S(1)} %collective-permute-done.d_text), channel_id=1, source_target_pairs={{0,14},{1,15},{2,0},{3,1},{4,2},{5,3},{6,4},{7,5},{8,6},{9,7},{10,... | collective-permute-start | bytes 1769480 | tf_op jit(solution)/shard_map/ppermute | solution.py:158
  78.2 3.9 %collective-permute-done.6.b_text = bf16[256,1152]{1,0:T(8,128)(2,1)S(1)} collective-permute-done((bf16[256,1152]{1,0:T(8,128)(2,1)}, bf16[256,1152]{1,0:T(8,128)(2,1)S(1)}, u32[]{:S(2)}, u32[]{:S(2)}) %collective-permute-start.6) | collective-permute-done | bytes 589856 | tf_op jit(solution)/shard_map/ppermute | solution.py:158
  82.2 0.0 collective-permute-done.7.b_image
  82.2 5.6 %shard_map.70 = (f32[256,1152]{1,0:T(8,128)S(1)}, f32[256,1152]{1,0:T(8,128)S(1)}, f32[256,1152]{1,0:T(8,128)S(1)}, f32[256,1152]{1,0:T(8,128)S(1)}) custom-call(f32[2]{0:T(128)S(1)} %pad_maximum_fusion.1.temper, s32[1]{0:T(128)} %bitcast.flags, ...), custom_call_target="tpu_custom_call", output_to_operand_aliasing={{0}: (10, {}), {1}: (11, {}), {2}: (12, {}), {3}: (13, {})} | custom-call | flops 1000 | bytes 1000 | tf_op jit(solution)/shard_map/pallas_call | solution.py:37
  87.8 0.2 collective-permute-done.8.c_block
  88.0 1.6 %shard_map.72 = (bf16[256,1152]{1,0:T(8,128)(2,1)S(1)}, f32[256,1152]{1,0:T(8,128)S(1)}) custom-call(f32[2]{0:T(128)S(1)} %pad_maximum_fusion.1.temper, bf16[256,1152]{1,0:T(8,128)(2,1)S(1)} %collective-permute-done.8.c_block, bf16[256,1152]{1,0:T(8,128)(2,1)S(1)} %get-tuple-element.45.text_other.other, ...), custom_call_target="tpu_custom_call", output_to_operand_aliasing={{1}: (3, {})} | custom-call | flops 1000 | bytes 1000 | tf_op jit(solution)/shard_map/pallas_call | solution.py:37
  89.6 12.1 %collective-permute-start.10 = (f32[256,1152]{1,0:T(8,128)S(1)}, f32[256,1152]{1,0:T(8,128)S(1)}, u32[]{:S(2)}, u32[]{:S(2)}) collective-permute-start(f32[256,1152]{1,0:T(8,128)S(1)} %get-tuple-element.69), channel_id=1, source_target_pairs={{0,1},{1,0},{2,3},{3,2},{4,5},{5,4},{6,7},{7,6},{8,9},{9,8},{10,11... | collective-permute-start | bytes 3538952 | tf_op jit(solution)/shard_map/ppermute | solution.py:158
  101.7 0.0 collective-permute-done.5.c_block
  101.7 1.6 %shard_map.71 = (bf16[256,1152]{1,0:T(8,128)(2,1)S(1)}, f32[256,1152]{1,0:T(8,128)S(1)}) custom-call(f32[2]{0:T(128)S(1)} %pad_maximum_fusion.1.temper, bf16[256,1152]{1,0:T(8,128)(2,1)S(1)} %collective-permute-done.5.c_block, bf16[256,1152]{1,0:T(8,128)(2,1)S(1)} %get-tuple-element.43.image_other.other, ...), custom_call_target="tpu_custom_call", output_to_operand_aliasing={{1}: (3, {})} | custom-call | flops 1000 | bytes 1000 | tf_op jit(solution)/shard_map/pallas_call | solution.py:37
  103.3 1.9 %collective-permute-start.9 = (f32[256,1152]{1,0:T(8,128)S(1)}, f32[256,1152]{1,0:T(8,128)S(1)}, u32[]{:S(2)}, u32[]{:S(2)}) collective-permute-start(f32[256,1152]{1,0:T(8,128)S(1)} %get-tuple-element.67), channel_id=1, source_target_pairs={{0,1},{1,0},{2,3},{3,2},{4,5},{5,4},{6,7},{7,6},{8,9},{9,8},{10,11... | collective-permute-start | bytes 3538952 | tf_op jit(solution)/shard_map/ppermute | solution.py:158
  105.3 2.3 %shard_map.73 = (f32[256,1152]{1,0:T(8,128)S(1)}, f32[256,1152]{1,0:T(8,128)S(1)}) custom-call(f32[2]{0:T(128)S(1)} %pad_maximum_fusion.1.temper, bf16[256,1152]{1,0:T(8,128)(2,1)S(1)} %get-tuple-element.61.c_text, bf16[256,1152]{1,0:T(8,128)(2,1)S(1)} %get-tuple-element.42.image_half, ...), custom_call_target="tpu_custom_call", output_to_operand_aliasing={{0}: (3, {}), {1}: (6, {})} | custom-call | flops 1000 | bytes 1000 | tf_op jit(solution)/shard_map/pallas_call | solution.py:37
  107.5 0.0 collective-permute-done.10.received
  107.5 1.5 %shard_map.75 = f32[256,1152]{1,0:T(8,128)} custom-call(bf16[256,1152]{1,0:T(8,128)(2,1)S(1)} %copy-done, f32[256,1152]{1,0:T(8,128)S(1)} %get-tuple-element.68.near, f32[256,1152]{1,0:T(8,128)S(1)} %collective-permute-done.10.received), custom_call_target="tpu_custom_call" | custom-call | flops 1000 | bytes 1000 | tf_op jit(solution)/shard_map/pallas_call | solution.py:37
  109.0 0.0 collective-permute-done.9.received
  109.0 1.5 %shard_map.74 = f32[256,1152]{1,0:T(8,128)} custom-call(bf16[256,1152]{1,0:T(8,128)(2,1)S(1)} %copy-done.1, f32[256,1152]{1,0:T(8,128)S(1)} %get-tuple-element.66.near, f32[256,1152]{1,0:T(8,128)S(1)} %collective-permute-done.9.received), custom_call_target="tpu_custom_call" | custom-call | flops 1000 | bytes 1000 | tf_op jit(solution)/shard_map/pallas_call | solution.py:37
  (1 shorter events, 0.0 us)
Async XLA Ops:
  0.6 13.2 %copy-start.1 = (bf16[256,1152]{1,0:T(8,128)(2,1)S(1)}, bf16[256,1152]{1,0:T(8,128)(2,1)}, u32[]{:S(2)}) copy-start(bf16[256,1152]{1,0:T(8,128)(2,1)} %rows.2) | copy-start | bytes 1769476
  0.6 11.2 %copy-start = (bf16[256,1152]{1,0:T(8,128)(2,1)S(1)}, bf16[256,1152]{1,0:T(8,128)(2,1)}, u32[]{:S(2)}) copy-start(bf16[256,1152]{1,0:T(8,128)(2,1)} %rows.3) | copy-start | bytes 1769476
  0.6 28.2 %copy-start.3 = (s32[256]{0:T(256)S(1)}, s32[256]{0:T(256)}, u32[]{:S(2)}) copy-start(s32[256]{0:T(256)} %param.7) | copy-start | bytes 3076
  3.1 28.0 %collective-permute-start.4 = (bf16[512,1152]{1,0:T(8,128)(2,1)}, bf16[512,1152]{1,0:T(8,128)(2,1)S(1)}, u32[]{:S(2)}, u32[]{:S(2)}) collective-permute-start(bf16[512,1152]{1,0:T(8,128)(2,1)} %pad_maximum_fusion), channel_id=1, source_target_pairs={{0,1},{1,0},{2,3},{3,2},{4,5},{5,4},{6,7},{7,6},{8,9},{9,8},{10,11... | collective-permute-start | bytes 3538952 | tf_op jit(solution)/shard_map/ppermute | solution.py:158
  11.9 23.6 %collective-permute-start.2 = (bf16[256,1152]{1,0:T(8,128)(2,1)S(1)}, bf16[256,1152]{1,0:T(8,128)(2,1)}, u32[]{:S(2)}, u32[]{:S(2)}) collective-permute-start(bf16[256,1152]{1,0:T(8,128)(2,1)S(1)} %copy-done), channel_id=1, source_target_pairs={{0,2},{1,3},{2,4},{3,5},{4,6},{5,7},{6,8},{7,9},{8,10},{9,11},{10,... | collective-permute-start | bytes 1769480 | tf_op jit(solution)/shard_map/ppermute | solution.py:158
  13.8 35.6 %collective-permute-start.3 = (bf16[256,1152]{1,0:T(8,128)(2,1)S(1)}, bf16[256,1152]{1,0:T(8,128)(2,1)}, u32[]{:S(2)}, u32[]{:S(2)}) collective-permute-start(bf16[256,1152]{1,0:T(8,128)(2,1)S(1)} %copy-done.1), channel_id=1, source_target_pairs={{0,14},{1,15},{2,0},{3,1},{4,2},{5,3},{6,4},{7,5},{8,6},{9,7},{10,... | collective-permute-start | bytes 1769480 | tf_op jit(solution)/shard_map/ppermute | solution.py:158
  19.3 51.5 %collective-permute-start = (bf16[256,1152]{1,0:T(8,128)(2,1)S(1)}, bf16[256,1152]{1,0:T(8,128)(2,1)S(1)}, u32[]{:S(2)}, u32[]{:S(2)}) collective-permute-start(bf16[256,1152]{1,0:T(8,128)(2,1)S(1)} %copy-done), channel_id=1, source_target_pairs={{0,22},{1,23},{2,24},{3,25},{4,26},{5,27},{6,28},{7,29},{8,30},{9,... | collective-permute-start | bytes 1769480 | tf_op jit(solution)/shard_map/ppermute | solution.py:158
  21.2 49.6 %collective-permute-start.1 = (bf16[256,1152]{1,0:T(8,128)(2,1)S(1)}, bf16[256,1152]{1,0:T(8,128)(2,1)S(1)}, u32[]{:S(2)}, u32[]{:S(2)}) collective-permute-start(bf16[256,1152]{1,0:T(8,128)(2,1)S(1)} %copy-done.1), channel_id=1, source_target_pairs={{0,506},{1,507},{2,508},{3,509},{4,510},{5,511},{6,496},{7,497},{8... | collective-permute-start | bytes 1769480 | tf_op jit(solution)/shard_map/ppermute | solution.py:158
  31.1 0.9 copy-start.2
  49.4 32.8 %collective-permute-start.6 = (bf16[256,1152]{1,0:T(8,128)(2,1)}, bf16[256,1152]{1,0:T(8,128)(2,1)S(1)}, u32[]{:S(2)}, u32[]{:S(2)}) collective-permute-start(bf16[256,1152]{1,0:T(8,128)(2,1)} %collective-permute-done.2.text), channel_id=1, source_target_pairs={{0,17},{1,2},{2,19},{3,4},{4,21},{5,6},{6,23},{7,8},{8,25},{9,10},... | collective-permute-start | bytes 1769480 | tf_op jit(solution)/shard_map/ppermute | solution.py:158
  51.3 30.9 %collective-permute-start.7 = (bf16[256,1152]{1,0:T(8,128)(2,1)}, bf16[256,1152]{1,0:T(8,128)(2,1)S(1)}, u32[]{:S(2)}, u32[]{:S(2)}) collective-permute-start(bf16[256,1152]{1,0:T(8,128)(2,1)} %collective-permute-done.3.image), channel_id=1, source_target_pairs={{0,15},{1,496},{2,1},{3,498},{4,3},{5,500},{6,5},{7,502},{8,7},{9,... | collective-permute-start | bytes 1769480 | tf_op jit(solution)/shard_map/ppermute | solution.py:158
  70.8 17.1 %collective-permute-start.8 = (bf16[256,1152]{1,0:T(8,128)(2,1)S(1)}, bf16[256,1152]{1,0:T(8,128)(2,1)S(1)}, u32[]{:S(2)}, u32[]{:S(2)}) collective-permute-start(bf16[256,1152]{1,0:T(8,128)(2,1)S(1)} %collective-permute-done.1.d_image), channel_id=1, source_target_pairs={{0,2},{1,3},{2,4},{3,5},{4,6},{5,7},{6,8},{7,9},{8,10},{9,11},{10,... | collective-permute-start | bytes 1769480 | tf_op jit(solution)/shard_map/ppermute | solution.py:158
  72.8 28.9 %collective-permute-start.5 = (bf16[256,1152]{1,0:T(8,128)(2,1)S(1)}, bf16[256,1152]{1,0:T(8,128)(2,1)S(1)}, u32[]{:S(2)}, u32[]{:S(2)}) collective-permute-start(bf16[256,1152]{1,0:T(8,128)(2,1)S(1)} %collective-permute-done.d_text), channel_id=1, source_target_pairs={{0,14},{1,15},{2,0},{3,1},{4,2},{5,3},{6,4},{7,5},{8,6},{9,7},{10,... | collective-permute-start | bytes 1769480 | tf_op jit(solution)/shard_map/ppermute | solution.py:158
  89.6 17.9 %collective-permute-start.10 = (f32[256,1152]{1,0:T(8,128)S(1)}, f32[256,1152]{1,0:T(8,128)S(1)}, u32[]{:S(2)}, u32[]{:S(2)}) collective-permute-start(f32[256,1152]{1,0:T(8,128)S(1)} %get-tuple-element.69), channel_id=1, source_target_pairs={{0,1},{1,0},{2,3},{3,2},{4,5},{5,4},{6,7},{7,6},{8,9},{9,8},{10,11... | collective-permute-start | bytes 3538952 | tf_op jit(solution)/shard_map/ppermute | solution.py:158
  103.3 5.7 %collective-permute-start.9 = (f32[256,1152]{1,0:T(8,128)S(1)}, f32[256,1152]{1,0:T(8,128)S(1)}, u32[]{:S(2)}, u32[]{:S(2)}) collective-permute-start(f32[256,1152]{1,0:T(8,128)S(1)} %get-tuple-element.67), channel_id=1, source_target_pairs={{0,1},{1,0},{2,3},{3,2},{4,5},{5,4},{6,7},{7,6},{8,9},{9,8},{10,11... | collective-permute-start | bytes 3538952 | tf_op jit(solution)/shard_map/ppermute | solution.py:158

commit v5 on v4

v5 whole, which is shorter than its diff:
```python
import functools

import jax
import jax.numpy as jnp
from jax import lax
from jax.experimental import pallas as pl
from jax.experimental.pallas import tpu as pltpu
from jax.sharding import PartitionSpec as P

EPS = 1e-06
AXES = ("wide", "narrow")
NT = (((1,), (1,)), ((), ()))
NN = (((1,), (0,)), ((), ()))
VMEM_LIMIT = 20 * 1024 * 1024
F32 = jnp.float32
BF16 = jnp.bfloat16


def mm(a, b, dims):
    return lax.dot_general(a, b, dims, preferred_element_type=F32)


def unit_of(rows):
    floats = rows.astype(F32)
    inverse = lax.rsqrt(jnp.sum(floats * floats, axis=-1, keepdims=True) + EPS)
    return floats * inverse, inverse


def half_of(rows):
    return unit_of(rows)[0].astype(BF16)


def call(kernel, outs, inputs, aliases=None):
    specs = [
        pl.BlockSpec(memory_space=pltpu.SMEM if x.ndim == 1 else pltpu.VMEM) for x in inputs
    ]
    return pl.pallas_call(
        kernel,
        out_shape=outs,
        in_specs=specs,
        out_specs=[pl.BlockSpec(memory_space=pltpu.VMEM) for _ in outs],
        input_output_aliases=aliases or {},
        compiler_params=pltpu.CompilerParams(vmem_limit_bytes=VMEM_LIMIT),
        cost_estimate=pl.CostEstimate(flops=1000, bytes_accessed=1000, transcendentals=0),
    )(*inputs)


def weigh(temper, resident, block, positive=None):
    scale, offset = temper[0], temper[1]
    residual = jax.nn.sigmoid(scale * mm(resident, block, NT) + offset)
    if positive is not None:
        residual = residual - positive.astype(F32)
    return (scale * residual).astype(BF16)


def own_kernel(
    temper, flags, column, row, texts, images, other,
    text_half, image_half, text_other, image_other,
    image_near, image_far, text_near, text_far,
):
    rows = texts.shape[0]
    text, image = half_of(texts[...]), half_of(images[...])
    text_half[...] = text
    image_half[...] = image
    text_other[...] = half_of(other[:rows])
    image_other[...] = half_of(other[rows:])
    target = lax.broadcasted_iota(jnp.int32, (rows, rows), 1)
    image_near[...] = mm(weigh(temper, image, text, column[...] == target), text, NN)
    target = lax.broadcasted_iota(jnp.int32, (rows, rows), 0)
    text_near[...] = mm(weigh(temper, text, image, row[...] == target), image, NN)

    @pl.when(flags[0] == 0)
    def _():
        image_far[...] = mm(weigh(temper, image_other[...], text), text, NN)
        text_far[...] = jnp.zeros(text_far.shape, F32)

    @pl.when(flags[0] == 1)
    def _():
        text_far[...] = mm(weigh(temper, text_other[...], image), image, NN)
        image_far[...] = jnp.zeros(image_far.shape, F32)


def meet(wanted, temper, resident, block, before, after):
    @pl.when(wanted != 0)
    def _():
        after[...] = before[...] + mm(weigh(temper, resident[...], block), block, NN)

    @pl.when(wanted == 0)
    def _():
        after[...] = before[...]


def visit_kernel(
    temper, flags, text, image, image_half, image_other, text_half, text_other,
    image_near_in, image_far_in, text_near_in, text_far_in,
    image_near, image_far, text_near, text_far,
):
    for k, visitor, near_res, far_res, near_in, far_in, near, far in (
        (0, text, image_half, image_other, image_near_in, image_far_in, image_near, image_far),
        (2, image, text_half, text_other, text_near_in, text_far_in, text_near, text_far),
    ):
        block = half_of(visitor[...])
        meet(flags[k], temper, near_res, block, near_in, near)
        meet(flags[k + 1], temper, far_res, block, far_in, far)


def far_kernel(k, temper, flags, visitor, far_res, far_in, half, far):
    block = half_of(visitor[...])
    half[...] = block
    meet(flags[k + 1], temper, far_res, block, far_in, far)


def near_kernel(
    temper, flags, text, image_half, image_in, image, text_half, text_in, image_out, text_out
):
    meet(flags[0], temper, image_half, text[...], image_in, image_out)
    meet(flags[2], temper, text_half, image[...], text_in, text_out)


def finish_kernel(rows, near, received, grad):
    upstream = near[...] + received[...]
    unit, inverse = unit_of(rows[...])
    along = jnp.sum(unit * upstream, axis=-1, keepdims=True)
    grad[...] = inverse * (upstream - unit * along)


STEPS = ({"A": (0, 1), "B": (1, 1), "C": (1, 2), "D": (1, 3)},
         {"A": (0, 1), "B": (0, 2), "C": (1, 2), "D": (1, 3)})
MEETS = ({"A": (1, 1), "B": (0, 1), "C": (1, 1), "D": (1, 0)},
         {"A": (1, 1), "B": (0, 1), "C": (1, 1), "D": (1, 1)})
PLAN = ("DACB", "ADBC")


def plan_of(chip, parity):
    return PLAN[parity]


def hops_of(n_wide, n_narrow):
    chips = n_narrow // 2
    pairs, kinds = [], []
    for k in range(4):
        moves, kind = {}, {}
        for w in range(n_wide):
            for n in range(n_narrow):
                chip, parity = n // 2, n % 2
                plan, steps = plan_of(chip, parity), STEPS[parity]
                before = (0, 0) if k < 2 else steps[plan[k - 2]]
                place = [
                    ((w + a) % n_wide, ((chip + b) % chips) * 2 + parity)
                    for a, b in (before, steps[plan[k]])
                ]
                moves[place[0]] = place[1]
                kind[place[1][1]] = plan[k]
        assert len(moves) == len(set(moves.values())) == n_wide * n_narrow
        pairs.append(moves)
        kinds.append([kind[n] for n in range(n_narrow)])
    return pairs, kinds


def shards(images, texts, labels, log_scale, bias):
    n_wide, n_narrow = lax.axis_size("wide"), lax.axis_size("narrow")
    wide, narrow = lax.axis_index("wide"), lax.axis_index("narrow")
    rows, width = images.shape
    core = narrow % 2
    pairs, kinds = hops_of(n_wide, n_narrow)

    def moved(value, moves):
        flat = [(a * n_narrow + b, c * n_narrow + d) for (a, b), (c, d) in sorted(moves.items())]
        return lax.ppermute(value, AXES, flat)

    def mirrored(moves):
        def turn(place):
            return ((-place[0]) % n_wide, n_narrow - 1 - place[1])

        return {turn(a): turn(b) for a, b in moves.items()}

    def hop(k, text, image):
        return moved(text, pairs[k]), moved(image, mirrored(pairs[k]))

    def swapped(value):
        return moved(
            value,
            {(w, n): (w, n + 1 - 2 * (n % 2)) for w in range(n_wide) for n in range(n_narrow)},
        )

    def flags_of(k):
        table = []
        for n in range(n_narrow):
            m = n_narrow - 1 - n
            line = [*MEETS[n % 2][kinds[k][n]], *MEETS[m % 2][kinds[k][m]]]
            table.append(line)
        return jnp.asarray(table, jnp.int32)[narrow]

    temper = jnp.stack([jnp.exp(log_scale[0]), bias[0]])
    local = labels - (wide * n_narrow + narrow) * rows
    half = jax.ShapeDtypeStruct((rows, width), BF16)
    full = jax.ShapeDtypeStruct((rows, width), F32)

    first = hop(0, texts, images)
    second = hop(1, texts, images)
    other = swapped(jnp.concatenate([texts, images]))
    flags = core.reshape(1).astype(jnp.int32)
    (text_half, image_half, text_other, image_other, *sums) = call(
        own_kernel,
        [half] * 4 + [full] * 4,
        [temper, flags, local.reshape(rows, 1), local.reshape(1, rows), texts, images, other],
    )
    residents = [image_half, image_other, text_half, text_other]

    def visit(k, visitors, sums):
        return call(
            visit_kernel,
            [full] * 4,
            [temper, flags_of(k), *visitors, *residents, *sums],
            {8: 0, 9: 1, 10: 2, 11: 3},
        )

    *first, a, b, c, d = lax.optimization_barrier((*first, *sums))
    third = hop(2, *first)
    sums = visit(0, first, [a, b, c, d])
    *second, a, b, c, d = lax.optimization_barrier((*second, *sums))
    fourth = hop(3, *second)
    sums = visit(1, second, [a, b, c, d])
    sums = visit(2, third, sums)
    image_near, image_far, text_near, text_far = sums

    def far(k, visitor, other, far_sum):
        kernel = functools.partial(far_kernel, k)
        return call(
            kernel, [half, full], [temper, flags_of(3), visitor, other, far_sum], {4: 1}
        )

    text, image_far = far(0, fourth[0], image_other, image_far)
    image_back = swapped(image_far)
    image, text_far = far(2, fourth[1], text_other, text_far)
    text_back = swapped(text_far)
    image_near, text_near = call(
        near_kernel,
        [full, full],
        [temper, flags_of(3), text, image_half, image_near, image, text_half, text_near],
        {4: 0, 7: 1},
    )
    (grad_images,) = call(finish_kernel, [full], [images, image_near, image_back])
    (grad_texts,) = call(finish_kernel, [full], [texts, text_near, text_back])
    return (grad_images, grad_texts)


def solution(mesh):
    return jax.shard_map(
        shards,
        mesh=mesh,
        in_specs=(P(AXES, None), P(AXES, None), P(AXES), P(), P()),
        out_specs=(P(AXES, None), P(AXES, None)),
        check_vma=False,
    )
```

time: 111 us -> 105 us (0.946)
  the two profiles are of different devices: /device:TPU:1 before, /device:TPU:7 now
where the time goes in v5:
time: 105 us
  starting transfers between devices  66 us (63%)
  Pallas kernels  24.7 us (24%)
  waiting for transfers between devices  5.16 us (5%)
  local copies, waits for them, and re-layouts  3.8 us (4%)
  other arithmetic  2.52 us (2%)
  between operations  2.25 us (2%)
    ppermute x11, starting transfers between devices, moved(): return lax.ppermute(value, AXES, flat)  66 us
    pallas_call x9, Pallas kernels, call(): pl.pallas_call(kernel, out_shape=outs, in_specs=specs, out_specs=[pl.Bloc...  24.7 us
    ppermute x11, waiting for transfers between devices, moved(): return lax.ppermute(value, AXES, flat)  5.16 us
    concatenate x1, other arithmetic, shards(): other = swapped(jnp.concatenate([texts, images]))  2.44 us
  transfers between devices with their start and end apart: 11, of which 1 were waited for; matrix products, arithmetic and copies ran while one was open for 3% of the time, Pallas kernels for 22%

profile of v5, /device:TPU:7, one launch (start us, length us, event | category | flops | bytes accessed | tf_op | source)
XLA Modules:
  0.0 104.5 jit_solution(10622804169199801035)
XLA Ops:
  0.6 0.0 copy-start.1
  0.6 0.0 copy-start
  0.6 0.0 copy-start.3
  0.7 2.4 %pad_maximum_fusion = bf16[512,1152]{1,0:T(8,128)(2,1)} fusion(bf16[256,1152]{1,0:T(8,128)(2,1)} %rows.2, bf16[256,1152]{1,0:T(8,128)(2,1)} %rows.3), kind=kLoop, calls=%fused_computation | loop fusion | flops 2359296 | bytes 2359296 | tf_op jit(solution)/shard_map/concatenate | solution.py:201
  3.1 2.6 %collective-permute-start.4 = (bf16[512,1152]{1,0:T(8,128)(2,1)}, bf16[512,1152]{1,0:T(8,128)(2,1)S(1)}, u32[]{:S(2)}, u32[]{:S(2)}) collective-permute-start(bf16[512,1152]{1,0:T(8,128)(2,1)} %pad_maximum_fusion), channel_id=1, source_target_pairs={{0,1},{1,0},{2,3},{3,2},{4,5},{5,4},{6,7},{7,6},{8,9},{9,8},{10,11... | collective-permute-start | bytes 3538952 | tf_op jit(solution)/shard_map/ppermute | solution.py:169
  5.7 0.0 copy-done
  5.7 3.1 %collective-permute-start.2 = (bf16[256,1152]{1,0:T(8,128)(2,1)S(1)}, bf16[256,1152]{1,0:T(8,128)(2,1)}, u32[]{:S(2)}, u32[]{:S(2)}) collective-permute-start(bf16[256,1152]{1,0:T(8,128)(2,1)S(1)} %copy-done), channel_id=1, source_target_pairs={{0,22},{1,3},{2,24},{3,5},{4,26},{5,7},{6,28},{7,9},{8,30},{9,11},... | collective-permute-start | bytes 1769480 | tf_op jit(solution)/shard_map/ppermute | solution.py:169
  8.8 0.0 copy-done.1
  8.8 14.3 %collective-permute-start.3 = (bf16[256,1152]{1,0:T(8,128)(2,1)S(1)}, bf16[256,1152]{1,0:T(8,128)(2,1)}, u32[]{:S(2)}, u32[]{:S(2)}) collective-permute-start(bf16[256,1152]{1,0:T(8,128)(2,1)S(1)} %copy-done.1), channel_id=1, source_target_pairs={{0,14},{1,507},{2,0},{3,509},{4,2},{5,511},{6,4},{7,497},{8,6},{9,... | collective-permute-start | bytes 1769480 | tf_op jit(solution)/shard_map/ppermute | solution.py:169
  23.1 1.9 %collective-permute-start = (bf16[256,1152]{1,0:T(8,128)(2,1)S(1)}, bf16[256,1152]{1,0:T(8,128)(2,1)S(1)}, u32[]{:S(2)}, u32[]{:S(2)}) collective-permute-start(bf16[256,1152]{1,0:T(8,128)(2,1)S(1)} %copy-done), channel_id=1, source_target_pairs={{0,2},{1,23},{2,4},{3,25},{4,6},{5,27},{6,8},{7,29},{8,10},{9,31},... | collective-permute-start | bytes 1769480 | tf_op jit(solution)/shard_map/ppermute | solution.py:169
  25.0 2.2 %collective-permute-start.1 = (bf16[256,1152]{1,0:T(8,128)(2,1)S(1)}, bf16[256,1152]{1,0:T(8,128)(2,1)S(1)}, u32[]{:S(2)}, u32[]{:S(2)}) collective-permute-start(bf16[256,1152]{1,0:T(8,128)(2,1)S(1)} %copy-done.1), channel_id=1, source_target_pairs={{0,506},{1,15},{2,508},{3,1},{4,510},{5,3},{6,496},{7,5},{8,498},{... | collective-permute-start | bytes 1769480 | tf_op jit(solution)/shard_map/ppermute | solution.py:169
  27.2 0.0 copy-done.3
  27.2 0.8 copy.29.column
  29.4 0.1 pad_maximum_fusion.1.temper
  29.5 0.7 fusion.2.flags
  30.2 0.0 collective-permute-done.4.other
  30.2 0.0 copy-start.2
  30.2 0.9 copy-done.2
  31.1 3.5 %shard_map.122 = (bf16[256,1152]{1,0:T(8,128)(2,1)S(1)}, bf16[256,1152]{1,0:T(8,128)(2,1)S(1)}, bf16[256,1152]{1,0:T(8,128)(2,1)S(1)}, bf16[256,1152]{1,0:T(8,12...) custom-call(f32[2]{0:T(128)S(1)} %pad_maximum_fusion.1.temper, ...), custom_call_target="tpu_custom_call" | custom-call | flops 1000 | bytes 1000 | tf_op jit(solution)/shard_map/pallas_call | solution.py:37
  34.6 0.0 collective-permute-done.2.text
  34.6 0.0 collective-permute-done.3.image
  34.6 14.9 %collective-permute-start.6 = (bf16[256,1152]{1,0:T(8,128)(2,1)}, bf16[256,1152]{1,0:T(8,128)(2,1)S(1)}, u32[]{:S(2)}, u32[]{:S(2)}) collective-permute-start(bf16[256,1152]{1,0:T(8,128)(2,1)} %collective-permute-done.2.text), channel_id=1, source_target_pairs={{0,14},{1,3},{2,0},{3,5},{4,2},{5,7},{6,4},{7,9},{8,6},{9,11},{10,... | collective-permute-start | bytes 1769480 | tf_op jit(solution)/shard_map/ppermute | solution.py:169
  49.5 1.9 %collective-permute-start.7 = (bf16[256,1152]{1,0:T(8,128)(2,1)}, bf16[256,1152]{1,0:T(8,128)(2,1)S(1)}, u32[]{:S(2)}, u32[]{:S(2)}) collective-permute-start(bf16[256,1152]{1,0:T(8,128)(2,1)} %collective-permute-done.3.image), channel_id=1, source_target_pairs={{0,14},{1,3},{2,0},{3,5},{4,2},{5,7},{6,4},{7,9},{8,6},{9,11},{10,... | collective-permute-start | bytes 1769480 | tf_op jit(solution)/shard_map/ppermute | solution.py:169
  51.4 4.6 %shard_map.123 = (f32[256,1152]{1,0:T(8,128)S(1)}, f32[256,1152]{1,0:T(8,128)S(1)}, f32[256,1152]{1,0:T(8,128)S(1)}, f32[256,1152]{1,0:T(8,128)S(1)}) custom-call(f32[2]{0:T(128)S(1)} %pad_maximum_fusion.1.temper, s32[4]{0:T(128)S(1)} %fusion.2.flags, ...), custom_call_target="tpu_custom_call", output_to_operand_aliasing={{0}: (8, {}), {1}: (9, {}), {2}: (10, {}), {3}: (11, {})} | custom-call | flops 1000 | bytes 1000 | tf_op jit(solution)/shard_map/pallas_call | solution.py:37
  56.0 0.0 collective-permute-done.text
  56.0 5.1 %collective-permute-done.1.image = bf16[256,1152]{1,0:T(8,128)(2,1)S(1)} collective-permute-done((bf16[256,1152]{1,0:T(8,128)(2,1)S(1)}, bf16[256,1152]{1,0:T(8,128)(2,1)S(1)}, u32[]{:S(2)}, u32[]{:S(2)}) %collective-permute-start.1) | collective-permute-done | bytes 589856 | tf_op jit(solution)/shard_map/ppermute | solution.py:169
  61.1 10.1 %collective-permute-start.8 = (bf16[256,1152]{1,0:T(8,128)(2,1)S(1)}, bf16[256,1152]{1,0:T(8,128)(2,1)S(1)}, u32[]{:S(2)}, u32[]{:S(2)}) collective-permute-start(bf16[256,1152]{1,0:T(8,128)(2,1)S(1)} %collective-permute-done.1.image), channel_id=1, source_target_pairs={{0,2},{1,497},{2,4},{3,499},{4,6},{5,501},{6,8},{7,503},{8,10},{9,... | collective-permute-start | bytes 1769480 | tf_op jit(solution)/shard_map/ppermute | solution.py:169
  71.2 3.4 %collective-permute-start.5 = (bf16[256,1152]{1,0:T(8,128)(2,1)S(1)}, bf16[256,1152]{1,0:T(8,128)(2,1)S(1)}, u32[]{:S(2)}, u32[]{:S(2)}) collective-permute-start(bf16[256,1152]{1,0:T(8,128)(2,1)S(1)} %collective-permute-done.text), channel_id=1, source_target_pairs={{0,16},{1,15},{2,18},{3,1},{4,20},{5,3},{6,22},{7,5},{8,24},{9,7},... | collective-permute-start | bytes 1769480 | tf_op jit(solution)/shard_map/ppermute | solution.py:169
  74.6 0.7 fusion.1.flags
  75.3 0.7 fusion.flags
  76.0 4.6 %shard_map.124 = (f32[256,1152]{1,0:T(8,128)S(1)}, f32[256,1152]{1,0:T(8,128)S(1)}, f32[256,1152]{1,0:T(8,128)S(1)}, f32[256,1152]{1,0:T(8,128)S(1)}) custom-call(f32[2]{0:T(128)S(1)} %pad_maximum_fusion.1.temper, s32[4]{0:T(128)S(1)} %broadcast.2.flags, ...), custom_call_target="tpu_custom_call", output_to_operand_aliasing={{0}: (8, {}), {1}: (9, {}), {2}: (10, {}), {3}: (11, {})} | custom-call | flops 1000 | bytes 1000 | tf_op jit(solution)/shard_map/pallas_call | solution.py:37
  80.6 0.0 collective-permute-done.6.text
  80.6 0.0 collective-permute-done.7.image
  80.7 4.1 %shard_map.125 = (f32[256,1152]{1,0:T(8,128)S(1)}, f32[256,1152]{1,0:T(8,128)S(1)}, f32[256,1152]{1,0:T(8,128)S(1)}, f32[256,1152]{1,0:T(8,128)S(1)}) custom-call(f32[2]{0:T(128)S(1)} %pad_maximum_fusion.1.temper, s32[4]{0:T(128)S(1)} %fusion.1.flags, ...), custom_call_target="tpu_custom_call", output_to_operand_aliasing={{0}: (8, {}), {1}: (9, {}), {2}: (10, {}), {3}: (11, {})} | custom-call | flops 1000 | bytes 1000 | tf_op jit(solution)/shard_map/pallas_call | solution.py:37
  84.7 0.0 collective-permute-done.8.visitor
  84.7 1.6 %shard_map.127 = (bf16[256,1152]{1,0:T(8,128)(2,1)S(1)}, f32[256,1152]{1,0:T(8,128)S(1)}) custom-call(f32[2]{0:T(128)S(1)} %pad_maximum_fusion.1.temper, s32[4]{0:T(128)S(1)} %fusion.flags, bf16[256,1152]{1,0:T(8,128)(2,1)S(1)} %collective-permute-done.8.visitor, ...), custom_call_target="tpu_custom_call", output_to_operand_aliasing={{1}: (4, {})} | custom-call | flops 1000 | bytes 1000 | tf_op jit(solution)/shard_map/pallas_call | solution.py:37
  86.4 1.9 %collective-permute-start.10 = (f32[256,1152]{1,0:T(8,128)S(1)}, f32[256,1152]{1,0:T(8,128)S(1)}, u32[]{:S(2)}, u32[]{:S(2)}) collective-permute-start(f32[256,1152]{1,0:T(8,128)S(1)} %get-tuple-element.77), channel_id=1, source_target_pairs={{0,1},{1,0},{2,3},{3,2},{4,5},{5,4},{6,7},{7,6},{8,9},{9,8},{10,11... | collective-permute-start | bytes 3538952 | tf_op jit(solution)/shard_map/ppermute | solution.py:169
  88.3 0.0 collective-permute-done.5.visitor
  88.3 1.6 %shard_map.126 = (bf16[256,1152]{1,0:T(8,128)(2,1)S(1)}, f32[256,1152]{1,0:T(8,128)S(1)}) custom-call(f32[2]{0:T(128)S(1)} %pad_maximum_fusion.1.temper, s32[4]{0:T(128)S(1)} %fusion.flags, bf16[256,1152]{1,0:T(8,128)(2,1)S(1)} %collective-permute-done.5.visitor, ...), custom_call_target="tpu_custom_call", output_to_operand_aliasing={{1}: (4, {})} | custom-call | flops 1000 | bytes 1000 | tf_op jit(solution)/shard_map/pallas_call | solution.py:37
  90.0 9.8 %collective-permute-start.9 = (f32[256,1152]{1,0:T(8,128)S(1)}, f32[256,1152]{1,0:T(8,128)S(1)}, u32[]{:S(2)}, u32[]{:S(2)}) collective-permute-start(f32[256,1152]{1,0:T(8,128)S(1)} %get-tuple-element.75), channel_id=1, source_target_pairs={{0,1},{1,0},{2,3},{3,2},{4,5},{5,4},{6,7},{7,6},{8,9},{9,8},{10,11... | collective-permute-start | bytes 3538952 | tf_op jit(solution)/shard_map/ppermute | solution.py:169
  99.8 1.7 %shard_map.128 = (f32[256,1152]{1,0:T(8,128)S(1)}, f32[256,1152]{1,0:T(8,128)S(1)}) custom-call(f32[2]{0:T(128)S(1)} %pad_maximum_fusion.1.temper, s32[4]{0:T(128)S(1)} %fusion.flags, bf16[256,1152]{1,0:T(8,128)(2,1)S(1)} %get-tuple-element.69.text, ...), custom_call_target="tpu_custom_call", output_to_operand_aliasing={{0}: (4, {}), {1}: (7, {})} | custom-call | flops 1000 | bytes 1000 | tf_op jit(solution)/shard_map/pallas_call | solution.py:37
  101.5 0.0 collective-permute-done.10.received
  101.5 1.5 %shard_map.130 = f32[256,1152]{1,0:T(8,128)} custom-call(bf16[256,1152]{1,0:T(8,128)(2,1)S(1)} %copy-done, f32[256,1152]{1,0:T(8,128)S(1)} %get-tuple-element.76.near, f32[256,1152]{1,0:T(8,128)S(1)} %collective-permute-done.10.received), custom_call_target="tpu_custom_call" | custom-call | flops 1000 | bytes 1000 | tf_op jit(solution)/shard_map/pallas_call | solution.py:37
  103.0 0.0 collective-permute-done.9.received
  103.0 1.5 %shard_map.129 = f32[256,1152]{1,0:T(8,128)} custom-call(bf16[256,1152]{1,0:T(8,128)(2,1)S(1)} %copy-done.1, f32[256,1152]{1,0:T(8,128)S(1)} %get-tuple-element.74.near, f32[256,1152]{1,0:T(8,128)S(1)} %collective-permute-done.9.received), custom_call_target="tpu_custom_call" | custom-call | flops 1000 | bytes 1000 | tf_op jit(solution)/shard_map/pallas_call | solution.py:37
  (2 shorter events, 0.0 us)
Async XLA Ops:
  0.6 8.2 %copy-start.1 = (bf16[256,1152]{1,0:T(8,128)(2,1)S(1)}, bf16[256,1152]{1,0:T(8,128)(2,1)}, u32[]{:S(2)}) copy-start(bf16[256,1152]{1,0:T(8,128)(2,1)} %rows.2) | copy-start | bytes 1769476
  0.6 5.0 %copy-start = (bf16[256,1152]{1,0:T(8,128)(2,1)S(1)}, bf16[256,1152]{1,0:T(8,128)(2,1)}, u32[]{:S(2)}) copy-start(bf16[256,1152]{1,0:T(8,128)(2,1)} %rows.3) | copy-start | bytes 1769476
  0.6 26.6 %copy-start.3 = (s32[256]{0:T(256)S(1)}, s32[256]{0:T(256)}, u32[]{:S(2)}) copy-start(s32[256]{0:T(256)} %param.13) | copy-start | bytes 3076
  3.1 27.1 %collective-permute-start.4 = (bf16[512,1152]{1,0:T(8,128)(2,1)}, bf16[512,1152]{1,0:T(8,128)(2,1)S(1)}, u32[]{:S(2)}, u32[]{:S(2)}) collective-permute-start(bf16[512,1152]{1,0:T(8,128)(2,1)} %pad_maximum_fusion), channel_id=1, source_target_pairs={{0,1},{1,0},{2,3},{3,2},{4,5},{5,4},{6,7},{7,6},{8,9},{9,8},{10,11... | collective-permute-start | bytes 3538952 | tf_op jit(solution)/shard_map/ppermute | solution.py:169
  5.7 28.9 %collective-permute-start.2 = (bf16[256,1152]{1,0:T(8,128)(2,1)S(1)}, bf16[256,1152]{1,0:T(8,128)(2,1)}, u32[]{:S(2)}, u32[]{:S(2)}) collective-permute-start(bf16[256,1152]{1,0:T(8,128)(2,1)S(1)} %copy-done), channel_id=1, source_target_pairs={{0,22},{1,3},{2,24},{3,5},{4,26},{5,7},{6,28},{7,9},{8,30},{9,11},... | collective-permute-start | bytes 1769480 | tf_op jit(solution)/shard_map/ppermute | solution.py:169
  8.8 25.8 %collective-permute-start.3 = (bf16[256,1152]{1,0:T(8,128)(2,1)S(1)}, bf16[256,1152]{1,0:T(8,128)(2,1)}, u32[]{:S(2)}, u32[]{:S(2)}) collective-permute-start(bf16[256,1152]{1,0:T(8,128)(2,1)S(1)} %copy-done.1), channel_id=1, source_target_pairs={{0,14},{1,507},{2,0},{3,509},{4,2},{5,511},{6,4},{7,497},{8,6},{9,... | collective-permute-start | bytes 1769480 | tf_op jit(solution)/shard_map/ppermute | solution.py:169
  23.1 32.9 %collective-permute-start = (bf16[256,1152]{1,0:T(8,128)(2,1)S(1)}, bf16[256,1152]{1,0:T(8,128)(2,1)S(1)}, u32[]{:S(2)}, u32[]{:S(2)}) collective-permute-start(bf16[256,1152]{1,0:T(8,128)(2,1)S(1)} %copy-done), channel_id=1, source_target_pairs={{0,2},{1,23},{2,4},{3,25},{4,6},{5,27},{6,8},{7,29},{8,10},{9,31},... | collective-permute-start | bytes 1769480 | tf_op jit(solution)/shard_map/ppermute | solution.py:169
  25.0 36.1 %collective-permute-start.1 = (bf16[256,1152]{1,0:T(8,128)(2,1)S(1)}, bf16[256,1152]{1,0:T(8,128)(2,1)S(1)}, u32[]{:S(2)}, u32[]{:S(2)}) collective-permute-start(bf16[256,1152]{1,0:T(8,128)(2,1)S(1)} %copy-done.1), channel_id=1, source_target_pairs={{0,506},{1,15},{2,508},{3,1},{4,510},{5,3},{6,496},{7,5},{8,498},{... | collective-permute-start | bytes 1769480 | tf_op jit(solution)/shard_map/ppermute | solution.py:169
  30.2 0.9 copy-start.2
  34.6 46.0 %collective-permute-start.6 = (bf16[256,1152]{1,0:T(8,128)(2,1)}, bf16[256,1152]{1,0:T(8,128)(2,1)S(1)}, u32[]{:S(2)}, u32[]{:S(2)}) collective-permute-start(bf16[256,1152]{1,0:T(8,128)(2,1)} %collective-permute-done.2.text), channel_id=1, source_target_pairs={{0,14},{1,3},{2,0},{3,5},{4,2},{5,7},{6,4},{7,9},{8,6},{9,11},{10,... | collective-permute-start | bytes 1769480 | tf_op jit(solution)/shard_map/ppermute | solution.py:169
  49.5 31.2 %collective-permute-start.7 = (bf16[256,1152]{1,0:T(8,128)(2,1)}, bf16[256,1152]{1,0:T(8,128)(2,1)S(1)}, u32[]{:S(2)}, u32[]{:S(2)}) collective-permute-start(bf16[256,1152]{1,0:T(8,128)(2,1)} %collective-permute-done.3.image), channel_id=1, source_target_pairs={{0,14},{1,3},{2,0},{3,5},{4,2},{5,7},{6,4},{7,9},{8,6},{9,11},{10,... | collective-permute-start | bytes 1769480 | tf_op jit(solution)/shard_map/ppermute | solution.py:169
  61.1 23.6 %collective-permute-start.8 = (bf16[256,1152]{1,0:T(8,128)(2,1)S(1)}, bf16[256,1152]{1,0:T(8,128)(2,1)S(1)}, u32[]{:S(2)}, u32[]{:S(2)}) collective-permute-start(bf16[256,1152]{1,0:T(8,128)(2,1)S(1)} %collective-permute-done.1.image), channel_id=1, source_target_pairs={{0,2},{1,497},{2,4},{3,499},{4,6},{5,501},{6,8},{7,503},{8,10},{9,... | collective-permute-start | bytes 1769480 | tf_op jit(solution)/shard_map/ppermute | solution.py:169
  71.2 17.1 %collective-permute-start.5 = (bf16[256,1152]{1,0:T(8,128)(2,1)S(1)}, bf16[256,1152]{1,0:T(8,128)(2,1)S(1)}, u32[]{:S(2)}, u32[]{:S(2)}) collective-permute-start(bf16[256,1152]{1,0:T(8,128)(2,1)S(1)} %collective-permute-done.text), channel_id=1, source_target_pairs={{0,16},{1,15},{2,18},{3,1},{4,20},{5,3},{6,22},{7,5},{8,24},{9,7},... | collective-permute-start | bytes 1769480 | tf_op jit(solution)/shard_map/ppermute | solution.py:169
  86.4 15.1 %collective-permute-start.10 = (f32[256,1152]{1,0:T(8,128)S(1)}, f32[256,1152]{1,0:T(8,128)S(1)}, u32[]{:S(2)}, u32[]{:S(2)}) collective-permute-start(f32[256,1152]{1,0:T(8,128)S(1)} %get-tuple-element.77), channel_id=1, source_target_pairs={{0,1},{1,0},{2,3},{3,2},{4,5},{5,4},{6,7},{7,6},{8,9},{9,8},{10,11... | collective-permute-start | bytes 3538952 | tf_op jit(solution)/shard_map/ppermute | solution.py:169
  90.0 13.0 %collective-permute-start.9 = (f32[256,1152]{1,0:T(8,128)S(1)}, f32[256,1152]{1,0:T(8,128)S(1)}, u32[]{:S(2)}, u32[]{:S(2)}) collective-permute-start(f32[256,1152]{1,0:T(8,128)S(1)} %get-tuple-element.75), channel_id=1, source_target_pairs={{0,1},{1,0},{2,3},{3,2},{4,5},{5,4},{6,7},{7,6},{8,9},{9,8},{10,11... | collective-permute-start | bytes 3538952 | tf_op jit(solution)/shard_map/ppermute | solution.py:169

commit v6 on v5

--- a/solution.py
+++ b/solution.py
@@ -51,6 +51,31 @@
     if positive is not None:
         residual = residual - positive.astype(F32)
     return (scale * residual).astype(BF16)
+
+
+def join_kernel(texts, images, both, semaphores):
+    rows = texts.shape[0]
+    copies = [
+        pltpu.make_async_copy(texts, both.at[pl.ds(0, rows)], semaphores.at[0]),
+        pltpu.make_async_copy(images, both.at[pl.ds(rows, rows)], semaphores.at[1]),
+    ]
+    for copy in copies:
+        copy.start()
+    for copy in copies:
+        copy.wait()
+
+
+def join(texts, images):
+    rows, width = texts.shape
+    return pl.pallas_call(
+        join_kernel,
+        out_shape=jax.ShapeDtypeStruct((2 * rows, width), BF16),
+        in_specs=[pl.BlockSpec(memory_space=pl.ANY)] * 2,
+        out_specs=pl.BlockSpec(memory_space=pltpu.VMEM),
+        scratch_shapes=[pltpu.SemaphoreType.DMA((2,))],
+        compiler_params=pltpu.CompilerParams(vmem_limit_bytes=VMEM_LIMIT),
+        cost_estimate=pl.CostEstimate(flops=1000, bytes_accessed=1000, transcendentals=0),
+    )(texts, images)
 
 
 def own_kernel(
@@ -198,7 +223,7 @@
 
     first = hop(0, texts, images)
     second = hop(1, texts, images)
-    other = swapped(jnp.concatenate([texts, images]))
+    other = swapped(join(texts, images))
     flags = core.reshape(1).astype(jnp.int32)
     (text_half, image_half, text_other, image_other, *sums) = call(
         own_kernel,

time: 105 us -> 106 us (level)
  Pallas kernels: 24.7 us -> 28.8 us
  other arithmetic: 2.52 us -> 0.08 us
    pallas_call x9, Pallas kernels: 24.7 us -> 27.6 us  [call(): pl.pallas_call(kernel, out_shape=outs, in_specs=specs, out_specs=[pl.Bloc...]
    concatenate x1 -> x0, other arithmetic: 2.44 us -> none  [shards(): other = swapped(jnp.concatenate([texts, images]))]
    pallas_call x0 -> x1, Pallas kernels: none -> 1.27 us  [join(): pl.pallas_call(join_kernel, out_shape=jax.ShapeDtypeStruct((2 * rows, wid...]
  transfers between devices with their start and end apart: 11 -> 11, of which waited for: 1 -> 1; matrix products, arithmetic and copies ran while one was open for 3% -> 3% of each run, Pallas kernels for 22% -> 24%
where the time goes in v6:
time: 106 us
  starting transfers between devices  65.6 us (62%)
  Pallas kernels  28.8 us (27%)
  waiting for transfers between devices  5.14 us (5%)
  local copies, waits for them, and re-layouts  3.79 us (4%)
  between operations  2.23 us (2%)
    ppermute x11, starting transfers between devices, moved(): return lax.ppermute(value, AXES, flat)  65.6 us
    pallas_call x9, Pallas kernels, call(): pl.pallas_call(kernel, out_shape=outs, in_specs=specs, out_specs=[pl.Bloc...  27.6 us
    ppermute x11, waiting for transfers between devices, moved(): return lax.ppermute(value, AXES, flat)  5.14 us
  transfers between devices with their start and end apart: 11, of which 1 were waited for; matrix products, arithmetic and copies ran while one was open for 3% of the time, Pallas kernels for 24%

profile of v6, /device:TPU:7, one launch (start us, length us, event | category | flops | bytes accessed | tf_op | source)
XLA Modules:
  0.0 105.7 jit_solution(890780427389457193)
XLA Ops:
  0.6 0.0 copy-start.1
  0.6 1.3 %shard_map.122 = bf16[512,1152]{1,0:T(8,128)(2,1)S(1)} custom-call(bf16[256,1152]{1,0:T(8,128)(2,1)} %rows.3, bf16[256,1152]{1,0:T(8,128)(2,1)} %rows.2), custom_call_target="tpu_custom_call" | custom-call | flops 1000 | bytes 1000 | tf_op jit(solution)/shard_map/pallas_call | solution.py:70
  1.9 2.6 %collective-permute-start.4 = (bf16[512,1152]{1,0:T(8,128)(2,1)S(1)}, bf16[512,1152]{1,0:T(8,128)(2,1)S(1)}, u32[]{:S(2)}, u32[]{:S(2)}) collective-permute-start(bf16[512,1152]{1,0:T(8,128)(2,1)S(1)} %shard_map.122), channel_id=1, source_target_pairs={{0,1},{1,0},{2,3},{3,2},{4,5},{5,4},{6,7},{7,6},{8,9},{9,8},{10,11... | collective-permute-start | bytes 3538952 | tf_op jit(solution)/shard_map/ppermute | solution.py:194
  4.5 3.1 %collective-permute-start.2 = (bf16[256,1152]{1,0:T(8,128)(2,1)}, bf16[256,1152]{1,0:T(8,128)(2,1)}, u32[]{:S(2)}, u32[]{:S(2)}) collective-permute-start(bf16[256,1152]{1,0:T(8,128)(2,1)} %rows.3), channel_id=1, source_target_pairs={{0,22},{1,3},{2,24},{3,5},{4,26},{5,7},{6,28},{7,9},{8,30},{9,11},... | collective-permute-start | bytes 1769480 | tf_op jit(solution)/shard_map/ppermute | solution.py:194
  7.6 14.3 %collective-permute-start.3 = (bf16[256,1152]{1,0:T(8,128)(2,1)}, bf16[256,1152]{1,0:T(8,128)(2,1)}, u32[]{:S(2)}, u32[]{:S(2)}) collective-permute-start(bf16[256,1152]{1,0:T(8,128)(2,1)} %rows.2), channel_id=1, source_target_pairs={{0,14},{1,507},{2,0},{3,509},{4,2},{5,511},{6,4},{7,497},{8,6},{9,... | collective-permute-start | bytes 1769480 | tf_op jit(solution)/shard_map/ppermute | solution.py:194
  21.9 1.9 %collective-permute-start = (bf16[256,1152]{1,0:T(8,128)(2,1)}, bf16[256,1152]{1,0:T(8,128)(2,1)S(1)}, u32[]{:S(2)}, u32[]{:S(2)}) collective-permute-start(bf16[256,1152]{1,0:T(8,128)(2,1)} %rows.3), channel_id=1, source_target_pairs={{0,2},{1,23},{2,4},{3,25},{4,6},{5,27},{6,8},{7,29},{8,10},{9,31},... | collective-permute-start | bytes 1769480 | tf_op jit(solution)/shard_map/ppermute | solution.py:194
  23.8 2.2 %collective-permute-start.1 = (bf16[256,1152]{1,0:T(8,128)(2,1)}, bf16[256,1152]{1,0:T(8,128)(2,1)S(1)}, u32[]{:S(2)}, u32[]{:S(2)}) collective-permute-start(bf16[256,1152]{1,0:T(8,128)(2,1)} %rows.2), channel_id=1, source_target_pairs={{0,506},{1,15},{2,508},{3,1},{4,510},{5,3},{6,496},{7,5},{8,498},{... | collective-permute-start | bytes 1769480 | tf_op jit(solution)/shard_map/ppermute | solution.py:194
  26.0 0.0 copy-done.1
  26.1 0.8 copy.29.column
  28.2 0.1 pad_maximum_fusion.temper
  28.3 0.7 fusion.2.flags
  29.0 0.0 collective-permute-done.4.other
  29.0 0.0 copy-start
  29.0 0.9 copy-done
  29.9 4.2 %shard_map.123 = (bf16[256,1152]{1,0:T(8,128)(2,1)S(1)}, bf16[256,1152]{1,0:T(8,128)(2,1)S(1)}, bf16[256,1152]{1,0:T(8,128)(2,1)S(1)}, bf16[256,1152]{1,0:T(8,12...) custom-call(f32[2]{0:T(128)S(1)} %pad_maximum_fusion.temper, ...), custom_call_target="tpu_custom_call" | custom-call | flops 1000 | bytes 1000 | tf_op jit(solution)/shard_map/pallas_call | solution.py:37
  34.1 0.0 collective-permute-done.2.text
  34.1 0.0 collective-permute-done.3.image
  34.1 14.4 %collective-permute-start.6 = (bf16[256,1152]{1,0:T(8,128)(2,1)}, bf16[256,1152]{1,0:T(8,128)(2,1)S(1)}, u32[]{:S(2)}, u32[]{:S(2)}) collective-permute-start(bf16[256,1152]{1,0:T(8,128)(2,1)} %collective-permute-done.2.text), channel_id=1, source_target_pairs={{0,14},{1,3},{2,0},{3,5},{4,2},{5,7},{6,4},{7,9},{8,6},{9,11},{10,... | collective-permute-start | bytes 1769480 | tf_op jit(solution)/shard_map/ppermute | solution.py:194
  48.5 1.9 %collective-permute-start.7 = (bf16[256,1152]{1,0:T(8,128)(2,1)}, bf16[256,1152]{1,0:T(8,128)(2,1)S(1)}, u32[]{:S(2)}, u32[]{:S(2)}) collective-permute-start(bf16[256,1152]{1,0:T(8,128)(2,1)} %collective-permute-done.3.image), channel_id=1, source_target_pairs={{0,14},{1,3},{2,0},{3,5},{4,2},{5,7},{6,4},{7,9},{8,6},{9,11},{10,... | collective-permute-start | bytes 1769480 | tf_op jit(solution)/shard_map/ppermute | solution.py:194
  50.4 4.6 %shard_map.124 = (f32[256,1152]{1,0:T(8,128)S(1)}, f32[256,1152]{1,0:T(8,128)S(1)}, f32[256,1152]{1,0:T(8,128)S(1)}, f32[256,1152]{1,0:T(8,128)S(1)}) custom-call(f32[2]{0:T(128)S(1)} %pad_maximum_fusion.temper, s32[4]{0:T(128)S(1)} %fusion.2.flags, ...), custom_call_target="tpu_custom_call", output_to_operand_aliasing={{0}: (8, {}), {1}: (9, {}), {2}: (10, {}), {3}: (11, {})} | custom-call | flops 1000 | bytes 1000 | tf_op jit(solution)/shard_map/pallas_call | solution.py:37
  55.0 0.0 collective-permute-done.text
  55.0 5.1 %collective-permute-done.1.image = bf16[256,1152]{1,0:T(8,128)(2,1)S(1)} collective-permute-done((bf16[256,1152]{1,0:T(8,128)(2,1)}, bf16[256,1152]{1,0:T(8,128)(2,1)S(1)}, u32[]{:S(2)}, u32[]{:S(2)}) %collective-permute-start.1) | collective-permute-done | bytes 589856 | tf_op jit(solution)/shard_map/ppermute | solution.py:194
  60.1 10.2 %collective-permute-start.8 = (bf16[256,1152]{1,0:T(8,128)(2,1)S(1)}, bf16[256,1152]{1,0:T(8,128)(2,1)S(1)}, u32[]{:S(2)}, u32[]{:S(2)}) collective-permute-start(bf16[256,1152]{1,0:T(8,128)(2,1)S(1)} %collective-permute-done.1.image), channel_id=1, source_target_pairs={{0,2},{1,497},{2,4},{3,499},{4,6},{5,501},{6,8},{7,503},{8,10},{9,... | collective-permute-start | bytes 1769480 | tf_op jit(solution)/shard_map/ppermute | solution.py:194
  70.3 3.4 %collective-permute-start.5 = (bf16[256,1152]{1,0:T(8,128)(2,1)S(1)}, bf16[256,1152]{1,0:T(8,128)(2,1)S(1)}, u32[]{:S(2)}, u32[]{:S(2)}) collective-permute-start(bf16[256,1152]{1,0:T(8,128)(2,1)S(1)} %collective-permute-done.text), channel_id=1, source_target_pairs={{0,16},{1,15},{2,18},{3,1},{4,20},{5,3},{6,22},{7,5},{8,24},{9,7},... | collective-permute-start | bytes 1769480 | tf_op jit(solution)/shard_map/ppermute | solution.py:194
  73.7 0.7 fusion.1.flags
  74.4 0.7 fusion.flags
  75.1 4.6 %shard_map.125 = (f32[256,1152]{1,0:T(8,128)S(1)}, f32[256,1152]{1,0:T(8,128)S(1)}, f32[256,1152]{1,0:T(8,128)S(1)}, f32[256,1152]{1,0:T(8,128)S(1)}) custom-call(f32[2]{0:T(128)S(1)} %pad_maximum_fusion.temper, s32[4]{0:T(128)S(1)} %broadcast.2.flags, ...), custom_call_target="tpu_custom_call", output_to_operand_aliasing={{0}: (8, {}), {1}: (9, {}), {2}: (10, {}), {3}: (11, {})} | custom-call | flops 1000 | bytes 1000 | tf_op jit(solution)/shard_map/pallas_call | solution.py:37
  79.7 0.0 collective-permute-done.6.text
  79.7 0.0 collective-permute-done.7.image
  79.7 4.1 %shard_map.126 = (f32[256,1152]{1,0:T(8,128)S(1)}, f32[256,1152]{1,0:T(8,128)S(1)}, f32[256,1152]{1,0:T(8,128)S(1)}, f32[256,1152]{1,0:T(8,128)S(1)}) custom-call(f32[2]{0:T(128)S(1)} %pad_maximum_fusion.temper, s32[4]{0:T(128)S(1)} %fusion.1.flags, ...), custom_call_target="tpu_custom_call", output_to_operand_aliasing={{0}: (8, {}), {1}: (9, {}), {2}: (10, {}), {3}: (11, {})} | custom-call | flops 1000 | bytes 1000 | tf_op jit(solution)/shard_map/pallas_call | solution.py:37
  83.8 0.0 collective-permute-done.8.visitor
  83.8 1.6 %shard_map.128 = (bf16[256,1152]{1,0:T(8,128)(2,1)S(1)}, f32[256,1152]{1,0:T(8,128)S(1)}) custom-call(f32[2]{0:T(128)S(1)} %pad_maximum_fusion.temper, s32[4]{0:T(128)S(1)} %fusion.flags, bf16[256,1152]{1,0:T(8,128)(2,1)S(1)} %collective-permute-done.8.visitor, ...), custom_call_target="tpu_custom_call", output_to_operand_aliasing={{1}: (4, {})} | custom-call | flops 1000 | bytes 1000 | tf_op jit(solution)/shard_map/pallas_call | solution.py:37
  85.4 1.9 %collective-permute-start.10 = (f32[256,1152]{1,0:T(8,128)S(1)}, f32[256,1152]{1,0:T(8,128)S(1)}, u32[]{:S(2)}, u32[]{:S(2)}) collective-permute-start(f32[256,1152]{1,0:T(8,128)S(1)} %get-tuple-element.77), channel_id=1, source_target_pairs={{0,1},{1,0},{2,3},{3,2},{4,5},{5,4},{6,7},{7,6},{8,9},{9,8},{10,11... | collective-permute-start | bytes 3538952 | tf_op jit(solution)/shard_map/ppermute | solution.py:194
  87.4 0.0 collective-permute-done.5.visitor
  87.4 1.6 %shard_map.127 = (bf16[256,1152]{1,0:T(8,128)(2,1)S(1)}, f32[256,1152]{1,0:T(8,128)S(1)}) custom-call(f32[2]{0:T(128)S(1)} %pad_maximum_fusion.temper, s32[4]{0:T(128)S(1)} %fusion.flags, bf16[256,1152]{1,0:T(8,128)(2,1)S(1)} %collective-permute-done.5.visitor, ...), custom_call_target="tpu_custom_call", output_to_operand_aliasing={{1}: (4, {})} | custom-call | flops 1000 | bytes 1000 | tf_op jit(solution)/shard_map/pallas_call | solution.py:37
  89.0 9.8 %collective-permute-start.9 = (f32[256,1152]{1,0:T(8,128)S(1)}, f32[256,1152]{1,0:T(8,128)S(1)}, u32[]{:S(2)}, u32[]{:S(2)}) collective-permute-start(f32[256,1152]{1,0:T(8,128)S(1)} %get-tuple-element.75), channel_id=1, source_target_pairs={{0,1},{1,0},{2,3},{3,2},{4,5},{5,4},{6,7},{7,6},{8,9},{9,8},{10,11... | collective-permute-start | bytes 3538952 | tf_op jit(solution)/shard_map/ppermute | solution.py:194
  98.9 1.7 %shard_map.129 = (f32[256,1152]{1,0:T(8,128)S(1)}, f32[256,1152]{1,0:T(8,128)S(1)}) custom-call(f32[2]{0:T(128)S(1)} %pad_maximum_fusion.temper, s32[4]{0:T(128)S(1)} %fusion.flags, bf16[256,1152]{1,0:T(8,128)(2,1)S(1)} %get-tuple-element.69.text, bf16[256,1152]{1,0:T(8,128)(2,1)S(1)} %get-tuple-element.46.image_half, ...), custom_call_target="tpu_custom_call", output_to_operand_aliasing={{0}: (4, {}), {1}: (7, {})} | custom-call | flops 1000 | bytes 1000 | tf_op jit(solution)/shard_map/pallas_call | solution.py:37
  100.6 0.0 collective-permute-done.10.received
  100.6 2.6 %shard_map.131 = f32[256,1152]{1,0:T(8,128)} custom-call(bf16[256,1152]{1,0:T(8,128)(2,1)} %rows.3, f32[256,1152]{1,0:T(8,128)S(1)} %get-tuple-element.76.near, f32[256,1152]{1,0:T(8,128)S(1)} %collective-permute-done.10.received), custom_call_target="tpu_custom_call" | custom-call | flops 1000 | bytes 1000 | tf_op jit(solution)/shard_map/pallas_call | solution.py:37
  103.1 0.0 collective-permute-done.9.received
  103.1 2.5 %shard_map.130 = f32[256,1152]{1,0:T(8,128)} custom-call(bf16[256,1152]{1,0:T(8,128)(2,1)} %rows.2, f32[256,1152]{1,0:T(8,128)S(1)} %get-tuple-element.74.near, f32[256,1152]{1,0:T(8,128)S(1)} %collective-permute-done.9.received), custom_call_target="tpu_custom_call" | custom-call | flops 1000 | bytes 1000 | tf_op jit(solution)/shard_map/pallas_call | solution.py:37
  (2 shorter events, 0.0 us)
Async XLA Ops:
  0.6 25.4 %copy-start.1 = (s32[256]{0:T(256)S(1)}, s32[256]{0:T(256)}, u32[]{:S(2)}) copy-start(s32[256]{0:T(256)} %param.13) | copy-start | bytes 3076
  1.9 27.1 %collective-permute-start.4 = (bf16[512,1152]{1,0:T(8,128)(2,1)S(1)}, bf16[512,1152]{1,0:T(8,128)(2,1)S(1)}, u32[]{:S(2)}, u32[]{:S(2)}) collective-permute-start(bf16[512,1152]{1,0:T(8,128)(2,1)S(1)} %shard_map.122), channel_id=1, source_target_pairs={{0,1},{1,0},{2,3},{3,2},{4,5},{5,4},{6,7},{7,6},{8,9},{9,8},{10,11... | collective-permute-start | bytes 3538952 | tf_op jit(solution)/shard_map/ppermute | solution.py:194
  4.5 29.6 %collective-permute-start.2 = (bf16[256,1152]{1,0:T(8,128)(2,1)}, bf16[256,1152]{1,0:T(8,128)(2,1)}, u32[]{:S(2)}, u32[]{:S(2)}) collective-permute-start(bf16[256,1152]{1,0:T(8,128)(2,1)} %rows.3), channel_id=1, source_target_pairs={{0,22},{1,3},{2,24},{3,5},{4,26},{5,7},{6,28},{7,9},{8,30},{9,11},... | collective-permute-start | bytes 1769480 | tf_op jit(solution)/shard_map/ppermute | solution.py:194
  7.6 26.5 %collective-permute-start.3 = (bf16[256,1152]{1,0:T(8,128)(2,1)}, bf16[256,1152]{1,0:T(8,128)(2,1)}, u32[]{:S(2)}, u32[]{:S(2)}) collective-permute-start(bf16[256,1152]{1,0:T(8,128)(2,1)} %rows.2), channel_id=1, source_target_pairs={{0,14},{1,507},{2,0},{3,509},{4,2},{5,511},{6,4},{7,497},{8,6},{9,... | collective-permute-start | bytes 1769480 | tf_op jit(solution)/shard_map/ppermute | solution.py:194
  21.9 33.1 %collective-permute-start = (bf16[256,1152]{1,0:T(8,128)(2,1)}, bf16[256,1152]{1,0:T(8,128)(2,1)S(1)}, u32[]{:S(2)}, u32[]{:S(2)}) collective-permute-start(bf16[256,1152]{1,0:T(8,128)(2,1)} %rows.3), channel_id=1, source_target_pairs={{0,2},{1,23},{2,4},{3,25},{4,6},{5,27},{6,8},{7,29},{8,10},{9,31},... | collective-permute-start | bytes 1769480 | tf_op jit(solution)/shard_map/ppermute | solution.py:194
  23.8 36.3 %collective-permute-start.1 = (bf16[256,1152]{1,0:T(8,128)(2,1)}, bf16[256,1152]{1,0:T(8,128)(2,1)S(1)}, u32[]{:S(2)}, u32[]{:S(2)}) collective-permute-start(bf16[256,1152]{1,0:T(8,128)(2,1)} %rows.2), channel_id=1, source_target_pairs={{0,506},{1,15},{2,508},{3,1},{4,510},{5,3},{6,496},{7,5},{8,498},{... | collective-permute-start | bytes 1769480 | tf_op jit(solution)/shard_map/ppermute | solution.py:194
  29.0 0.9 copy-start
  34.1 45.6 %collective-permute-start.6 = (bf16[256,1152]{1,0:T(8,128)(2,1)}, bf16[256,1152]{1,0:T(8,128)(2,1)S(1)}, u32[]{:S(2)}, u32[]{:S(2)}) collective-permute-start(bf16[256,1152]{1,0:T(8,128)(2,1)} %collective-permute-done.2.text), channel_id=1, source_target_pairs={{0,14},{1,3},{2,0},{3,5},{4,2},{5,7},{6,4},{7,9},{8,6},{9,11},{10,... | collective-permute-start | bytes 1769480 | tf_op jit(solution)/shard_map/ppermute | solution.py:194
  48.5 31.2 %collective-permute-start.7 = (bf16[256,1152]{1,0:T(8,128)(2,1)}, bf16[256,1152]{1,0:T(8,128)(2,1)S(1)}, u32[]{:S(2)}, u32[]{:S(2)}) collective-permute-start(bf16[256,1152]{1,0:T(8,128)(2,1)} %collective-permute-done.3.image), channel_id=1, source_target_pairs={{0,14},{1,3},{2,0},{3,5},{4,2},{5,7},{6,4},{7,9},{8,6},{9,11},{10,... | collective-permute-start | bytes 1769480 | tf_op jit(solution)/shard_map/ppermute | solution.py:194
  60.1 23.6 %collective-permute-start.8 = (bf16[256,1152]{1,0:T(8,128)(2,1)S(1)}, bf16[256,1152]{1,0:T(8,128)(2,1)S(1)}, u32[]{:S(2)}, u32[]{:S(2)}) collective-permute-start(bf16[256,1152]{1,0:T(8,128)(2,1)S(1)} %collective-permute-done.1.image), channel_id=1, source_target_pairs={{0,2},{1,497},{2,4},{3,499},{4,6},{5,501},{6,8},{7,503},{8,10},{9,... | collective-permute-start | bytes 1769480 | tf_op jit(solution)/shard_map/ppermute | solution.py:194
  70.3 17.1 %collective-permute-start.5 = (bf16[256,1152]{1,0:T(8,128)(2,1)S(1)}, bf16[256,1152]{1,0:T(8,128)(2,1)S(1)}, u32[]{:S(2)}, u32[]{:S(2)}) collective-permute-start(bf16[256,1152]{1,0:T(8,128)(2,1)S(1)} %collective-permute-done.text), channel_id=1, source_target_pairs={{0,16},{1,15},{2,18},{3,1},{4,20},{5,3},{6,22},{7,5},{8,24},{9,7},... | collective-permute-start | bytes 1769480 | tf_op jit(solution)/shard_map/ppermute | solution.py:194
  85.4 15.1 %collective-permute-start.10 = (f32[256,1152]{1,0:T(8,128)S(1)}, f32[256,1152]{1,0:T(8,128)S(1)}, u32[]{:S(2)}, u32[]{:S(2)}) collective-permute-start(f32[256,1152]{1,0:T(8,128)S(1)} %get-tuple-element.77), channel_id=1, source_target_pairs={{0,1},{1,0},{2,3},{3,2},{4,5},{5,4},{6,7},{7,6},{8,9},{9,8},{10,11... | collective-permute-start | bytes 3538952 | tf_op jit(solution)/shard_map/ppermute | solution.py:194
  89.0 14.1 %collective-permute-start.9 = (f32[256,1152]{1,0:T(8,128)S(1)}, f32[256,1152]{1,0:T(8,128)S(1)}, u32[]{:S(2)}, u32[]{:S(2)}) collective-permute-start(f32[256,1152]{1,0:T(8,128)S(1)} %get-tuple-element.75), channel_id=1, source_target_pairs={{0,1},{1,0},{2,3},{3,2},{4,5},{5,4},{6,7},{7,6},{8,9},{9,8},{10,11... | collective-permute-start | bytes 3538952 | tf_op jit(solution)/shard_map/ppermute | solution.py:194

commit v7 on v5

--- a/solution.py
+++ b/solution.py
@@ -110,18 +110,37 @@
     meet(flags[k + 1], temper, far_res, block, far_in, far)
 
 
-def near_kernel(
-    temper, flags, text, image_half, image_in, image, text_half, text_in, image_out, text_out
-):
-    meet(flags[0], temper, image_half, text[...], image_in, image_out)
-    meet(flags[2], temper, text_half, image[...], text_in, text_out)
-
-
-def finish_kernel(rows, near, received, grad):
-    upstream = near[...] + received[...]
-    unit, inverse = unit_of(rows[...])
-    along = jnp.sum(unit * upstream, axis=-1, keepdims=True)
-    grad[...] = inverse * (upstream - unit * along)
+def near_kernel(k, temper, flags, visitor, near_res, near_in, near):
+    meet(flags[k], temper, near_res, visitor[...], near_in, near)
+
+
+def finish_kernel(rows, near, received, grad, held, semaphores):
+    parts = semaphores.shape[0]
+    step = rows.shape[0] // parts
+    copies = []
+    for k in range(parts):
+        part = slice(k * step, (k + 1) * step)
+        upstream = near[part] + received[part]
+        unit, inverse = unit_of(rows[part])
+        along = jnp.sum(unit * upstream, axis=-1, keepdims=True)
+        held[part] = inverse * (upstream - unit * along)
+        copy = pltpu.make_async_copy(held.at[part], grad.at[part], semaphores.at[k])
+        copy.start()
+        copies.append(copy)
+    for copy in copies:
+        copy.wait()
+
+
+def finish(rows, near, received):
+    return pl.pallas_call(
+        finish_kernel,
+        out_shape=jax.ShapeDtypeStruct(near.shape, F32),
+        in_specs=[pl.BlockSpec(memory_space=pltpu.VMEM)] * 3,
+        out_specs=pl.BlockSpec(memory_space=pl.ANY),
+        scratch_shapes=[pltpu.VMEM(near.shape, F32), pltpu.SemaphoreType.DMA((4,))],
+        compiler_params=pltpu.CompilerParams(vmem_limit_bytes=VMEM_LIMIT),
+        cost_estimate=pl.CostEstimate(flops=1000, bytes_accessed=1000, transcendentals=0),
+    )(rows, near, received)
 
 
 STEPS = ({"A": (0, 1), "B": (1, 1), "C": (1, 2), "D": (1, 3)},
@@ -230,18 +249,23 @@
             kernel, [half, full], [temper, flags_of(3), visitor, other, far_sum], {4: 1}
         )
 
+    def near(k, visitor, own, near_sum):
+        return call(
+            functools.partial(near_kernel, k),
+            [full],
+            [temper, flags_of(3), visitor, own, near_sum],
+            {4: 0},
+        )[0]
+
+    image, text_far = far(2, fourth[1], text_other, text_far)
+    text_back = swapped(text_far)
+    text_near = near(2, image, text_half, text_near)
+    image_far, text_near = lax.optimization_barrier((image_far, text_near))
     text, image_far = far(0, fourth[0], image_other, image_far)
     image_back = swapped(image_far)
-    image, text_far = far(2, fourth[1], text_other, text_far)
-    text_back = swapped(text_far)
-    image_near, text_near = call(
-        near_kernel,
-        [full, full],
-        [temper, flags_of(3), text, image_half, image_near, image, text_half, text_near],
-        {4: 0, 7: 1},
-    )
-    (grad_images,) = call(finish_kernel, [full], [images, image_near, image_back])
-    (grad_texts,) = call(finish_kernel, [full], [texts, text_near, text_back])
+    image_near = near(0, text, image_half, image_near)
+    grad_images = finish(images, image_near, image_back)
+    grad_texts = finish(texts, text_near, text_back)
     return (grad_images, grad_texts)
 
 

time: 105 us -> 105 us (level)
    pallas_call x0 -> x2, Pallas kernels: none -> 2.84 us  [finish(): pl.pallas_call(finish_kernel, out_shape=jax.ShapeDtypeStruct(near.shape,...]
    pallas_call x9 -> x8, Pallas kernels: 24.7 us -> 22.3 us  [call(): pl.pallas_call(kernel, out_shape=outs, in_specs=specs, out_specs=[pl.Bloc...]
  transfers between devices with their start and end apart: 11 -> 11, of which waited for: 1 -> 1; matrix products, arithmetic and copies ran while one was open for 3% -> 3% of each run, Pallas kernels for 22% -> 23%
where the time goes in v7:
time: 105 us; the launch traced here: 104 us
  starting transfers between devices  65.3 us (62%)
  Pallas kernels  25.1 us (24%)
  waiting for transfers between devices  5.16 us (5%)
  local copies, waits for them, and re-layouts  3.8 us (4%)
  other arithmetic  2.52 us (2%)
  between operations  2.44 us (2%)
    ppermute x11, starting transfers between devices, moved(): return lax.ppermute(value, AXES, flat)  65.3 us
    pallas_call x8, Pallas kernels, call(): pl.pallas_call(kernel, out_shape=outs, in_specs=specs, out_specs=[pl.Bloc...  22.3 us
    ppermute x11, waiting for transfers between devices, moved(): return lax.ppermute(value, AXES, flat)  5.16 us
    pallas_call x2, Pallas kernels, finish(): pl.pallas_call(finish_kernel, out_shape=jax.ShapeDtypeStruct(near.shape,...  2.84 us
    concatenate x1, other arithmetic, shards(): other = swapped(jnp.concatenate([texts, images]))  2.44 us
  transfers between devices with their start and end apart: 11, of which 1 were waited for; matrix products, arithmetic and copies ran while one was open for 3% of the time, Pallas kernels for 23%

profile of v7, /device:TPU:7, one launch (start us, length us, event | category | flops | bytes accessed | tf_op | source)
XLA Modules:
  0.0 104.4 jit_solution(5609975414514356585)
XLA Ops:
  0.6 0.0 copy-start.1
  0.6 0.0 copy-start
  0.6 0.0 copy-start.3
  0.7 2.4 %pad_maximum_fusion = bf16[512,1152]{1,0:T(8,128)(2,1)} fusion(bf16[256,1152]{1,0:T(8,128)(2,1)} %rows.2, bf16[256,1152]{1,0:T(8,128)(2,1)} %rows.3), kind=kLoop, calls=%fused_computation | loop fusion | flops 2359296 | bytes 2359296 | tf_op jit(solution)/shard_map/concatenate | solution.py:220
  3.1 2.6 %collective-permute-start.4 = (bf16[512,1152]{1,0:T(8,128)(2,1)}, bf16[512,1152]{1,0:T(8,128)(2,1)S(1)}, u32[]{:S(2)}, u32[]{:S(2)}) collective-permute-start(bf16[512,1152]{1,0:T(8,128)(2,1)} %pad_maximum_fusion), channel_id=1, source_target_pairs={{0,1},{1,0},{2,3},{3,2},{4,5},{5,4},{6,7},{7,6},{8,9},{9,8},{10,11... | collective-permute-start | bytes 3538952 | tf_op jit(solution)/shard_map/ppermute | solution.py:188
  5.7 0.0 copy-done
  5.7 3.1 %collective-permute-start.2 = (bf16[256,1152]{1,0:T(8,128)(2,1)S(1)}, bf16[256,1152]{1,0:T(8,128)(2,1)}, u32[]{:S(2)}, u32[]{:S(2)}) collective-permute-start(bf16[256,1152]{1,0:T(8,128)(2,1)S(1)} %copy-done), channel_id=1, source_target_pairs={{0,22},{1,3},{2,24},{3,5},{4,26},{5,7},{6,28},{7,9},{8,30},{9,11},... | collective-permute-start | bytes 1769480 | tf_op jit(solution)/shard_map/ppermute | solution.py:188
  8.8 0.0 copy-done.1
  8.8 14.3 %collective-permute-start.3 = (bf16[256,1152]{1,0:T(8,128)(2,1)S(1)}, bf16[256,1152]{1,0:T(8,128)(2,1)}, u32[]{:S(2)}, u32[]{:S(2)}) collective-permute-start(bf16[256,1152]{1,0:T(8,128)(2,1)S(1)} %copy-done.1), channel_id=1, source_target_pairs={{0,14},{1,507},{2,0},{3,509},{4,2},{5,511},{6,4},{7,497},{8,6},{9,... | collective-permute-start | bytes 1769480 | tf_op jit(solution)/shard_map/ppermute | solution.py:188
  23.1 1.9 %collective-permute-start = (bf16[256,1152]{1,0:T(8,128)(2,1)S(1)}, bf16[256,1152]{1,0:T(8,128)(2,1)S(1)}, u32[]{:S(2)}, u32[]{:S(2)}) collective-permute-start(bf16[256,1152]{1,0:T(8,128)(2,1)S(1)} %copy-done), channel_id=1, source_target_pairs={{0,2},{1,23},{2,4},{3,25},{4,6},{5,27},{6,8},{7,29},{8,10},{9,31},... | collective-permute-start | bytes 1769480 | tf_op jit(solution)/shard_map/ppermute | solution.py:188
  25.0 2.2 %collective-permute-start.1 = (bf16[256,1152]{1,0:T(8,128)(2,1)S(1)}, bf16[256,1152]{1,0:T(8,128)(2,1)S(1)}, u32[]{:S(2)}, u32[]{:S(2)}) collective-permute-start(bf16[256,1152]{1,0:T(8,128)(2,1)S(1)} %copy-done.1), channel_id=1, source_target_pairs={{0,506},{1,15},{2,508},{3,1},{4,510},{5,3},{6,496},{7,5},{8,498},{... | collective-permute-start | bytes 1769480 | tf_op jit(solution)/shard_map/ppermute | solution.py:188
  27.2 0.0 copy-done.3
  27.2 0.8 copy.30.column
  29.4 0.1 pad_maximum_fusion.1.temper
  29.5 0.7 fusion.2.flags
  30.2 0.0 collective-permute-done.4.other
  30.2 0.0 copy-start.2
  30.2 0.9 copy-done.2
  31.1 3.5 %shard_map.131 = (bf16[256,1152]{1,0:T(8,128)(2,1)S(1)}, bf16[256,1152]{1,0:T(8,128)(2,1)S(1)}, bf16[256,1152]{1,0:T(8,128)(2,1)S(1)}, bf16[256,1152]{1,0:T(8,12...) custom-call(f32[2]{0:T(128)S(1)} %pad_maximum_fusion.1.temper, ...), custom_call_target="tpu_custom_call" | custom-call | flops 1000 | bytes 1000 | tf_op jit(solution)/shard_map/pallas_call | solution.py:37
  34.6 0.0 collective-permute-done.2.text
  34.6 0.0 collective-permute-done.3.image
  34.6 14.9 %collective-permute-start.6 = (bf16[256,1152]{1,0:T(8,128)(2,1)}, bf16[256,1152]{1,0:T(8,128)(2,1)S(1)}, u32[]{:S(2)}, u32[]{:S(2)}) collective-permute-start(bf16[256,1152]{1,0:T(8,128)(2,1)} %collective-permute-done.2.text), channel_id=1, source_target_pairs={{0,14},{1,3},{2,0},{3,5},{4,2},{5,7},{6,4},{7,9},{8,6},{9,11},{10,... | collective-permute-start | bytes 1769480 | tf_op jit(solution)/shard_map/ppermute | solution.py:188
  49.5 1.9 %collective-permute-start.7 = (bf16[256,1152]{1,0:T(8,128)(2,1)}, bf16[256,1152]{1,0:T(8,128)(2,1)S(1)}, u32[]{:S(2)}, u32[]{:S(2)}) collective-permute-start(bf16[256,1152]{1,0:T(8,128)(2,1)} %collective-permute-done.3.image), channel_id=1, source_target_pairs={{0,14},{1,3},{2,0},{3,5},{4,2},{5,7},{6,4},{7,9},{8,6},{9,11},{10,... | collective-permute-start | bytes 1769480 | tf_op jit(solution)/shard_map/ppermute | solution.py:188
  51.4 4.6 %shard_map.132 = (f32[256,1152]{1,0:T(8,128)S(1)}, f32[256,1152]{1,0:T(8,128)S(1)}, f32[256,1152]{1,0:T(8,128)S(1)}, f32[256,1152]{1,0:T(8,128)S(1)}) custom-call(f32[2]{0:T(128)S(1)} %pad_maximum_fusion.1.temper, s32[4]{0:T(128)S(1)} %fusion.2.flags, ...), custom_call_target="tpu_custom_call", output_to_operand_aliasing={{0}: (8, {}), {1}: (9, {}), {2}: (10, {}), {3}: (11, {})} | custom-call | flops 1000 | bytes 1000 | tf_op jit(solution)/shard_map/pallas_call | solution.py:37
  56.0 0.0 collective-permute-done.text
  56.0 5.1 %collective-permute-done.1.image = bf16[256,1152]{1,0:T(8,128)(2,1)S(1)} collective-permute-done((bf16[256,1152]{1,0:T(8,128)(2,1)S(1)}, bf16[256,1152]{1,0:T(8,128)(2,1)S(1)}, u32[]{:S(2)}, u32[]{:S(2)}) %collective-permute-start.1) | collective-permute-done | bytes 589856 | tf_op jit(solution)/shard_map/ppermute | solution.py:188
  61.1 10.1 %collective-permute-start.8 = (bf16[256,1152]{1,0:T(8,128)(2,1)S(1)}, bf16[256,1152]{1,0:T(8,128)(2,1)S(1)}, u32[]{:S(2)}, u32[]{:S(2)}) collective-permute-start(bf16[256,1152]{1,0:T(8,128)(2,1)S(1)} %collective-permute-done.1.image), channel_id=1, source_target_pairs={{0,2},{1,497},{2,4},{3,499},{4,6},{5,501},{6,8},{7,503},{8,10},{9,... | collective-permute-start | bytes 1769480 | tf_op jit(solution)/shard_map/ppermute | solution.py:188
  71.2 3.4 %collective-permute-start.5 = (bf16[256,1152]{1,0:T(8,128)(2,1)S(1)}, bf16[256,1152]{1,0:T(8,128)(2,1)S(1)}, u32[]{:S(2)}, u32[]{:S(2)}) collective-permute-start(bf16[256,1152]{1,0:T(8,128)(2,1)S(1)} %collective-permute-done.text), channel_id=1, source_target_pairs={{0,16},{1,15},{2,18},{3,1},{4,20},{5,3},{6,22},{7,5},{8,24},{9,7},... | collective-permute-start | bytes 1769480 | tf_op jit(solution)/shard_map/ppermute | solution.py:188
  74.6 0.7 fusion.1.flags
  75.3 0.7 fusion.flags
  76.0 4.6 %shard_map.133 = (f32[256,1152]{1,0:T(8,128)S(1)}, f32[256,1152]{1,0:T(8,128)S(1)}, f32[256,1152]{1,0:T(8,128)S(1)}, f32[256,1152]{1,0:T(8,128)S(1)}) custom-call(f32[2]{0:T(128)S(1)} %pad_maximum_fusion.1.temper, s32[4]{0:T(128)S(1)} %broadcast.2.flags, ...), custom_call_target="tpu_custom_call", output_to_operand_aliasing={{0}: (8, {}), {1}: (9, {}), {2}: (10, {}), {3}: (11, {})} | custom-call | flops 1000 | bytes 1000 | tf_op jit(solution)/shard_map/pallas_call | solution.py:37
  80.6 0.0 collective-permute-done.6.text
  80.6 0.0 collective-permute-done.7.image
  80.7 4.1 %shard_map.134 = (f32[256,1152]{1,0:T(8,128)S(1)}, f32[256,1152]{1,0:T(8,128)S(1)}, f32[256,1152]{1,0:T(8,128)S(1)}, f32[256,1152]{1,0:T(8,128)S(1)}) custom-call(f32[2]{0:T(128)S(1)} %pad_maximum_fusion.1.temper, s32[4]{0:T(128)S(1)} %fusion.1.flags, ...), custom_call_target="tpu_custom_call", output_to_operand_aliasing={{0}: (8, {}), {1}: (9, {}), {2}: (10, {}), {3}: (11, {})} | custom-call | flops 1000 | bytes 1000 | tf_op jit(solution)/shard_map/pallas_call | solution.py:37
  84.7 0.0 collective-permute-done.8.visitor
  84.7 1.6 %shard_map.135 = (bf16[256,1152]{1,0:T(8,128)(2,1)S(1)}, f32[256,1152]{1,0:T(8,128)S(1)}) custom-call(f32[2]{0:T(128)S(1)} %pad_maximum_fusion.1.temper, s32[4]{0:T(128)S(1)} %fusion.flags, bf16[256,1152]{1,0:T(8,128)(2,1)S(1)} %collective-permute-done.8.visitor, ...), custom_call_target="tpu_custom_call", output_to_operand_aliasing={{1}: (4, {})} | custom-call | flops 1000 | bytes 1000 | tf_op jit(solution)/shard_map/pallas_call | solution.py:37
  86.4 1.9 %collective-permute-start.10 = (f32[256,1152]{1,0:T(8,128)S(1)}, f32[256,1152]{1,0:T(8,128)S(1)}, u32[]{:S(2)}, u32[]{:S(2)}) collective-permute-start(f32[256,1152]{1,0:T(8,128)S(1)} %get-tuple-element.77), channel_id=1, source_target_pairs={{0,1},{1,0},{2,3},{3,2},{4,5},{5,4},{6,7},{7,6},{8,9},{9,8},{10,11... | collective-permute-start | bytes 3538952 | tf_op jit(solution)/shard_map/ppermute | solution.py:188
  88.3 0.7 shard_map.136.near
  89.1 0.0 collective-permute-done.5.visitor
  89.1 1.6 %shard_map.137 = (bf16[256,1152]{1,0:T(8,128)(2,1)S(1)}, f32[256,1152]{1,0:T(8,128)S(1)}) custom-call(f32[2]{0:T(128)S(1)} %pad_maximum_fusion.1.temper, s32[4]{0:T(128)S(1)} %fusion.flags, bf16[256,1152]{1,0:T(8,128)(2,1)S(1)} %collective-permute-done.5.visitor, ...), custom_call_target="tpu_custom_call", output_to_operand_aliasing={{1}: (4, {})} | custom-call | flops 1000 | bytes 1000 | tf_op jit(solution)/shard_map/pallas_call | solution.py:37
  90.7 9.1 %collective-permute-start.9 = (f32[256,1152]{1,0:T(8,128)S(1)}, f32[256,1152]{1,0:T(8,128)S(1)}, u32[]{:S(2)}, u32[]{:S(2)}) collective-permute-start(f32[256,1152]{1,0:T(8,128)S(1)} %get-tuple-element.75), channel_id=1, source_target_pairs={{0,1},{1,0},{2,3},{3,2},{4,5},{5,4},{6,7},{7,6},{8,9},{9,8},{10,11... | collective-permute-start | bytes 3538952 | tf_op jit(solution)/shard_map/ppermute | solution.py:188
  99.8 1.5 %shard_map.138.near = f32[256,1152]{1,0:T(8,128)S(1)} custom-call(f32[2]{0:T(128)S(1)} %pad_maximum_fusion.1.temper, s32[4]{0:T(128)S(1)} %fusion.flags, bf16[256,1152]{1,0:T(8,128)(2,1)S(1)} %get-tuple-element.73.visitor, bf16[256,1152]{1,0:T(8,128)(2,1)S(1)} %get-tuple-element.46.image_half.near_res, ...), custom_call_target="tpu_custom_call", output_to_operand_aliasing={{}: (4, {})} | custom-call | flops 1000 | bytes 1000 | tf_op jit(solution)/shard_map/pallas_call | solution.py:37
  101.3 0.0 collective-permute-done.10.received
  101.3 1.4 %shard_map.140 = f32[256,1152]{1,0:T(8,128)} custom-call(bf16[256,1152]{1,0:T(8,128)(2,1)S(1)} %copy-done, f32[256,1152]{1,0:T(8,128)S(1)} %shard_map.136.near, f32[256,1152]{1,0:T(8,128)S(1)} %collective-permute-done.10.received), custom_call_target="tpu_custom_call" | custom-call | flops 1000 | bytes 1000 | tf_op jit(solution)/shard_map/pallas_call | solution.py:135
  102.8 0.0 collective-permute-done.9.received
  102.8 1.4 %shard_map.139 = f32[256,1152]{1,0:T(8,128)} custom-call(bf16[256,1152]{1,0:T(8,128)(2,1)S(1)} %copy-done.1, f32[256,1152]{1,0:T(8,128)S(1)} %shard_map.138.near, f32[256,1152]{1,0:T(8,128)S(1)} %collective-permute-done.9.received), custom_call_target="tpu_custom_call" | custom-call | flops 1000 | bytes 1000 | tf_op jit(solution)/shard_map/pallas_call | solution.py:135
  (2 shorter events, 0.0 us)
Async XLA Ops:
  0.6 8.2 %copy-start.1 = (bf16[256,1152]{1,0:T(8,128)(2,1)S(1)}, bf16[256,1152]{1,0:T(8,128)(2,1)}, u32[]{:S(2)}) copy-start(bf16[256,1152]{1,0:T(8,128)(2,1)} %rows.2) | copy-start | bytes 1769476
  0.6 5.0 %copy-start = (bf16[256,1152]{1,0:T(8,128)(2,1)S(1)}, bf16[256,1152]{1,0:T(8,128)(2,1)}, u32[]{:S(2)}) copy-start(bf16[256,1152]{1,0:T(8,128)(2,1)} %rows.3) | copy-start | bytes 1769476
  0.6 26.6 %copy-start.3 = (s32[256]{0:T(256)S(1)}, s32[256]{0:T(256)}, u32[]{:S(2)}) copy-start(s32[256]{0:T(256)} %param.14) | copy-start | bytes 3076
  3.1 27.1 %collective-permute-start.4 = (bf16[512,1152]{1,0:T(8,128)(2,1)}, bf16[512,1152]{1,0:T(8,128)(2,1)S(1)}, u32[]{:S(2)}, u32[]{:S(2)}) collective-permute-start(bf16[512,1152]{1,0:T(8,128)(2,1)} %pad_maximum_fusion), channel_id=1, source_target_pairs={{0,1},{1,0},{2,3},{3,2},{4,5},{5,4},{6,7},{7,6},{8,9},{9,8},{10,11... | collective-permute-start | bytes 3538952 | tf_op jit(solution)/shard_map/ppermute | solution.py:188
  5.7 28.9 %collective-permute-start.2 = (bf16[256,1152]{1,0:T(8,128)(2,1)S(1)}, bf16[256,1152]{1,0:T(8,128)(2,1)}, u32[]{:S(2)}, u32[]{:S(2)}) collective-permute-start(bf16[256,1152]{1,0:T(8,128)(2,1)S(1)} %copy-done), channel_id=1, source_target_pairs={{0,22},{1,3},{2,24},{3,5},{4,26},{5,7},{6,28},{7,9},{8,30},{9,11},... | collective-permute-start | bytes 1769480 | tf_op jit(solution)/shard_map/ppermute | solution.py:188
  8.8 25.8 %collective-permute-start.3 = (bf16[256,1152]{1,0:T(8,128)(2,1)S(1)}, bf16[256,1152]{1,0:T(8,128)(2,1)}, u32[]{:S(2)}, u32[]{:S(2)}) collective-permute-start(bf16[256,1152]{1,0:T(8,128)(2,1)S(1)} %copy-done.1), channel_id=1, source_target_pairs={{0,14},{1,507},{2,0},{3,509},{4,2},{5,511},{6,4},{7,497},{8,6},{9,... | collective-permute-start | bytes 1769480 | tf_op jit(solution)/shard_map/ppermute | solution.py:188
  23.1 32.9 %collective-permute-start = (bf16[256,1152]{1,0:T(8,128)(2,1)S(1)}, bf16[256,1152]{1,0:T(8,128)(2,1)S(1)}, u32[]{:S(2)}, u32[]{:S(2)}) collective-permute-start(bf16[256,1152]{1,0:T(8,128)(2,1)S(1)} %copy-done), channel_id=1, source_target_pairs={{0,2},{1,23},{2,4},{3,25},{4,6},{5,27},{6,8},{7,29},{8,10},{9,31},... | collective-permute-start | bytes 1769480 | tf_op jit(solution)/shard_map/ppermute | solution.py:188
  25.0 36.1 %collective-permute-start.1 = (bf16[256,1152]{1,0:T(8,128)(2,1)S(1)}, bf16[256,1152]{1,0:T(8,128)(2,1)S(1)}, u32[]{:S(2)}, u32[]{:S(2)}) collective-permute-start(bf16[256,1152]{1,0:T(8,128)(2,1)S(1)} %copy-done.1), channel_id=1, source_target_pairs={{0,506},{1,15},{2,508},{3,1},{4,510},{5,3},{6,496},{7,5},{8,498},{... | collective-permute-start | bytes 1769480 | tf_op jit(solution)/shard_map/ppermute | solution.py:188
  30.2 0.9 copy-start.2
  34.6 46.0 %collective-permute-start.6 = (bf16[256,1152]{1,0:T(8,128)(2,1)}, bf16[256,1152]{1,0:T(8,128)(2,1)S(1)}, u32[]{:S(2)}, u32[]{:S(2)}) collective-permute-start(bf16[256,1152]{1,0:T(8,128)(2,1)} %collective-permute-done.2.text), channel_id=1, source_target_pairs={{0,14},{1,3},{2,0},{3,5},{4,2},{5,7},{6,4},{7,9},{8,6},{9,11},{10,... | collective-permute-start | bytes 1769480 | tf_op jit(solution)/shard_map/ppermute | solution.py:188
  49.5 31.2 %collective-permute-start.7 = (bf16[256,1152]{1,0:T(8,128)(2,1)}, bf16[256,1152]{1,0:T(8,128)(2,1)S(1)}, u32[]{:S(2)}, u32[]{:S(2)}) collective-permute-start(bf16[256,1152]{1,0:T(8,128)(2,1)} %collective-permute-done.3.image), channel_id=1, source_target_pairs={{0,14},{1,3},{2,0},{3,5},{4,2},{5,7},{6,4},{7,9},{8,6},{9,11},{10,... | collective-permute-start | bytes 1769480 | tf_op jit(solution)/shard_map/ppermute | solution.py:188
  61.1 23.6 %collective-permute-start.8 = (bf16[256,1152]{1,0:T(8,128)(2,1)S(1)}, bf16[256,1152]{1,0:T(8,128)(2,1)S(1)}, u32[]{:S(2)}, u32[]{:S(2)}) collective-permute-start(bf16[256,1152]{1,0:T(8,128)(2,1)S(1)} %collective-permute-done.1.image), channel_id=1, source_target_pairs={{0,2},{1,497},{2,4},{3,499},{4,6},{5,501},{6,8},{7,503},{8,10},{9,... | collective-permute-start | bytes 1769480 | tf_op jit(solution)/shard_map/ppermute | solution.py:188
  71.2 17.8 %collective-permute-start.5 = (bf16[256,1152]{1,0:T(8,128)(2,1)S(1)}, bf16[256,1152]{1,0:T(8,128)(2,1)S(1)}, u32[]{:S(2)}, u32[]{:S(2)}) collective-permute-start(bf16[256,1152]{1,0:T(8,128)(2,1)S(1)} %collective-permute-done.text), channel_id=1, source_target_pairs={{0,16},{1,15},{2,18},{3,1},{4,20},{5,3},{6,22},{7,5},{8,24},{9,7},... | collective-permute-start | bytes 1769480 | tf_op jit(solution)/shard_map/ppermute | solution.py:188
  86.4 14.9 %collective-permute-start.10 = (f32[256,1152]{1,0:T(8,128)S(1)}, f32[256,1152]{1,0:T(8,128)S(1)}, u32[]{:S(2)}, u32[]{:S(2)}) collective-permute-start(f32[256,1152]{1,0:T(8,128)S(1)} %get-tuple-element.77), channel_id=1, source_target_pairs={{0,1},{1,0},{2,3},{3,2},{4,5},{5,4},{6,7},{7,6},{8,9},{9,8},{10,11... | collective-permute-start | bytes 3538952 | tf_op jit(solution)/shard_map/ppermute | solution.py:188
  90.7 12.1 %collective-permute-start.9 = (f32[256,1152]{1,0:T(8,128)S(1)}, f32[256,1152]{1,0:T(8,128)S(1)}, u32[]{:S(2)}, u32[]{:S(2)}) collective-permute-start(f32[256,1152]{1,0:T(8,128)S(1)} %get-tuple-element.75), channel_id=1, source_target_pairs={{0,1},{1,0},{2,3},{3,2},{4,5},{5,4},{6,7},{7,6},{8,9},{9,8},{10,11... | collective-permute-start | bytes 3538952 | tf_op jit(solution)/shard_map/ppermute | solution.py:188

commit v8 on v7

--- a/solution.py
+++ b/solution.py
@@ -234,9 +234,9 @@
             {8: 0, 9: 1, 10: 2, 11: 3},
         )
 
-    *first, a, b, c, d = lax.optimization_barrier((*first, *sums))
+    first = lax.optimization_barrier(first)
     third = hop(2, *first)
-    sums = visit(0, first, [a, b, c, d])
+    sums = visit(0, first, sums)
     *second, a, b, c, d = lax.optimization_barrier((*second, *sums))
     fourth = hop(3, *second)
     sums = visit(1, second, [a, b, c, d])

time: 105 us -> 105 us (level)
  waiting for transfers between devices: 5.16 us -> 0.83 us
  starting transfers between devices: 65.3 us -> 69.6 us
    ppermute x11, starting transfers between devices: 65.3 us -> 69.6 us  [moved(): return lax.ppermute(value, AXES, flat)]
    ppermute x11, waiting for transfers between devices: 5.16 us -> 0.83 us  [moved(): return lax.ppermute(value, AXES, flat)]
  transfers between devices with their start and end apart: 11 -> 11, of which waited for: 1 -> 2; matrix products, arithmetic and copies ran while one was open for 3% -> 3% of each run, Pallas kernels for 23% -> 23%
where the time goes in v8:
time: 105 us; the launch traced here: 104 us
  starting transfers between devices  69.6 us (66%)
  Pallas kernels  25.1 us (24%)
  local copies, waits for them, and re-layouts  3.8 us (4%)
  other arithmetic  2.52 us (2%)
  between operations  2.44 us (2%)
    ppermute x11, starting transfers between devices, moved(): return lax.ppermute(value, AXES, flat)  69.6 us
    pallas_call x8, Pallas kernels, call(): pl.pallas_call(kernel, out_shape=outs, in_specs=specs, out_specs=[pl.Bloc...  22.3 us
    pallas_call x2, Pallas kernels, finish(): pl.pallas_call(finish_kernel, out_shape=jax.ShapeDtypeStruct(near.shape,...  2.84 us
    concatenate x1, other arithmetic, shards(): other = swapped(jnp.concatenate([texts, images]))  2.44 us
  transfers between devices with their start and end apart: 11, of which 2 were waited for; matrix products, arithmetic and copies ran while one was open for 3% of the time, Pallas kernels for 23%

profile of v8, /device:TPU:7, one launch (start us, length us, event | category | flops | bytes accessed | tf_op | source)
XLA Modules:
  0.0 104.4 jit_solution(17453514760210401302)
XLA Ops:
  0.6 0.0 copy-start.1
  0.6 0.0 copy-start
  0.6 0.0 copy-start.3
  0.7 2.4 %pad_maximum_fusion = bf16[512,1152]{1,0:T(8,128)(2,1)} fusion(bf16[256,1152]{1,0:T(8,128)(2,1)} %rows.2, bf16[256,1152]{1,0:T(8,128)(2,1)} %rows.3), kind=kLoop, calls=%fused_computation | loop fusion | flops 2359296 | bytes 2359296 | tf_op jit(solution)/shard_map/concatenate | solution.py:220
  3.1 2.6 %collective-permute-start.4 = (bf16[512,1152]{1,0:T(8,128)(2,1)}, bf16[512,1152]{1,0:T(8,128)(2,1)S(1)}, u32[]{:S(2)}, u32[]{:S(2)}) collective-permute-start(bf16[512,1152]{1,0:T(8,128)(2,1)} %pad_maximum_fusion), channel_id=1, source_target_pairs={{0,1},{1,0},{2,3},{3,2},{4,5},{5,4},{6,7},{7,6},{8,9},{9,8},{10,11... | collective-permute-start | bytes 3538952 | tf_op jit(solution)/shard_map/ppermute | solution.py:188
  5.7 0.0 copy-done
  5.7 3.1 %collective-permute-start.2 = (bf16[256,1152]{1,0:T(8,128)(2,1)S(1)}, bf16[256,1152]{1,0:T(8,128)(2,1)}, u32[]{:S(2)}, u32[]{:S(2)}) collective-permute-start(bf16[256,1152]{1,0:T(8,128)(2,1)S(1)} %copy-done), channel_id=1, source_target_pairs={{0,22},{1,3},{2,24},{3,5},{4,26},{5,7},{6,28},{7,9},{8,30},{9,11},... | collective-permute-start | bytes 1769480 | tf_op jit(solution)/shard_map/ppermute | solution.py:188
  8.8 0.0 copy-done.1
  8.8 14.3 %collective-permute-start.3 = (bf16[256,1152]{1,0:T(8,128)(2,1)S(1)}, bf16[256,1152]{1,0:T(8,128)(2,1)}, u32[]{:S(2)}, u32[]{:S(2)}) collective-permute-start(bf16[256,1152]{1,0:T(8,128)(2,1)S(1)} %copy-done.1), channel_id=1, source_target_pairs={{0,14},{1,507},{2,0},{3,509},{4,2},{5,511},{6,4},{7,497},{8,6},{9,... | collective-permute-start | bytes 1769480 | tf_op jit(solution)/shard_map/ppermute | solution.py:188
  23.1 1.9 %collective-permute-start = (bf16[256,1152]{1,0:T(8,128)(2,1)S(1)}, bf16[256,1152]{1,0:T(8,128)(2,1)S(1)}, u32[]{:S(2)}, u32[]{:S(2)}) collective-permute-start(bf16[256,1152]{1,0:T(8,128)(2,1)S(1)} %copy-done), channel_id=1, source_target_pairs={{0,2},{1,23},{2,4},{3,25},{4,6},{5,27},{6,8},{7,29},{8,10},{9,31},... | collective-permute-start | bytes 1769480 | tf_op jit(solution)/shard_map/ppermute | solution.py:188
  25.0 2.2 %collective-permute-start.1 = (bf16[256,1152]{1,0:T(8,128)(2,1)S(1)}, bf16[256,1152]{1,0:T(8,128)(2,1)S(1)}, u32[]{:S(2)}, u32[]{:S(2)}) collective-permute-start(bf16[256,1152]{1,0:T(8,128)(2,1)S(1)} %copy-done.1), channel_id=1, source_target_pairs={{0,506},{1,15},{2,508},{3,1},{4,510},{5,3},{6,496},{7,5},{8,498},{... | collective-permute-start | bytes 1769480 | tf_op jit(solution)/shard_map/ppermute | solution.py:188
  27.2 0.0 copy-done.3
  27.2 0.8 copy.30.column
  29.4 0.1 pad_maximum_fusion.1.temper
  29.5 0.7 fusion.2.flags
  30.2 0.0 collective-permute-done.2.text
  30.2 0.1 collective-permute-done.3.image
  30.3 19.2 %collective-permute-start.6 = (bf16[256,1152]{1,0:T(8,128)(2,1)}, bf16[256,1152]{1,0:T(8,128)(2,1)S(1)}, u32[]{:S(2)}, u32[]{:S(2)}) collective-permute-start(bf16[256,1152]{1,0:T(8,128)(2,1)} %collective-permute-done.2.text), channel_id=1, source_target_pairs={{0,14},{1,3},{2,0},{3,5},{4,2},{5,7},{6,4},{7,9},{8,6},{9,11},{10,... | collective-permute-start | bytes 1769480 | tf_op jit(solution)/shard_map/ppermute | solution.py:188
  49.5 1.9 %collective-permute-start.7 = (bf16[256,1152]{1,0:T(8,128)(2,1)}, bf16[256,1152]{1,0:T(8,128)(2,1)S(1)}, u32[]{:S(2)}, u32[]{:S(2)}) collective-permute-start(bf16[256,1152]{1,0:T(8,128)(2,1)} %collective-permute-done.3.image), channel_id=1, source_target_pairs={{0,14},{1,3},{2,0},{3,5},{4,2},{5,7},{6,4},{7,9},{8,6},{9,11},{10,... | collective-permute-start | bytes 1769480 | tf_op jit(solution)/shard_map/ppermute | solution.py:188
  51.4 0.0 collective-permute-done.4.other
  51.4 0.0 copy-start.2
  51.4 0.9 copy-done.2
  52.3 3.5 %shard_map.131 = (bf16[256,1152]{1,0:T(8,128)(2,1)S(1)}, bf16[256,1152]{1,0:T(8,128)(2,1)S(1)}, bf16[256,1152]{1,0:T(8,128)(2,1)S(1)}, bf16[256,1152]{1,0:T(8,12...) custom-call(f32[2]{0:T(128)S(1)} %pad_maximum_fusion.1.temper, ...), custom_call_target="tpu_custom_call" | custom-call | flops 1000 | bytes 1000 | tf_op jit(solution)/shard_map/pallas_call | solution.py:37
  55.8 4.6 %shard_map.132 = (f32[256,1152]{1,0:T(8,128)S(1)}, f32[256,1152]{1,0:T(8,128)S(1)}, f32[256,1152]{1,0:T(8,128)S(1)}, f32[256,1152]{1,0:T(8,128)S(1)}) custom-call(f32[2]{0:T(128)S(1)} %pad_maximum_fusion.1.temper, s32[4]{0:T(128)S(1)} %fusion.2.flags, ...), custom_call_target="tpu_custom_call", output_to_operand_aliasing={{0}: (8, {}), {1}: (9, {}), {2}: (10, {}), {3}: (11, {})} | custom-call | flops 1000 | bytes 1000 | tf_op jit(solution)/shard_map/pallas_call | solution.py:37
  60.4 0.0 collective-permute-done.text
  60.4 0.7 collective-permute-done.1.image
  61.1 14.5 %collective-permute-start.8 = (bf16[256,1152]{1,0:T(8,128)(2,1)S(1)}, bf16[256,1152]{1,0:T(8,128)(2,1)S(1)}, u32[]{:S(2)}, u32[]{:S(2)}) collective-permute-start(bf16[256,1152]{1,0:T(8,128)(2,1)S(1)} %collective-permute-done.1.image), channel_id=1, source_target_pairs={{0,2},{1,497},{2,4},{3,499},{4,6},{5,501},{6,8},{7,503},{8,10},{9,... | collective-permute-start | bytes 1769480 | tf_op jit(solution)/shard_map/ppermute | solution.py:188
  75.7 3.4 %collective-permute-start.5 = (bf16[256,1152]{1,0:T(8,128)(2,1)S(1)}, bf16[256,1152]{1,0:T(8,128)(2,1)S(1)}, u32[]{:S(2)}, u32[]{:S(2)}) collective-permute-start(bf16[256,1152]{1,0:T(8,128)(2,1)S(1)} %collective-permute-done.text), channel_id=1, source_target_pairs={{0,16},{1,15},{2,18},{3,1},{4,20},{5,3},{6,22},{7,5},{8,24},{9,7},... | collective-permute-start | bytes 1769480 | tf_op jit(solution)/shard_map/ppermute | solution.py:188
  79.0 0.7 fusion.1.flags
  79.7 0.7 fusion.flags
  80.4 4.6 %shard_map.133 = (f32[256,1152]{1,0:T(8,128)S(1)}, f32[256,1152]{1,0:T(8,128)S(1)}, f32[256,1152]{1,0:T(8,128)S(1)}, f32[256,1152]{1,0:T(8,128)S(1)}) custom-call(f32[2]{0:T(128)S(1)} %pad_maximum_fusion.1.temper, s32[4]{0:T(128)S(1)} %broadcast.2.flags, ...), custom_call_target="tpu_custom_call", output_to_operand_aliasing={{0}: (8, {}), {1}: (9, {}), {2}: (10, {}), {3}: (11, {})} | custom-call | flops 1000 | bytes 1000 | tf_op jit(solution)/shard_map/pallas_call | solution.py:37
  85.1 0.0 collective-permute-done.6.text
  85.1 0.0 collective-permute-done.7.image
  85.1 4.1 %shard_map.134 = (f32[256,1152]{1,0:T(8,128)S(1)}, f32[256,1152]{1,0:T(8,128)S(1)}, f32[256,1152]{1,0:T(8,128)S(1)}, f32[256,1152]{1,0:T(8,128)S(1)}) custom-call(f32[2]{0:T(128)S(1)} %pad_maximum_fusion.1.temper, s32[4]{0:T(128)S(1)} %fusion.1.flags, ...), custom_call_target="tpu_custom_call", output_to_operand_aliasing={{0}: (8, {}), {1}: (9, {}), {2}: (10, {}), {3}: (11, {})} | custom-call | flops 1000 | bytes 1000 | tf_op jit(solution)/shard_map/pallas_call | solution.py:37
  89.2 0.0 collective-permute-done.8.visitor
  89.2 1.6 %shard_map.135 = (bf16[256,1152]{1,0:T(8,128)(2,1)S(1)}, f32[256,1152]{1,0:T(8,128)S(1)}) custom-call(f32[2]{0:T(128)S(1)} %pad_maximum_fusion.1.temper, s32[4]{0:T(128)S(1)} %fusion.flags, bf16[256,1152]{1,0:T(8,128)(2,1)S(1)} %collective-permute-done.8.visitor, ...), custom_call_target="tpu_custom_call", output_to_operand_aliasing={{1}: (4, {})} | custom-call | flops 1000 | bytes 1000 | tf_op jit(solution)/shard_map/pallas_call | solution.py:37
  90.8 1.9 %collective-permute-start.10 = (f32[256,1152]{1,0:T(8,128)S(1)}, f32[256,1152]{1,0:T(8,128)S(1)}, u32[]{:S(2)}, u32[]{:S(2)}) collective-permute-start(f32[256,1152]{1,0:T(8,128)S(1)} %get-tuple-element.69), channel_id=1, source_target_pairs={{0,1},{1,0},{2,3},{3,2},{4,5},{5,4},{6,7},{7,6},{8,9},{9,8},{10,11... | collective-permute-start | bytes 3538952 | tf_op jit(solution)/shard_map/ppermute | solution.py:188
  92.8 0.7 shard_map.136.near
  93.5 0.0 collective-permute-done.5.visitor
  93.5 1.6 %shard_map.137 = (bf16[256,1152]{1,0:T(8,128)(2,1)S(1)}, f32[256,1152]{1,0:T(8,128)S(1)}) custom-call(f32[2]{0:T(128)S(1)} %pad_maximum_fusion.1.temper, s32[4]{0:T(128)S(1)} %fusion.flags, bf16[256,1152]{1,0:T(8,128)(2,1)S(1)} %collective-permute-done.5.visitor, ...), custom_call_target="tpu_custom_call", output_to_operand_aliasing={{1}: (4, {})} | custom-call | flops 1000 | bytes 1000 | tf_op jit(solution)/shard_map/pallas_call | solution.py:37
  95.2 4.6 %collective-permute-start.9 = (f32[256,1152]{1,0:T(8,128)S(1)}, f32[256,1152]{1,0:T(8,128)S(1)}, u32[]{:S(2)}, u32[]{:S(2)}) collective-permute-start(f32[256,1152]{1,0:T(8,128)S(1)} %get-tuple-element.67), channel_id=1, source_target_pairs={{0,1},{1,0},{2,3},{3,2},{4,5},{5,4},{6,7},{7,6},{8,9},{9,8},{10,11... | collective-permute-start | bytes 3538952 | tf_op jit(solution)/shard_map/ppermute | solution.py:188
  99.8 1.5 %shard_map.138.near = f32[256,1152]{1,0:T(8,128)S(1)} custom-call(f32[2]{0:T(128)S(1)} %pad_maximum_fusion.1.temper, s32[4]{0:T(128)S(1)} %fusion.flags, bf16[256,1152]{1,0:T(8,128)(2,1)S(1)} %get-tuple-element.65.visitor, bf16[256,1152]{1,0:T(8,128)(2,1)S(1)} %get-tuple-element.38.image_half.near_res, ...), custom_call_target="tpu_custom_call", output_to_operand_aliasing={{}: (4, {})} | custom-call | flops 1000 | bytes 1000 | tf_op jit(solution)/shard_map/pallas_call | solution.py:37
  101.3 0.0 collective-permute-done.10.received
  101.3 1.4 %shard_map.140 = f32[256,1152]{1,0:T(8,128)} custom-call(bf16[256,1152]{1,0:T(8,128)(2,1)S(1)} %copy-done, f32[256,1152]{1,0:T(8,128)S(1)} %shard_map.136.near, f32[256,1152]{1,0:T(8,128)S(1)} %collective-permute-done.10.received), custom_call_target="tpu_custom_call" | custom-call | flops 1000 | bytes 1000 | tf_op jit(solution)/shard_map/pallas_call | solution.py:135
  102.8 0.0 collective-permute-done.9.received
  102.8 1.4 %shard_map.139 = f32[256,1152]{1,0:T(8,128)} custom-call(bf16[256,1152]{1,0:T(8,128)(2,1)S(1)} %copy-done.1, f32[256,1152]{1,0:T(8,128)S(1)} %shard_map.138.near, f32[256,1152]{1,0:T(8,128)S(1)} %collective-permute-done.9.received), custom_call_target="tpu_custom_call" | custom-call | flops 1000 | bytes 1000 | tf_op jit(solution)/shard_map/pallas_call | solution.py:135
  (2 shorter events, 0.0 us)
Async XLA Ops:
  0.6 8.2 %copy-start.1 = (bf16[256,1152]{1,0:T(8,128)(2,1)S(1)}, bf16[256,1152]{1,0:T(8,128)(2,1)}, u32[]{:S(2)}) copy-start(bf16[256,1152]{1,0:T(8,128)(2,1)} %rows.2) | copy-start | bytes 1769476
  0.6 5.0 %copy-start = (bf16[256,1152]{1,0:T(8,128)(2,1)S(1)}, bf16[256,1152]{1,0:T(8,128)(2,1)}, u32[]{:S(2)}) copy-start(bf16[256,1152]{1,0:T(8,128)(2,1)} %rows.3) | copy-start | bytes 1769476
  0.6 26.6 %copy-start.3 = (s32[256]{0:T(256)S(1)}, s32[256]{0:T(256)}, u32[]{:S(2)}) copy-start(s32[256]{0:T(256)} %param.14) | copy-start | bytes 3076
  3.1 48.3 %collective-permute-start.4 = (bf16[512,1152]{1,0:T(8,128)(2,1)}, bf16[512,1152]{1,0:T(8,128)(2,1)S(1)}, u32[]{:S(2)}, u32[]{:S(2)}) collective-permute-start(bf16[512,1152]{1,0:T(8,128)(2,1)} %pad_maximum_fusion), channel_id=1, source_target_pairs={{0,1},{1,0},{2,3},{3,2},{4,5},{5,4},{6,7},{7,6},{8,9},{9,8},{10,11... | collective-permute-start | bytes 3538952 | tf_op jit(solution)/shard_map/ppermute | solution.py:188
  5.7 24.5 %collective-permute-start.2 = (bf16[256,1152]{1,0:T(8,128)(2,1)S(1)}, bf16[256,1152]{1,0:T(8,128)(2,1)}, u32[]{:S(2)}, u32[]{:S(2)}) collective-permute-start(bf16[256,1152]{1,0:T(8,128)(2,1)S(1)} %copy-done), channel_id=1, source_target_pairs={{0,22},{1,3},{2,24},{3,5},{4,26},{5,7},{6,28},{7,9},{8,30},{9,11},... | collective-permute-start | bytes 1769480 | tf_op jit(solution)/shard_map/ppermute | solution.py:188
  8.8 21.4 %collective-permute-start.3 = (bf16[256,1152]{1,0:T(8,128)(2,1)S(1)}, bf16[256,1152]{1,0:T(8,128)(2,1)}, u32[]{:S(2)}, u32[]{:S(2)}) collective-permute-start(bf16[256,1152]{1,0:T(8,128)(2,1)S(1)} %copy-done.1), channel_id=1, source_target_pairs={{0,14},{1,507},{2,0},{3,509},{4,2},{5,511},{6,4},{7,497},{8,6},{9,... | collective-permute-start | bytes 1769480 | tf_op jit(solution)/shard_map/ppermute | solution.py:188
  23.1 37.3 %collective-permute-start = (bf16[256,1152]{1,0:T(8,128)(2,1)S(1)}, bf16[256,1152]{1,0:T(8,128)(2,1)S(1)}, u32[]{:S(2)}, u32[]{:S(2)}) collective-permute-start(bf16[256,1152]{1,0:T(8,128)(2,1)S(1)} %copy-done), channel_id=1, source_target_pairs={{0,2},{1,23},{2,4},{3,25},{4,6},{5,27},{6,8},{7,29},{8,10},{9,31},... | collective-permute-start | bytes 1769480 | tf_op jit(solution)/shard_map/ppermute | solution.py:188
  25.0 36.1 %collective-permute-start.1 = (bf16[256,1152]{1,0:T(8,128)(2,1)S(1)}, bf16[256,1152]{1,0:T(8,128)(2,1)S(1)}, u32[]{:S(2)}, u32[]{:S(2)}) collective-permute-start(bf16[256,1152]{1,0:T(8,128)(2,1)S(1)} %copy-done.1), channel_id=1, source_target_pairs={{0,506},{1,15},{2,508},{3,1},{4,510},{5,3},{6,496},{7,5},{8,498},{... | collective-permute-start | bytes 1769480 | tf_op jit(solution)/shard_map/ppermute | solution.py:188
  30.3 54.8 %collective-permute-start.6 = (bf16[256,1152]{1,0:T(8,128)(2,1)}, bf16[256,1152]{1,0:T(8,128)(2,1)S(1)}, u32[]{:S(2)}, u32[]{:S(2)}) collective-permute-start(bf16[256,1152]{1,0:T(8,128)(2,1)} %collective-permute-done.2.text), channel_id=1, source_target_pairs={{0,14},{1,3},{2,0},{3,5},{4,2},{5,7},{6,4},{7,9},{8,6},{9,11},{10,... | collective-permute-start | bytes 1769480 | tf_op jit(solution)/shard_map/ppermute | solution.py:188
  49.5 35.6 %collective-permute-start.7 = (bf16[256,1152]{1,0:T(8,128)(2,1)}, bf16[256,1152]{1,0:T(8,128)(2,1)S(1)}, u32[]{:S(2)}, u32[]{:S(2)}) collective-permute-start(bf16[256,1152]{1,0:T(8,128)(2,1)} %collective-permute-done.3.image), channel_id=1, source_target_pairs={{0,14},{1,3},{2,0},{3,5},{4,2},{5,7},{6,4},{7,9},{8,6},{9,11},{10,... | collective-permute-start | bytes 1769480 | tf_op jit(solution)/shard_map/ppermute | solution.py:188
  51.4 0.9 copy-start.2
  61.1 28.0 %collective-permute-start.8 = (bf16[256,1152]{1,0:T(8,128)(2,1)S(1)}, bf16[256,1152]{1,0:T(8,128)(2,1)S(1)}, u32[]{:S(2)}, u32[]{:S(2)}) collective-permute-start(bf16[256,1152]{1,0:T(8,128)(2,1)S(1)} %collective-permute-done.1.image), channel_id=1, source_target_pairs={{0,2},{1,497},{2,4},{3,499},{4,6},{5,501},{6,8},{7,503},{8,10},{9,... | collective-permute-start | bytes 1769480 | tf_op jit(solution)/shard_map/ppermute | solution.py:188
  75.7 17.8 %collective-permute-start.5 = (bf16[256,1152]{1,0:T(8,128)(2,1)S(1)}, bf16[256,1152]{1,0:T(8,128)(2,1)S(1)}, u32[]{:S(2)}, u32[]{:S(2)}) collective-permute-start(bf16[256,1152]{1,0:T(8,128)(2,1)S(1)} %collective-permute-done.text), channel_id=1, source_target_pairs={{0,16},{1,15},{2,18},{3,1},{4,20},{5,3},{6,22},{7,5},{8,24},{9,7},... | collective-permute-start | bytes 1769480 | tf_op jit(solution)/shard_map/ppermute | solution.py:188
  90.8 10.5 %collective-permute-start.10 = (f32[256,1152]{1,0:T(8,128)S(1)}, f32[256,1152]{1,0:T(8,128)S(1)}, u32[]{:S(2)}, u32[]{:S(2)}) collective-permute-start(f32[256,1152]{1,0:T(8,128)S(1)} %get-tuple-element.69), channel_id=1, source_target_pairs={{0,1},{1,0},{2,3},{3,2},{4,5},{5,4},{6,7},{7,6},{8,9},{9,8},{10,11... | collective-permute-start | bytes 3538952 | tf_op jit(solution)/shard_map/ppermute | solution.py:188
  95.2 7.6 %collective-permute-start.9 = (f32[256,1152]{1,0:T(8,128)S(1)}, f32[256,1152]{1,0:T(8,128)S(1)}, u32[]{:S(2)}, u32[]{:S(2)}) collective-permute-start(f32[256,1152]{1,0:T(8,128)S(1)} %get-tuple-element.67), channel_id=1, source_target_pairs={{0,1},{1,0},{2,3},{3,2},{4,5},{5,4},{6,7},{7,6},{8,9},{9,8},{10,11... | collective-permute-start | bytes 3538952 | tf_op jit(solution)/shard_map/ppermute | solution.py:188
